TPU v7x, 32 devices: a whole 2x2x4 slice. The times are simulated.
32 devices in a mesh: groups: 2 (over y), win: 4 (over z), samp: 2 (over x), head: 2 (over core).
Axes of the slice: x: 2, y: 2, z: 4, core: 2. Of those that a mesh axis runs over, the one named last changes fastest.
Arguments:
- queries: bfloat16 [4, 512, 1280], P(('groups', 'samp'), 'win', 'head'), parts along dimension 0, may hold values from -8 to 8
- key_vectors: bfloat16 [4, 512, 1280], P(('groups', 'samp'), 'win', 'head'), parts along dimension 0, may hold values from -8 to 8
- value_vectors: bfloat16 [4, 512, 1280], P(('groups', 'samp'), 'win', 'head'), parts along dimension 0, may hold values from -6 to 6
- out_grad: bfloat16 [4, 512, 1280], P(('groups', 'samp'), 'win', 'head'), parts along dimension 0, may hold values from -6 to 6
- keep_mask: int32 [4, 512], P(('groups', 'samp'), 'win'), parts along dimension 0, may hold values from 0 to 1, as said below
Outputs:
- attended: bfloat16 [4, 512, 1280], P(('groups', 'samp'), 'win', 'head'), parts along dimension 0
- grad_queries: bfloat16 [4, 512, 1280], P(('groups', 'samp'), 'win', 'head'), parts along dimension 0
- grad_keys: bfloat16 [4, 512, 1280], P(('groups', 'samp'), 'win', 'head'), parts along dimension 0
- grad_values: bfloat16 [4, 512, 1280], P(('groups', 'samp'), 'win', 'head'), parts along dimension 0
There are 2 independent parts, one for each index of `groups`. A program takes and returns all parts, laid end to end along the dimension named above; each array names one. Nothing has to cross between parts.
Inputs may be any that keep to these rules, and one draw needn't show every extreme that they name: `keep_mask`: in every sample exactly 256 of the 512 tokens are kept (1) and the others dropped (0); in every sample the 128 tokens of some one index of win are all kept.
All inputs are finite; a program needn't handle non-finite values.
Results may differ from a plain program's by a relative error of at most 0.03.
Values may be sent and summed in bfloat16 or wider, within the bound.
No kernel may reach another device: no remote copies, remote signals or barrier semaphores. Data moves between devices by JAX's collectives and lax.ppermute only.
A program may use at most 64 MiB of HBM per device.

v0:
```python
import math

import jax
import jax.numpy as jnp
from jax import lax
from jax.sharding import PartitionSpec as P

HEAD_DIM = 128


def fold_blocks(step_fn, carried, arrays):
    count = arrays[0].shape[0]
    width = 512 if count % 512 == 0 else count
    blocks = tuple(
        (member.reshape((count // width, width) + member.shape[1:]) for member in arrays)
    )

    def inner_step(state, current):
        return (step_fn(state, current), None)

    result, unused = lax.scan(inner_step, carried, blocks)
    return result


def shards(queries, key_vectors, value_vectors, out_grad, keep_mask):
    win_count = lax.axis_size("win")
    win_index = lax.axis_index("win")
    tok_rows = queries.shape[1]
    feat_dev = queries.shape[2]
    head_count = feat_dev // HEAD_DIM
    slot_rows = tok_rows // win_count
    own_rows = tok_rows // 2
    inv_root = 1.0 / math.sqrt(HEAD_DIM)
    kept_flag = keep_mask[0]
    kept_here = jnp.sum(kept_flag)
    counts = lax.all_gather(kept_here.reshape(1), "win", axis=0, tiled=True)
    starts = jnp.cumsum(counts) - counts
    ends = starts + counts
    start_here = starts[win_index]
    kept_order = jnp.argsort(1 - kept_flag, stable=True)
    kept_rank = jnp.cumsum(kept_flag) - 1
    slot_index = jnp.arange(tok_rows, dtype=jnp.int32)
    target = slot_index // slot_rows
    within = slot_index % slot_rows
    leading = start_here + jnp.mod(target - start_here, win_count)
    global_pos = leading + within * win_count
    send_live = global_pos < start_here + kept_here
    send_rows = kept_order[jnp.clip(global_pos - start_here, 0, tok_rows - 1)]

    def pack(matrix):
        return jnp.where(send_live[:, None], matrix[0][send_rows], jnp.zeros((), matrix.dtype))

    own_index = jnp.arange(own_rows, dtype=jnp.int32)
    wanted = own_index * win_count + win_index
    source = jnp.sum((ends[None, :] <= wanted[:, None]).astype(jnp.int32), axis=1)
    source_start = starts[source]
    source_lead = source_start + jnp.mod(win_index - source_start, win_count)
    recv_rows = source * slot_rows + (wanted - source_lead) // win_count

    def unpack(matrix):
        return matrix[recv_rows]

    back_start = starts[target]
    back_lead = back_start + jnp.mod(win_index - back_start, win_count)
    back_global = back_lead + within * win_count
    back_live = back_global < ends[target]
    back_rows = jnp.clip(back_global // win_count, 0, own_rows - 1)

    def repack(matrix):
        return jnp.where(back_live[:, None], matrix[back_rows], jnp.zeros((), matrix.dtype))

    global_here = start_here + kept_rank
    owner = jnp.mod(global_here, win_count)
    owner_lead = start_here + jnp.mod(owner - start_here, win_count)
    land_rows = jnp.clip(
        owner * slot_rows + (global_here - owner_lead) // win_count, 0, tok_rows - 1
    )

    def place(matrix):
        return jnp.where(kept_flag[:, None] == 1, matrix[land_rows], jnp.zeros((), matrix.dtype))[
            None
        ]

    def heads_view(matrix):
        return matrix.reshape(matrix.shape[0], head_count, HEAD_DIM)

    got_query, got_key, got_value = (
        lax.all_to_all(pack(queries), "win", split_axis=0, concat_axis=0, tiled=True),
        lax.all_to_all(pack(key_vectors), "win", split_axis=0, concat_axis=0, tiled=True),
        lax.all_to_all(pack(value_vectors), "win", split_axis=0, concat_axis=0, tiled=True),
    )
    query_rows = unpack(got_query)
    key_rows = unpack(got_key)
    value_rows = unpack(got_value)
    query_heads = heads_view(query_rows)

    def soft_step(carried, current):
        highest, totals, summed = carried
        block_keys, block_values = current
        scores = (
            jnp.einsum(
                "qhe,khe->hqk",
                query_heads,
                heads_view(block_keys),
                preferred_element_type=jnp.float32,
            )
            * inv_root
        )
        peak_new = jnp.maximum(highest, jnp.max(scores, axis=-1))
        shrink = jnp.exp(highest - peak_new)
        raised = jnp.exp(scores - peak_new[..., None])
        totals = totals * shrink + jnp.sum(raised, axis=-1)
        summed = summed * shrink.T[..., None] + jnp.einsum(
            "hqk,khe->qhe",
            raised.astype(jnp.bfloat16),
            heads_view(block_values),
            preferred_element_type=jnp.float32,
        )
        return (peak_new, totals, summed)

    start_state = (
        jnp.full((head_count, own_rows), -jnp.inf, jnp.float32),
        jnp.zeros((head_count, own_rows), jnp.float32),
        jnp.zeros((own_rows, head_count, HEAD_DIM), jnp.float32),
    )
    highest, totals, summed = fold_blocks(
        soft_step,
        start_state,
        (
            lax.all_gather(key_rows, "win", axis=0, tiled=True),
            lax.all_gather(value_rows, "win", axis=0, tiled=True),
        ),
    )
    log_total = highest + jnp.log(totals)
    attended = (summed / totals.T[..., None]).astype(jnp.bfloat16)
    grad_rows = unpack(
        lax.all_to_all(pack(out_grad), "win", split_axis=0, concat_axis=0, tiled=True)
    )
    grad_heads = heads_view(grad_rows)
    inner = jnp.sum(grad_heads.astype(jnp.float32) * attended.astype(jnp.float32), axis=-1).T

    def query_step(carried, current):
        block_keys, block_values = current
        key_heads = heads_view(block_keys)
        scores = (
            jnp.einsum("qhe,khe->hqk", query_heads, key_heads, preferred_element_type=jnp.float32)
            * inv_root
        )
        weights = jnp.exp(scores - log_total[..., None]).astype(jnp.bfloat16)
        grad_scores = jnp.einsum(
            "qhe,khe->hqk", grad_heads, heads_view(block_values), preferred_element_type=jnp.float32
        )
        grad_logits = (
            weights.astype(jnp.float32) * (grad_scores - inner[..., None]) * inv_root
        ).astype(jnp.bfloat16)
        return carried + jnp.einsum(
            "hqk,khe->qhe", grad_logits, key_heads, preferred_element_type=jnp.float32
        )

    query_zero = jnp.zeros((own_rows, head_count, HEAD_DIM), jnp.float32)
    grad_query = fold_blocks(
        query_step,
        query_zero,
        (
            lax.all_gather(key_rows, "win", axis=0, tiled=True),
            lax.all_gather(value_rows, "win", axis=0, tiled=True),
        ),
    )
    all_log, all_inner = (
        lax.all_gather(log_total.T, "win", axis=0, tiled=True),
        lax.all_gather(inner.T, "win", axis=0, tiled=True),
    )
    own_key_heads = heads_view(key_rows)
    own_value_heads = heads_view(value_rows)

    def key_step(carried, current):
        key_total, value_total = carried
        block_queries, block_grads, block_log, block_inner = current
        query_block = heads_view(block_queries)
        grad_block = heads_view(block_grads)
        scores = (
            jnp.einsum(
                "khe,qhe->hkq", own_key_heads, query_block, preferred_element_type=jnp.float32
            )
            * inv_root
        )
        weights = jnp.exp(scores - block_log.T[:, None, :]).astype(jnp.bfloat16)
        value_total = value_total + jnp.einsum(
            "hkq,qhe->khe", weights, grad_block, preferred_element_type=jnp.float32
        )
        grad_scores = jnp.einsum(
            "khe,qhe->hkq", own_value_heads, grad_block, preferred_element_type=jnp.float32
        )
        grad_logits = (
            weights.astype(jnp.float32) * (grad_scores - block_inner.T[:, None, :]) * inv_root
        ).astype(jnp.bfloat16)
        key_total = key_total + jnp.einsum(
            "hkq,qhe->khe", grad_logits, query_block, preferred_element_type=jnp.float32
        )
        return (key_total, value_total)

    key_rows_count = key_rows.shape[0]
    empty_grads = jnp.zeros((key_rows_count, head_count, HEAD_DIM), jnp.float32)
    key_total, value_total = fold_blocks(
        key_step,
        (empty_grads, empty_grads),
        (
            lax.all_gather(query_rows, "win", axis=0, tiled=True),
            lax.all_gather(grad_rows, "win", axis=0, tiled=True),
            all_log,
            all_inner,
        ),
    )
    grad_key = key_total.reshape(key_rows_count, feat_dev).astype(jnp.bfloat16)
    grad_value = value_total.reshape(key_rows_count, feat_dev).astype(jnp.bfloat16)
    attended_flat = attended.reshape(own_rows, feat_dev)
    grad_query_flat = grad_query.reshape(own_rows, feat_dev).astype(jnp.bfloat16)
    back_attended, back_query, back_key, back_value = (
        lax.all_to_all(repack(attended_flat), "win", split_axis=0, concat_axis=0, tiled=True),
        lax.all_to_all(repack(grad_query_flat), "win", split_axis=0, concat_axis=0, tiled=True),
        lax.all_to_all(repack(grad_key), "win", split_axis=0, concat_axis=0, tiled=True),
        lax.all_to_all(repack(grad_value), "win", split_axis=0, concat_axis=0, tiled=True),
    )
    grad_key_out = place(back_key)
    grad_value_out = place(back_value)
    return (place(back_attended), place(back_query), grad_key_out, grad_value_out)


def solution(mesh):
    placed = (
        P(("groups", "samp"), "win", "head"),
        P(("groups", "samp"), "win", "head"),
        P(("groups", "samp"), "win", "head"),
        P(("groups", "samp"), "win", "head"),
        P(("groups", "samp"), "win"),
    )
    return jax.shard_map(
        shards,
        mesh=mesh,
        in_specs=placed,
        out_specs=(
            P(("groups", "samp"), "win", "head"),
            P(("groups", "samp"), "win", "head"),
            P(("groups", "samp"), "win", "head"),
            P(("groups", "samp"), "win", "head"),
        ),
        check_vma=False,
    )
```

profile of v0, /device:TPU:0, one launch (start us, length us, event | category | flops | bytes accessed | tf_op | source)
XLA Modules:
  0.0 189.9 jit_solution(12656629376011903870)
XLA Ops:
  0.7 0.7 copy-done.4
  3.2 1.4 dynamic-update-slice
  4.6 9.9 %all-reduce = s32[4]{0:T(128)S(1)} all-reduce(s32[4]{0:T(128)S(1)} %dynamic-update-slice), channel_id=1, replica_groups=mesh['groups'=2,'win'=4,'samp'=2,'head'=2] {'win'}, use_global_device_ids=true, to_apply=%add | all-reduce | flops 4 | bytes 32
  16.7 0.8 fusion.74
  17.5 0.7 fusion.93
  18.3 2.5 %sort.17 = (s32[128]{0:T(128)}, s32[128]{0:T(128)S(1)}) sort(s32[128]{0:T(128)S(1)} %get-tuple-element.103, s32[128]{0:T(128)S(1)} %iota.75), dimensions={0}, to_apply=%region_2.3 | sort | flops 896 | bytes 2048 | tf_op jit(solution)/shard_map/jit(argsort)/sort | solution.py:40
  20.8 1.2 gather_fusion
  22.3 0.9 gather_fusion.9
  23.2 0.9 gather_fusion.5
  24.1 0.9 gather_fusion.3
  25.0 0.9 gather_fusion.1
  25.9 1.0 broadcast_select_fusion
  26.9 3.3 %all-to-all-start.1 = ((bf16[4,32,640]{2,1,0:T(8,128)(2,1)}), bf16[4,32,640]{2,1,0:T(8,128)(2,1)S(1)}, u32[]{:S(2)}, u32[]{:S(2)}) async-start(bf16[4,32,640]{2,1,0:T(8,128)(2,1)} %get-tuple-element.81), calls=%async_computation.1 | async-start | bytes 327680 | tf_op jit(solution)/shard_map/all_to_all | solution.py:89
  30.3 0.7 fusion.106
  31.0 2.6 %fusion.72 = (s32[128]{0:T(128)S(1)}, s32[128]{0:T(128)S(1)}) fusion(s32[]{:T(128)} %bitcast.5, s32[]{:T(128)} %bitcast.6, s32[]{:T(128)} %bitcast.8, s32[]{:T(128)} %bitcast.7, s32[]{:T(128)S(6)} %axis_index.15), kind=kLoop, calls=%fused_computation.138 | loop fusion | flops 7040 | bytes 1044 | tf_op jit(solution)/shard_map/select_n | solution.py:70
  33.6 2.5 %fusion.102 = s32[64]{0:T(128)S(1)} fusion(s32[64]{0:T(128)S(1)} %convert_reduce_fusion, s32[]{:T(128)} %bitcast.5, s32[]{:T(128)} %bitcast.6, s32[]{:T(128)} %bitcast.8, s32[]{:T(128)} %bitcast.7, s32[]{:T(128)S(6)} %axis_index.15), kind=kLoop, calls=%fused_computation.206 | loop fusion | flops 2880 | bytes 532 | tf_op jit(solution)/shard_map/select_n | solution.py:61
  36.2 4.9 %all-to-all-start = ((bf16[4,32,640]{2,1,0:T(8,128)(2,1)}), bf16[4,32,640]{2,1,0:T(8,128)(2,1)S(1)}, u32[]{:S(2)}, u32[]{:S(2)}) async-start(bf16[4,32,640]{2,1,0:T(8,128)(2,1)} %get-tuple-element.83), calls=%async_computation | async-start | bytes 327680 | tf_op jit(solution)/shard_map/all_to_all | solution.py:88
  41.2 2.5 %select_reduce_fusion = s32[128]{0:T(128)S(1)} fusion(s32[]{:T(128)} %bitcast.9, s32[]{:T(128)} %bitcast.10, s32[]{:T(128)} %bitcast.12, s32[]{:T(128)} %bitcast.11), kind=kLoop, calls=%fused_computation.139 | loop fusion | flops 2176 | bytes 528 | tf_op jit(solution)/shard_map/gather | solution.py:66
  43.9 0.7 gather_fusion.4
  44.6 2.6 %all-to-all-done = bf16[4,32,640]{2,1,0:T(8,128)(2,1)S(1)} async-done(((bf16[4,32,640]{2,1,0:T(8,128)(2,1)}), bf16[4,32,640]{2,1,0:T(8,128)(2,1)S(1)}, u32[]{:S(2)}, u32[]{:S(2)}) %all-to-all-start) | async-done | bytes 163872 | tf_op jit(solution)/shard_map/all_to_all | solution.py:88
  47.2 3.3 %all-to-all-start.4 = ((bf16[4,32,640]{2,1,0:T(8,128)(2,1)}), bf16[4,32,640]{2,1,0:T(8,128)(2,1)S(1)}, u32[]{:S(2)}, u32[]{:S(2)}) async-start(bf16[4,32,640]{2,1,0:T(8,128)(2,1)} %get-tuple-element.80), calls=%async_computation.4 | async-start | bytes 327680 | tf_op jit(solution)/shard_map/all_to_all | solution.py:137
  50.5 0.7 gather_fusion.2
  51.2 15.1 %all-gather = bf16[256,640]{1,0:T(8,128)(2,1)S(1)} all-gather(bf16[64,640]{1,0:T(8,128)(2,1)S(1)} %gather_fusion.4), channel_id=2, replica_groups=mesh['groups'=2,'win'=4,'samp'=2,'head'=2] {'win'}, dimensions={0}, use_global_device_ids=true | all-gather | bytes 409600 | tf_op jit(solution)/shard_map/all_gather | solution.py:130
  67.1 4.5 %all-to-all-start.2 = ((bf16[4,32,640]{2,1,0:T(8,128)(2,1)}), bf16[4,32,640]{2,1,0:T(8,128)(2,1)S(1)}, u32[]{:S(2)}, u32[]{:S(2)}) async-start(bf16[4,32,640]{2,1,0:T(8,128)(2,1)} %get-tuple-element.82), calls=%async_computation.2 | async-start | bytes 327680 | tf_op jit(solution)/shard_map/all_to_all | solution.py:90
  71.6 15.7 %all-gather.2 = bf16[256,640]{1,0:T(8,128)(2,1)S(1)} all-gather(bf16[64,640]{1,0:T(8,128)(2,1)S(1)} %gather_fusion.2), channel_id=4, replica_groups=mesh['groups'=2,'win'=4,'samp'=2,'head'=2] {'win'}, dimensions={0}, use_global_device_ids=true | all-gather | bytes 409600 | tf_op jit(solution)/shard_map/all_gather | solution.py:208
  87.3 0.7 gather_fusion.10
  88.0 0.7 gather_fusion.6
  88.9 14.0 %all-gather.1 = bf16[256,640]{1,0:T(8,128)(2,1)S(1)} all-gather(bf16[64,640]{1,0:T(8,128)(2,1)S(1)} %gather_fusion.6), channel_id=3, replica_groups=mesh['groups'=2,'win'=4,'samp'=2,'head'=2] {'win'}, dimensions={0}, use_global_device_ids=true | all-gather | bytes 409600 | tf_op jit(solution)/shard_map/all_gather | solution.py:131
  103.1 13.2 %all-gather.4 = f32[4,64,5]{1,2,0:T(8,128)S(1)} all-gather(f32[1,64,5]{1,2,0:T(8,128)S(1)} %get-tuple-element.60), channel_id=1, replica_groups=mesh['groups'=2,'win'=4,'samp'=2,'head'=2] {'win'}, dimensions={0}, use_global_device_ids=true | all-gather | bytes 6400 | tf_op jit(solution)/shard_map/all_gather | solution.py:170
  116.4 14.0 %all-gather.3 = bf16[256,640]{1,0:T(8,128)(2,1)S(1)} all-gather(bf16[64,640]{1,0:T(8,128)(2,1)S(1)} %gather_fusion.10), channel_id=5, replica_groups=mesh['groups'=2,'win'=4,'samp'=2,'head'=2] {'win'}, dimensions={0}, use_global_device_ids=true | all-gather | bytes 409600 | tf_op jit(solution)/shard_map/all_gather | solution.py:209
  131.2 13.1 %all-gather.5 = f32[4,64,5]{1,2,0:T(8,128)S(1)} all-gather(f32[1,64,5]{1,2,0:T(8,128)S(1)} %bitcast.203), channel_id=1, replica_groups=mesh['groups'=2,'win'=4,'samp'=2,'head'=2] {'win'}, dimensions={0}, use_global_device_ids=true | all-gather | bytes 6400 | tf_op jit(solution)/shard_map/all_gather | solution.py:171
  144.4 0.9 gather_fusion.11
  145.3 0.9 gather_fusion.7
  147.2 0.9 gather_fusion.13
  148.1 0.9 gather_fusion.15
  149.0 0.9 broadcast_select_fusion.4
  149.9 10.5 %all_to_all.72 = bf16[4,32,640]{2,1,0:T(8,128)(2,1)S(1)} all-to-all(bf16[4,32,640]{2,1,0:T(8,128)(2,1)S(1)} %get-tuple-element.67), channel_id=1, replica_groups=mesh['groups'=2,'win'=4,'samp'=2,'head'=2] {'win'}, dimensions={0} | all-to-all | bytes 327680 | tf_op jit(solution)/shard_map/all_to_all | solution.py:222
  160.3 9.1 %all_to_all.73 = bf16[4,32,640]{2,1,0:T(8,128)(2,1)S(1)} all-to-all(bf16[4,32,640]{2,1,0:T(8,128)(2,1)S(1)} %get-tuple-element.68), channel_id=1, replica_groups=mesh['groups'=2,'win'=4,'samp'=2,'head'=2] {'win'}, dimensions={0} | all-to-all | bytes 327680 | tf_op jit(solution)/shard_map/all_to_all | solution.py:220
  169.4 3.3 %all-to-all-start.6 = ((bf16[4,32,640]{2,1,0:T(8,128)(2,1)}), bf16[4,32,640]{2,1,0:T(8,128)(2,1)S(1)}, u32[]{:S(2)}, u32[]{:S(2)}) async-start(bf16[4,32,640]{2,1,0:T(8,128)(2,1)} %get-tuple-element.78), calls=%async_computation.6 | async-start | bytes 327680 | tf_op jit(solution)/shard_map/all_to_all | solution.py:221
  173.0 0.9 fusion.73
  173.9 4.8 %all-to-all-done.6 = bf16[4,32,640]{2,1,0:T(8,128)(2,1)S(1)} async-done(((bf16[4,32,640]{2,1,0:T(8,128)(2,1)}), bf16[4,32,640]{2,1,0:T(8,128)(2,1)S(1)}, u32[]{:S(2)}, u32[]{:S(2)}) %all-to-all-start.6) | async-done | bytes 163872 | tf_op jit(solution)/shard_map/all_to_all | solution.py:221
  178.7 3.3 %all-to-all-start.3 = ((bf16[4,32,640]{2,1,0:T(8,128)(2,1)}), bf16[4,32,640]{2,1,0:T(8,128)(2,1)S(1)}, u32[]{:S(2)}, u32[]{:S(2)}) async-start(bf16[4,32,640]{2,1,0:T(8,128)(2,1)} %get-tuple-element.79), calls=%async_computation.3 | async-start | bytes 327680 | tf_op jit(solution)/shard_map/all_to_all | solution.py:219
  182.1 0.9 gather_fusion.16
  183.0 0.9 gather_fusion.12
  183.9 0.9 gather_fusion.14
  184.8 3.3 %all-to-all-done.3 = bf16[4,32,640]{2,1,0:T(8,128)(2,1)S(1)} async-done(((bf16[4,32,640]{2,1,0:T(8,128)(2,1)}), bf16[4,32,640]{2,1,0:T(8,128)(2,1)S(1)}, u32[]{:S(2)}, u32[]{:S(2)}) %all-to-all-start.3) | async-done | bytes 163872 | tf_op jit(solution)/shard_map/all_to_all | solution.py:219
  188.1 0.9 gather_fusion.8
  188.9 1.0 bitcast_select_fusion
  (57 shorter events, 6.7 us)
Async XLA Ops:
  0.6 21.7 %copy-start = (bf16[1,128,640]{2,1,0:T(8,128)(2,1)S(1)}, bf16[1,128,640]{2,1,0:T(8,128)(2,1)}, u32[]{:S(2)}) copy-start(bf16[1,128,640]{2,1,0:T(8,128)(2,1)} %param.8) | copy-start | bytes 491524
  0.7 0.7 copy-start.4
  2.0 0.7 copy-start.5
  22.3 0.9 copy-start.1
  23.2 0.9 copy-start.2
  24.1 0.9 copy-start.3
  26.9 9.3 %all-to-all-start.1 = ((bf16[4,32,640]{2,1,0:T(8,128)(2,1)}), bf16[4,32,640]{2,1,0:T(8,128)(2,1)S(1)}, u32[]{:S(2)}, u32[]{:S(2)}) async-start(bf16[4,32,640]{2,1,0:T(8,128)(2,1)} %get-tuple-element.81), calls=%async_computation.1 | async-start | bytes 327680 | tf_op jit(solution)/shard_map/all_to_all | solution.py:89
  36.2 10.9 %all-to-all-start = ((bf16[4,32,640]{2,1,0:T(8,128)(2,1)}), bf16[4,32,640]{2,1,0:T(8,128)(2,1)S(1)}, u32[]{:S(2)}, u32[]{:S(2)}) async-start(bf16[4,32,640]{2,1,0:T(8,128)(2,1)} %get-tuple-element.83), calls=%async_computation | async-start | bytes 327680 | tf_op jit(solution)/shard_map/all_to_all | solution.py:88
  47.2 19.9 %all-to-all-start.4 = ((bf16[4,32,640]{2,1,0:T(8,128)(2,1)}), bf16[4,32,640]{2,1,0:T(8,128)(2,1)S(1)}, u32[]{:S(2)}, u32[]{:S(2)}) async-start(bf16[4,32,640]{2,1,0:T(8,128)(2,1)} %get-tuple-element.80), calls=%async_computation.4 | async-start | bytes 327680 | tf_op jit(solution)/shard_map/all_to_all | solution.py:137
  67.1 20.9 %all-to-all-start.2 = ((bf16[4,32,640]{2,1,0:T(8,128)(2,1)}), bf16[4,32,640]{2,1,0:T(8,128)(2,1)S(1)}, u32[]{:S(2)}, u32[]{:S(2)}) async-start(bf16[4,32,640]{2,1,0:T(8,128)(2,1)} %get-tuple-element.82), calls=%async_computation.2 | async-start | bytes 327680 | tf_op jit(solution)/shard_map/all_to_all | solution.py:90
  169.4 9.3 %all-to-all-start.6 = ((bf16[4,32,640]{2,1,0:T(8,128)(2,1)}), bf16[4,32,640]{2,1,0:T(8,128)(2,1)S(1)}, u32[]{:S(2)}, u32[]{:S(2)}) async-start(bf16[4,32,640]{2,1,0:T(8,128)(2,1)} %get-tuple-element.78), calls=%async_computation.6 | async-start | bytes 327680 | tf_op jit(solution)/shard_map/all_to_all | solution.py:221
  178.7 9.3 %all-to-all-start.3 = ((bf16[4,32,640]{2,1,0:T(8,128)(2,1)}), bf16[4,32,640]{2,1,0:T(8,128)(2,1)S(1)}, u32[]{:S(2)}, u32[]{:S(2)}) async-start(bf16[4,32,640]{2,1,0:T(8,128)(2,1)} %get-tuple-element.79), calls=%async_computation.3 | async-start | bytes 327680 | tf_op jit(solution)/shard_map/all_to_all | solution.py:219
where the time goes:
time: 191 us; the launch traced here: 190 us
  blocking collectives  115 us (60%)
  starting transfers between devices  22.8 us (12%)
  local copies, waits for them, and re-layouts  20.8 us (11%)
  other arithmetic  16.8 us (9%)
  waiting for transfers between devices  10.8 us (6%)
  between operations  2.26 us (1%)
    all_gather x1, blocking collectives, shards(): lax.all_gather(query_rows, 'win', axis=0, tiled=True)  15.7 us
    all_gather x1, blocking collectives, shards(): lax.all_gather(key_rows, 'win', axis=0, tiled=True)  15.1 us
    all_gather x1, blocking collectives, shards(): lax.all_gather(grad_rows, 'win', axis=0, tiled=True)  14 us
    all_gather x1, blocking collectives, shards(): lax.all_gather(value_rows, 'win', axis=0, tiled=True)  14 us
    all_gather x1, blocking collectives, shards(): lax.all_gather(log_total.T, 'win', axis=0, tiled=True)  13.2 us
    all_gather x1, blocking collectives, shards(): lax.all_gather(inner.T, 'win', axis=0, tiled=True)  13.1 us
    all_to_all x1, blocking collectives, shards(): lax.all_to_all(repack(grad_value), 'win', split_axis=0, concat_axis=0, ti...  10.5 us
    unnamed x1, blocking collectives  9.89 us
  transfers between devices with their start and end apart: 6, of which 4 were waited for; matrix products, arithmetic and copies ran while one was open for 8% of the time, Pallas kernels for 0%

commit v1 on v0

--- a/solution.py
+++ b/solution.py
@@ -1,11 +1,195 @@
+import functools
 import math
 
 import jax
 import jax.numpy as jnp
 from jax import lax
+from jax.experimental import pallas as pl
+from jax.experimental.pallas import tpu as pltpu
 from jax.sharding import PartitionSpec as P
 
 HEAD_DIM = 128
+MASK_ROWS = 16
+QUAD = 4 * HEAD_DIM
+BF16 = jnp.bfloat16
+F32 = jnp.float32
+
+
+def dot(left, right, left_dim=1, right_dim=0):
+    return lax.dot_general(
+        left, right, (((left_dim,), (right_dim,)), ((), ())), preferred_element_type=F32
+    )
+
+
+def head_lanes(head):
+    return pl.ds(pl.multiple_of(head * HEAD_DIM, HEAD_DIM), HEAD_DIM)
+
+
+def attend_head(quad):
+    inv_root = 1.0 / math.sqrt(HEAD_DIM)
+    q, k, v, g = (quad[:, n * HEAD_DIM : (n + 1) * HEAD_DIM] for n in range(4))
+    scores = dot(q, k, 1, 1) * inv_root
+    highest = jnp.max(scores, axis=1, keepdims=True)
+    raised = jnp.exp(scores - highest)
+    totals = jnp.sum(raised, axis=1, keepdims=True)
+    attended = (dot(raised.astype(BF16), v) / totals).astype(BF16)
+    weights = (raised * (1.0 / totals)).astype(BF16)
+    inner = jnp.sum(g.astype(F32) * attended.astype(F32), axis=1, keepdims=True)
+    grad_scores = dot(g, v, 1, 1)
+    grad_logits = (weights.astype(F32) * (grad_scores - inner) * inv_root).astype(BF16)
+    grad_q = dot(grad_logits, k).astype(BF16)
+    grad_k = dot(grad_logits, q, 0, 0).astype(BF16)
+    grad_v = dot(weights, g, 0, 0).astype(BF16)
+    return jnp.concatenate([attended, grad_q, grad_k, grad_v], axis=1)
+
+
+def pick_matrix(masks, kept):
+    rows, tokens = masks[0].shape
+    upto = (
+        lax.broadcasted_iota(jnp.int32, (tokens, tokens), 0)
+        <= lax.broadcasted_iota(jnp.int32, (tokens, tokens), 1)
+    ).astype(BF16)
+    slot = lax.broadcasted_iota(jnp.int32, (kept, tokens), 0).astype(F32)
+    before = jnp.zeros((1, 1), F32)
+    picks = []
+    for mask in masks:
+        rank = dot(mask, upto)[0:1]
+        place = jnp.where(mask[0:1].astype(F32) > 0.5, rank + (before - 1.0), -1.0)
+        picks.append((slot == place).astype(F32).astype(BF16))
+        before = before + rank[:, tokens - 1 : tokens]
+    return jnp.concatenate(picks, axis=1)
+
+
+def gather_rows(pick, blocks):
+    return dot(pick, jnp.concatenate(blocks, axis=0)).astype(BF16)
+
+
+def pack_body(plan, q_ref, k_ref, v_ref, g_ref, mask_ref, *out_refs):
+    win_count, per, extra, tokens = plan
+    me = lax.axis_index("win")
+    mask = jnp.broadcast_to(mask_ref[...].astype(F32), (MASK_ROWS, tokens)).astype(BF16)
+    refs = (q_ref, k_ref, v_ref, g_ref)
+    for step in range(1, win_count):
+        out = out_refs[step - 1]
+        for one in range(per):
+            lanes = head_lanes((me ^ step) * per + one)
+            for n, ref in enumerate(refs):
+                at = one * QUAD + n * HEAD_DIM
+                out[0:tokens, at : at + HEAD_DIM] = ref[0, :, lanes]
+        out[tokens : tokens + MASK_ROWS, :] = jnp.zeros((MASK_ROWS, per * QUAD), BF16)
+        out[tokens : tokens + MASK_ROWS, 0:tokens] = mask
+    if extra:
+        out = out_refs[win_count - 1]
+        for one in range(extra):
+            head = win_count * per + one
+            for n, ref in enumerate(refs):
+                at = one * QUAD + n * HEAD_DIM
+                out[:, at : at + HEAD_DIM] = ref[0, :, head * HEAD_DIM : (head + 1) * HEAD_DIM]
+
+
+def main_body(plan, q_ref, k_ref, v_ref, g_ref, mask_ref, *refs):
+    win_count, per, extra, tokens = plan
+    kept = win_count * tokens // 2
+    got, outs, masks_out = refs[: win_count - 1], refs[win_count - 1 : -1], refs[-1]
+    me = lax.axis_index("win")
+    masks = [jnp.broadcast_to(mask_ref[...].astype(F32), (MASK_ROWS, tokens)).astype(BF16)]
+    masks += [ref[tokens : tokens + MASK_ROWS, 0:tokens] for ref in got]
+    for n, mask in enumerate(masks):
+        masks_out[n] = mask
+    pick = pick_matrix(masks, kept)
+    for one in range(per):
+        lanes = head_lanes(me * per + one)
+        mine = jnp.concatenate([ref[0, :, lanes] for ref in (q_ref, k_ref, v_ref, g_ref)], axis=1)
+        at = slice(one * QUAD, (one + 1) * QUAD)
+        result = attend_head(gather_rows(pick, [mine] + [ref[0:tokens, at] for ref in got]))
+        for n, out in enumerate(outs):
+            out[:, at] = dot(pick[:, n * tokens : (n + 1) * tokens], result, 0, 0).astype(BF16)
+
+
+def extra_body(plan, masks_ref, *refs):
+    win_count, per, extra, tokens = plan
+    kept = win_count * tokens // 2
+    blocks, out = refs[:-1], refs[-1]
+    pick = pick_matrix([masks_ref[n] for n in range(win_count)], kept)
+    for one in range(extra):
+        at = slice(one * QUAD, (one + 1) * QUAD)
+        result = attend_head(gather_rows(pick, [ref[:, at] for ref in blocks]))
+        out[:, at] = dot(pick[:, 0:tokens], result, 0, 0).astype(BF16)
+
+
+def place_body(plan, *refs):
+    win_count, per, extra, tokens = plan
+    backs, outs = refs[:-4], refs[-4:]
+    me = lax.axis_index("win")
+    for step in range(win_count):
+        for one in range(per):
+            lanes = head_lanes((me ^ step) * per + one)
+            for n, out in enumerate(outs):
+                at = one * QUAD + n * HEAD_DIM
+                out[0, :, lanes] = backs[step][:, at : at + HEAD_DIM]
+    for one in range(extra):
+        head = win_count * per + one
+        for n, out in enumerate(outs):
+            at = one * QUAD + n * HEAD_DIM
+            out[0, :, head * HEAD_DIM : (head + 1) * HEAD_DIM] = backs[win_count][:, at : at + HEAD_DIM]
+
+
+def exchange(array, step):
+    count = lax.axis_size("win")
+    return lax.ppermute(array, "win", [(n, n ^ step) for n in range(count)])
+
+
+def shards_by_head(queries, key_vectors, value_vectors, out_grad, keep_mask):
+    win_count = lax.axis_size("win")
+    tokens, feat_dev = queries.shape[1:]
+    head_count = feat_dev // HEAD_DIM
+    per, extra = head_count // win_count, head_count % win_count
+    plan = (win_count, per, extra, tokens)
+    steps = range(1, win_count)
+    arrays = (queries, key_vectors, value_vectors, out_grad)
+    kept = win_count * tokens // 2
+    cost = pl.CostEstimate(
+        flops=2 * kept * kept * HEAD_DIM * 12, bytes_accessed=1 << 20, transcendentals=kept * kept
+    )
+
+    def call(body, out_shape, *operands):
+        return pl.pallas_call(
+            functools.partial(body, plan), out_shape=out_shape, cost_estimate=cost
+        )(*operands)
+
+    def shape(rows, heads):
+        return jax.ShapeDtypeStruct((rows, heads * QUAD), BF16)
+
+    packed = call(
+        pack_body,
+        [shape(tokens + MASK_ROWS, per)] * (win_count - 1) + [shape(tokens, extra)] * bool(extra),
+        *arrays,
+        keep_mask,
+    )
+    got = {step: exchange(packed[step - 1], step) for step in reversed(steps)}
+    blocks = {0: packed[-1]}
+    if extra:
+        span = win_count // 2
+        while span:
+            for have in sorted(blocks):
+                blocks[have ^ span] = exchange(blocks[have], span)
+            span //= 2
+    *results, masks = call(
+        main_body,
+        [shape(tokens, per)] * win_count
+        + [jax.ShapeDtypeStruct((win_count, MASK_ROWS, tokens), BF16)],
+        *arrays,
+        keep_mask,
+        *[got[step] for step in steps],
+    )
+    backs = [results[0]] + [exchange(results[step], step) for step in steps]
+    if extra:
+        backs.append(
+            call(extra_body, shape(tokens, extra), masks, *[blocks[n] for n in range(win_count)])
+        )
+    return call(
+        place_body, [jax.ShapeDtypeStruct(queries.shape, BF16)] * 4, *backs
+    )
 
 
 def fold_blocks(step_fn, carried, arrays):
@@ -226,6 +410,15 @@
     return (place(back_attended), place(back_query), grad_key_out, grad_value_out)
 
 
+def by_plan(queries, key_vectors, value_vectors, out_grad, keep_mask):
+    win_count = lax.axis_size("win")
+    enough = queries.shape[2] // HEAD_DIM >= win_count
+    paired = win_count > 1 and win_count & (win_count - 1) == 0
+    shaped = queries.shape[1] % 16 == 0 and queries.shape[1] == HEAD_DIM
+    run = shards_by_head if enough and paired and shaped else shards
+    return run(queries, key_vectors, value_vectors, out_grad, keep_mask)
+
+
 def solution(mesh):
     placed = (
         P(("groups", "samp"), "win", "head"),
@@ -235,7 +428,7 @@
         P(("groups", "samp"), "win"),
     )
     return jax.shard_map(
-        shards,
+        by_plan,
         mesh=mesh,
         in_specs=placed,
         out_specs=(

time: 191 us -> 48.9 us (0.26)
  blocking collectives: 115 us -> 0 us
  local copies, waits for them, and re-layouts: 20.8 us -> 2.73 us
  other arithmetic: 16.8 us -> 0 us
  Pallas kernels: 0 us -> 10.7 us
  waiting for transfers between devices: 10.8 us -> 20 us
  starting transfers between devices: 22.8 us -> 14.5 us
    all_gather x6 -> x0, blocking collectives: 85.2 us -> none  [the longest x1 15.7 us: shards(): lax.all_gather(query_rows, 'win', axis=0, tiled=True)]
    all_to_all x6 -> x0, starting transfers between devices: 22.8 us -> none  [the longest x1 4.92 us: shards(): lax.all_to_all(pack(queries), 'win', split_axis=0, concat_axis=0, tiled=T...]
    ppermute x0 -> x9, waiting for transfers between devices: none -> 20 us  [exchange(): return lax.ppermute(array, 'win', [(n, n ^ step) for n in range(count)])]
    all_to_all x2 -> x0, blocking collectives: 19.5 us -> none  [the longest x1 10.5 us: shards(): lax.all_to_all(repack(grad_value), 'win', split_axis=0, concat_axis=0, ti...]
    gather x22 -> x0, local copies, waits for them, and re-layouts: 16.3 us -> none  [the longest x4 3.54 us: place(): matrix[land_rows]]
    ppermute x0 -> x9, starting transfers between devices: none -> 14.5 us  [exchange(): return lax.ppermute(array, 'win', [(n, n ^ step) for n in range(count)])]
    all_to_all x6 -> x0, waiting for transfers between devices: 10.8 us -> none  [the longest x1 4.8 us: shards(): lax.all_to_all(repack(grad_key), 'win', split_axis=0, concat_axis=0, tile...]
    pallas_call x0 -> x4, Pallas kernels: none -> 10.7 us  [call(): pl.pallas_call(functools.partial(body, plan), out_shape=out_shape, cost_e...]
  transfers between devices with their start and end apart: 6 -> 9, of which waited for: 4 -> 2; matrix products, arithmetic and copies ran while one was open for 8% -> 0% of each run, Pallas kernels for 0% -> 14%
where the time goes in v1:
time: 48.9 us; the launch traced here: 48.7 us
  waiting for transfers between devices  20 us (41%)
  starting transfers between devices  14.5 us (30%)
  Pallas kernels  10.7 us (22%)
  local copies, waits for them, and re-layouts  2.73 us (6%)
  between operations  0.7 us (1%)
    ppermute x9, waiting for transfers between devices, exchange(): return lax.ppermute(array, 'win', [(n, n ^ step) for n in range(count)])  20 us
    ppermute x9, starting transfers between devices, exchange(): return lax.ppermute(array, 'win', [(n, n ^ step) for n in range(count)])  14.5 us
    pallas_call x4, Pallas kernels, call(): pl.pallas_call(functools.partial(body, plan), out_shape=out_shape, cost_e...  10.7 us
    unnamed x18, local copies, waits for them, and re-layouts  2.73 us
  transfers between devices with their start and end apart: 9, of which 2 were waited for; matrix products, arithmetic and copies ran while one was open for 0% of the time, Pallas kernels for 14%

profile of v1, /device:TPU:0, one launch (start us, length us, event | category | flops | bytes accessed | tf_op | source)
XLA Modules:
  0.0 48.7 jit_solution(14875737044126480464)
XLA Ops:
  0.6 2.1 %shard_map.84 = (bf16[144,512]{1,0:T(8,128)(2,1)}, bf16[144,512]{1,0:T(8,128)(2,1)}, bf16[144,512]{1,0:T(8,128)(2,1)}, bf16[128,512]{1,0:T(8,128)(2,1)}) custom-call(bf16[1,128,640]{2,1,0:T(8,128)(2,1)} %q_ref.3, bf16[1,128,640]{2,1,0:T(8,128)(2,1)} %k_ref.3, bf16[1,128,640]{2,1,0:T(8,128)(2,1)} %v_ref.3, bf16[1,128,640]{2,1,0:T(8,128)(2,1)} %g_ref.3, ...), custom_call_target="tpu_custom_call" | custom-call | flops 201326592 | bytes 1048576 | tf_op jit(solution)/shard_map/pallas_call | solution.py:156
  2.7 3.0 %collective-permute-start = (bf16[144,512]{1,0:T(8,128)(2,1)}, bf16[144,512]{1,0:T(8,128)(2,1)S(1)}, u32[]{:S(2)}, u32[]{:S(2)}) collective-permute-start(bf16[144,512]{1,0:T(8,128)(2,1)} %get-tuple-element.13), channel_id=1, source_target_pairs={{0,4},{4,0},{8,12},{12,8},{1,5},{5,1},{9,13},{13,9},{2,6},{6,2},{1... | collective-permute-start | bytes 442376 | tf_op jit(solution)/shard_map/ppermute | solution.py:139
  5.7 2.6 %collective-permute-start.1 = (bf16[144,512]{1,0:T(8,128)(2,1)}, bf16[144,512]{1,0:T(8,128)(2,1)S(1)}, u32[]{:S(2)}, u32[]{:S(2)}) collective-permute-start(bf16[144,512]{1,0:T(8,128)(2,1)} %get-tuple-element.14), channel_id=1, source_target_pairs={{0,8},{4,12},{8,0},{12,4},{1,9},{5,13},{9,1},{13,5},{2,10},{6,14},... | collective-permute-start | bytes 442376 | tf_op jit(solution)/shard_map/ppermute | solution.py:139
  8.3 0.0 collective-permute-start.2
  8.3 1.9 %collective-permute-start.7 = (bf16[128,512]{1,0:T(8,128)(2,1)}, bf16[128,512]{1,0:T(8,128)(2,1)S(1)}, u32[]{:S(2)}, u32[]{:S(2)}) collective-permute-start(bf16[128,512]{1,0:T(8,128)(2,1)} %get-tuple-element.21.refs_0_), channel_id=1, source_target_pairs={{0,8},{4,12},{8,0},{12,4},{1,9},{5,13},{9,1},{13,5},{2,10},{6,14},... | collective-permute-start | bytes 393224 | tf_op jit(solution)/shard_map/ppermute | solution.py:139
  10.2 2.5 %collective-permute-start.6 = (bf16[128,512]{1,0:T(8,128)(2,1)}, bf16[128,512]{1,0:T(8,128)(2,1)S(1)}, u32[]{:S(2)}, u32[]{:S(2)}) collective-permute-start(bf16[128,512]{1,0:T(8,128)(2,1)} %get-tuple-element.21.refs_0_), channel_id=1, source_target_pairs={{0,4},{4,0},{8,12},{12,8},{1,5},{5,1},{9,13},{13,9},{2,6},{6,2},{1... | collective-permute-start | bytes 393224 | tf_op jit(solution)/shard_map/ppermute | solution.py:139
  12.7 14.6 %collective-permute-done.7.refs_2_ = bf16[128,512]{1,0:T(8,128)(2,1)S(1)} collective-permute-done((bf16[128,512]{1,0:T(8,128)(2,1)}, bf16[128,512]{1,0:T(8,128)(2,1)S(1)}, u32[]{:S(2)}, u32[]{:S(2)}) %collective-permute-start.7) | collective-permute-done | bytes 131104 | tf_op jit(solution)/shard_map/ppermute | solution.py:139
  27.3 0.0 copy-start.3
  27.3 0.0 collective-permute-start.8
  27.3 0.0 collective-permute-done.refs_0_
  27.3 0.0 copy-start
  27.3 0.0 collective-permute-done.1.refs_1_
  27.3 0.0 copy-start.1
  27.3 0.0 collective-permute-done.2.refs_2_
  27.3 0.6 %copy-done = bf16[144,512]{1,0:T(8,128)(2,1)} copy-done((bf16[144,512]{1,0:T(8,128)(2,1)}, bf16[144,512]{1,0:T(8,128)(2,1)S(1)}, u32[]{:S(2)}) %copy-start) | copy-done | bytes 147480
  28.0 0.0 copy-done.1
  28.0 0.0 copy-start.2
  28.0 0.7 %copy-done.2 = bf16[144,512]{1,0:T(8,128)(2,1)} copy-done((bf16[144,512]{1,0:T(8,128)(2,1)}, bf16[144,512]{1,0:T(8,128)(2,1)S(1)}, u32[]{:S(2)}) %copy-start.2) | copy-done | bytes 147480
  28.7 3.5 %shard_map.85 = (bf16[128,512]{1,0:T(8,128)(2,1)}, bf16[128,512]{1,0:T(8,128)(2,1)}, bf16[128,512]{1,0:T(8,128)(2,1)}, bf16[128,512]{1,0:T(8,128)(2,1)}, bf16[4,16,128]{2,1,0:T(8,128)(2,1)}) custom-call(bf16[1,128,640]{2,1,0:T(8,128)(2,1)} %q_ref.3, bf16[1,128,640]{2,1,0:T(8,128)(2,1)} %k_ref.3, bf16[1,128,640]{2,1,0:T(8,128)(2,1)} %v_ref.3, ...), custom_call_target="tpu_custom_call" | custom-call | flops 201326592 | bytes 1048576 | tf_op jit(solution)/shard_map/pallas_call | solution.py:156
  32.2 0.0 copy-done.3
  32.2 2.0 %collective-permute-start.3 = (bf16[128,512]{1,0:T(8,128)(2,1)}, bf16[128,512]{1,0:T(8,128)(2,1)S(1)}, u32[]{:S(2)}, u32[]{:S(2)}) collective-permute-start(bf16[128,512]{1,0:T(8,128)(2,1)} %get-tuple-element.17), channel_id=1, source_target_pairs={{0,4},{4,0},{8,12},{12,8},{1,5},{5,1},{9,13},{13,9},{2,6},{6,2},{1... | collective-permute-start | bytes 393224 | tf_op jit(solution)/shard_map/ppermute | solution.py:139
  34.2 1.1 %collective-permute-start.4 = (bf16[128,512]{1,0:T(8,128)(2,1)}, bf16[128,512]{1,0:T(8,128)(2,1)S(1)}, u32[]{:S(2)}, u32[]{:S(2)}) collective-permute-start(bf16[128,512]{1,0:T(8,128)(2,1)} %get-tuple-element.18), channel_id=1, source_target_pairs={{0,8},{4,12},{8,0},{12,4},{1,9},{5,13},{9,1},{13,5},{2,10},{6,14},... | collective-permute-start | bytes 393224 | tf_op jit(solution)/shard_map/ppermute | solution.py:139
  35.3 1.4 %collective-permute-start.5 = (bf16[128,512]{1,0:T(8,128)(2,1)}, bf16[128,512]{1,0:T(8,128)(2,1)S(1)}, u32[]{:S(2)}, u32[]{:S(2)}) collective-permute-start(bf16[128,512]{1,0:T(8,128)(2,1)} %get-tuple-element.19), channel_id=1, source_target_pairs={{0,12},{4,8},{8,4},{12,0},{1,13},{5,9},{9,5},{13,1},{2,14},{6,10},... | collective-permute-start | bytes 393224 | tf_op jit(solution)/shard_map/ppermute | solution.py:139
  36.7 0.0 collective-permute-done.6.refs_1_
  36.7 0.0 copy-start.4
  36.7 0.0 collective-permute-done.8.refs_3_
  36.7 0.0 copy-start.5
  36.7 0.6 %copy-done.4 = bf16[128,512]{1,0:T(8,128)(2,1)} copy-done((bf16[128,512]{1,0:T(8,128)(2,1)}, bf16[128,512]{1,0:T(8,128)(2,1)S(1)}, u32[]{:S(2)}) %copy-start.4) | copy-done | bytes 131096
  37.3 0.0 copy-done.5
  37.4 3.1 %shard_map.86.refs_4_ = bf16[128,512]{1,0:T(8,128)(2,1)} custom-call(bf16[4,16,128]{2,1,0:T(8,128)(2,1)} %get-tuple-element.20.masks_ref, bf16[128,512]{1,0:T(8,128)(2,1)} %get-tuple-element.21.refs_0_, bf16[128,512]{1,0:T(8,128)(2,1)} %copy-done.4, bf16[128,512]{1,0:T(8,128)(2,1)} %copy-done.3, bf16[128,512]{1,0:T(8,128)(2,1)} %copy-done.5), custom_call_target="tpu_custom_call" | custom-call | flops 201326592 | bytes 1048576 | tf_op jit(solution)/shard_map/pallas_call | solution.py:156
  40.5 0.0 collective-permute-done.3.refs_1_
  40.5 0.0 copy-start.6
  40.5 5.4 %collective-permute-done.4.refs_2_ = bf16[128,512]{1,0:T(8,128)(2,1)S(1)} collective-permute-done((bf16[128,512]{1,0:T(8,128)(2,1)}, bf16[128,512]{1,0:T(8,128)(2,1)S(1)}, u32[]{:S(2)}, u32[]{:S(2)}) %collective-permute-start.4) | collective-permute-done | bytes 131104 | tf_op jit(solution)/shard_map/ppermute | solution.py:139
  45.9 0.0 copy-start.7
  45.9 0.0 collective-permute-done.5.refs_3_
  45.9 0.0 copy-start.8
  45.9 0.0 copy-done.6
  45.9 0.6 %copy-done.7 = bf16[128,512]{1,0:T(8,128)(2,1)} copy-done((bf16[128,512]{1,0:T(8,128)(2,1)}, bf16[128,512]{1,0:T(8,128)(2,1)S(1)}, u32[]{:S(2)}) %copy-start.7) | copy-done | bytes 131096
  46.5 0.0 copy-done.8
  46.6 2.1 %shard_map.87 = (bf16[1,128,640]{2,1,0:T(8,128)(2,1)}, bf16[1,128,640]{2,1,0:T(8,128)(2,1)}, bf16[1,128,640]{2,1,0:T(8,128)(2,1)}, bf16[1,128,640]{2,1,0:T(8,128)(2,1)}) custom-call(bf16[128,512]{1,0:T(8,128)(2,1)} %get-tuple-element.16.refs_0_, bf16[128,512]{1,0:T(8,128)(2,1)} %copy-done.6, bf16[128,512]{1,0:T(8,128)(2,1)} %copy-done.7, ...), custom_call_target="tpu_custom_call" | custom-call | flops 201326592 | bytes 1048576 | tf_op jit(solution)/shard_map/pallas_call | solution.py:156
Async XLA Ops:
  2.7 24.6 %collective-permute-start = (bf16[144,512]{1,0:T(8,128)(2,1)}, bf16[144,512]{1,0:T(8,128)(2,1)S(1)}, u32[]{:S(2)}, u32[]{:S(2)}) collective-permute-start(bf16[144,512]{1,0:T(8,128)(2,1)} %get-tuple-element.13), channel_id=1, source_target_pairs={{0,4},{4,0},{8,12},{12,8},{1,5},{5,1},{9,13},{13,9},{2,6},{6,2},{1... | collective-permute-start | bytes 442376 | tf_op jit(solution)/shard_map/ppermute | solution.py:139
  5.7 21.6 %collective-permute-start.1 = (bf16[144,512]{1,0:T(8,128)(2,1)}, bf16[144,512]{1,0:T(8,128)(2,1)S(1)}, u32[]{:S(2)}, u32[]{:S(2)}) collective-permute-start(bf16[144,512]{1,0:T(8,128)(2,1)} %get-tuple-element.14), channel_id=1, source_target_pairs={{0,8},{4,12},{8,0},{12,4},{1,9},{5,13},{9,1},{13,5},{2,10},{6,14},... | collective-permute-start | bytes 442376 | tf_op jit(solution)/shard_map/ppermute | solution.py:139
  8.3 19.0 %collective-permute-start.2 = (bf16[144,512]{1,0:T(8,128)(2,1)}, bf16[144,512]{1,0:T(8,128)(2,1)S(1)}, u32[]{:S(2)}, u32[]{:S(2)}) collective-permute-start(bf16[144,512]{1,0:T(8,128)(2,1)} %get-tuple-element.15), channel_id=1, source_target_pairs={{0,12},{4,8},{8,4},{12,0},{1,13},{5,9},{9,5},{13,1},{2,14},{6,10},... | collective-permute-start | bytes 442376 | tf_op jit(solution)/shard_map/ppermute | solution.py:139
  8.3 19.0 %collective-permute-start.7 = (bf16[128,512]{1,0:T(8,128)(2,1)}, bf16[128,512]{1,0:T(8,128)(2,1)S(1)}, u32[]{:S(2)}, u32[]{:S(2)}) collective-permute-start(bf16[128,512]{1,0:T(8,128)(2,1)} %get-tuple-element.21.refs_0_), channel_id=1, source_target_pairs={{0,8},{4,12},{8,0},{12,4},{1,9},{5,13},{9,1},{13,5},{2,10},{6,14},... | collective-permute-start | bytes 393224 | tf_op jit(solution)/shard_map/ppermute | solution.py:139
  10.2 26.5 %collective-permute-start.6 = (bf16[128,512]{1,0:T(8,128)(2,1)}, bf16[128,512]{1,0:T(8,128)(2,1)S(1)}, u32[]{:S(2)}, u32[]{:S(2)}) collective-permute-start(bf16[128,512]{1,0:T(8,128)(2,1)} %get-tuple-element.21.refs_0_), channel_id=1, source_target_pairs={{0,4},{4,0},{8,12},{12,8},{1,5},{5,1},{9,13},{13,9},{2,6},{6,2},{1... | collective-permute-start | bytes 393224 | tf_op jit(solution)/shard_map/ppermute | solution.py:139
  27.3 4.9 %copy-start.3 = (bf16[128,512]{1,0:T(8,128)(2,1)}, bf16[128,512]{1,0:T(8,128)(2,1)S(1)}, u32[]{:S(2)}) copy-start(bf16[128,512]{1,0:T(8,128)(2,1)S(1)} %collective-permute-done.7.refs_2_) | copy-start | bytes 393220
  27.3 9.4 %collective-permute-start.8 = (bf16[128,512]{1,0:T(8,128)(2,1)S(1)}, bf16[128,512]{1,0:T(8,128)(2,1)S(1)}, u32[]{:S(2)}, u32[]{:S(2)}) collective-permute-start(bf16[128,512]{1,0:T(8,128)(2,1)S(1)} %collective-permute-done.7.refs_2_), channel_id=1, source_target_pairs={{0,4},{4,0},{8,12},{12,8},{1,5},{5,1},{9,13},{13,9},{2,6},{6,2},{1... | collective-permute-start | bytes 393224 | tf_op jit(solution)/shard_map/ppermute | solution.py:139
  27.3 0.7 %copy-start = (bf16[144,512]{1,0:T(8,128)(2,1)}, bf16[144,512]{1,0:T(8,128)(2,1)S(1)}, u32[]{:S(2)}) copy-start(bf16[144,512]{1,0:T(8,128)(2,1)S(1)} %collective-permute-done.refs_0_) | copy-start | bytes 442372
  27.3 0.7 %copy-start.1 = (bf16[144,512]{1,0:T(8,128)(2,1)}, bf16[144,512]{1,0:T(8,128)(2,1)S(1)}, u32[]{:S(2)}) copy-start(bf16[144,512]{1,0:T(8,128)(2,1)S(1)} %collective-permute-done.1.refs_1_) | copy-start | bytes 442372
  28.0 0.7 %copy-start.2 = (bf16[144,512]{1,0:T(8,128)(2,1)}, bf16[144,512]{1,0:T(8,128)(2,1)S(1)}, u32[]{:S(2)}) copy-start(bf16[144,512]{1,0:T(8,128)(2,1)S(1)} %collective-permute-done.2.refs_2_) | copy-start | bytes 442372
  32.2 8.3 %collective-permute-start.3 = (bf16[128,512]{1,0:T(8,128)(2,1)}, bf16[128,512]{1,0:T(8,128)(2,1)S(1)}, u32[]{:S(2)}, u32[]{:S(2)}) collective-permute-start(bf16[128,512]{1,0:T(8,128)(2,1)} %get-tuple-element.17), channel_id=1, source_target_pairs={{0,4},{4,0},{8,12},{12,8},{1,5},{5,1},{9,13},{13,9},{2,6},{6,2},{1... | collective-permute-start | bytes 393224 | tf_op jit(solution)/shard_map/ppermute | solution.py:139
  34.2 11.7 %collective-permute-start.4 = (bf16[128,512]{1,0:T(8,128)(2,1)}, bf16[128,512]{1,0:T(8,128)(2,1)S(1)}, u32[]{:S(2)}, u32[]{:S(2)}) collective-permute-start(bf16[128,512]{1,0:T(8,128)(2,1)} %get-tuple-element.18), channel_id=1, source_target_pairs={{0,8},{4,12},{8,0},{12,4},{1,9},{5,13},{9,1},{13,5},{2,10},{6,14},... | collective-permute-start | bytes 393224 | tf_op jit(solution)/shard_map/ppermute | solution.py:139
  35.3 10.6 %collective-permute-start.5 = (bf16[128,512]{1,0:T(8,128)(2,1)}, bf16[128,512]{1,0:T(8,128)(2,1)S(1)}, u32[]{:S(2)}, u32[]{:S(2)}) collective-permute-start(bf16[128,512]{1,0:T(8,128)(2,1)} %get-tuple-element.19), channel_id=1, source_target_pairs={{0,12},{4,8},{8,4},{12,0},{1,13},{5,9},{9,5},{13,1},{2,14},{6,10},... | collective-permute-start | bytes 393224 | tf_op jit(solution)/shard_map/ppermute | solution.py:139
  36.7 0.7 %copy-start.4 = (bf16[128,512]{1,0:T(8,128)(2,1)}, bf16[128,512]{1,0:T(8,128)(2,1)S(1)}, u32[]{:S(2)}) copy-start(bf16[128,512]{1,0:T(8,128)(2,1)S(1)} %collective-permute-done.6.refs_1_) | copy-start | bytes 393220
  36.7 0.7 %copy-start.5 = (bf16[128,512]{1,0:T(8,128)(2,1)}, bf16[128,512]{1,0:T(8,128)(2,1)S(1)}, u32[]{:S(2)}) copy-start(bf16[128,512]{1,0:T(8,128)(2,1)S(1)} %collective-permute-done.8.refs_3_) | copy-start | bytes 393220
  40.5 5.4 %copy-start.6 = (bf16[128,512]{1,0:T(8,128)(2,1)}, bf16[128,512]{1,0:T(8,128)(2,1)S(1)}, u32[]{:S(2)}) copy-start(bf16[128,512]{1,0:T(8,128)(2,1)S(1)} %collective-permute-done.3.refs_1_) | copy-start | bytes 393220
  45.9 0.6 %copy-start.7 = (bf16[128,512]{1,0:T(8,128)(2,1)}, bf16[128,512]{1,0:T(8,128)(2,1)S(1)}, u32[]{:S(2)}) copy-start(bf16[128,512]{1,0:T(8,128)(2,1)S(1)} %collective-permute-done.4.refs_2_) | copy-start | bytes 393220
  45.9 0.7 %copy-start.8 = (bf16[128,512]{1,0:T(8,128)(2,1)}, bf16[128,512]{1,0:T(8,128)(2,1)S(1)}, u32[]{:S(2)}) copy-start(bf16[128,512]{1,0:T(8,128)(2,1)S(1)} %collective-permute-done.5.refs_3_) | copy-start | bytes 393220

commit v2 on v1

--- a/solution.py
+++ b/solution.py
@@ -10,6 +10,7 @@
 
 HEAD_DIM = 128
 MASK_ROWS = 16
+VMEM_BYTES = 16 << 20
 QUAD = 4 * HEAD_DIM
 BF16 = jnp.bfloat16
 F32 = jnp.float32
@@ -22,6 +23,8 @@
 
 
 def head_lanes(head):
+    if isinstance(head, int):
+        return pl.ds(head * HEAD_DIM, HEAD_DIM)
     return pl.ds(pl.multiple_of(head * HEAD_DIM, HEAD_DIM), HEAD_DIM)
 
 
@@ -60,83 +63,134 @@
     return jnp.concatenate(picks, axis=1)
 
 
-def gather_rows(pick, blocks):
-    return dot(pick, jnp.concatenate(blocks, axis=0)).astype(BF16)
-
-
-def pack_body(plan, q_ref, k_ref, v_ref, g_ref, mask_ref, *out_refs):
-    win_count, per, extra, tokens = plan
+def pieces(plan, step):
+    order, per, extra, tokens = plan
+    win_count = len(order)
+    shared = extra if step == len(order) // 2 else 0
+    return 4 * tokens * per, 4 * tokens * shared
+
+
+def pack_body(plan, q_ref, k_ref, v_ref, g_ref, mask_ref, *refs):
+    order, per, extra, tokens = plan
+    win_count = len(order)
+    outs, (mask_here, sems) = refs[:-2], refs[-2:]
     me = lax.axis_index("win")
-    mask = jnp.broadcast_to(mask_ref[...].astype(F32), (MASK_ROWS, tokens)).astype(BF16)
-    refs = (q_ref, k_ref, v_ref, g_ref)
-    for step in range(1, win_count):
-        out = out_refs[step - 1]
+    copies = [pltpu.make_async_copy(mask_ref, mask_here, sems.at[0])]
+
+    def lay(out, at, head):
+        for n, ref in enumerate((q_ref, k_ref, v_ref, g_ref)):
+            copies.append(
+                pltpu.make_async_copy(
+                    ref.at[0, :, head_lanes(head)],
+                    out.at[at + n * tokens : at + (n + 1) * tokens, :],
+                    sems.at[len(copies)],
+                )
+            )
+
+    for out, step in zip(outs, order):
+        own, shared = pieces(plan, step)
         for one in range(per):
-            lanes = head_lanes((me ^ step) * per + one)
-            for n, ref in enumerate(refs):
-                at = one * QUAD + n * HEAD_DIM
-                out[0:tokens, at : at + HEAD_DIM] = ref[0, :, lanes]
-        out[tokens : tokens + MASK_ROWS, :] = jnp.zeros((MASK_ROWS, per * QUAD), BF16)
-        out[tokens : tokens + MASK_ROWS, 0:tokens] = mask
-    if extra:
-        out = out_refs[win_count - 1]
-        for one in range(extra):
-            head = win_count * per + one
-            for n, ref in enumerate(refs):
-                at = one * QUAD + n * HEAD_DIM
-                out[:, at : at + HEAD_DIM] = ref[0, :, head * HEAD_DIM : (head + 1) * HEAD_DIM]
-
-
-def main_body(plan, q_ref, k_ref, v_ref, g_ref, mask_ref, *refs):
-    win_count, per, extra, tokens = plan
+            lay(out, 4 * tokens * one, (me ^ step) * per + one)
+        for one in range(extra if shared else 0):
+            lay(out, own + MASK_ROWS + 4 * tokens * one, win_count * per + one)
+    for one in range(extra):
+        lay(outs[win_count], 4 * tokens * one, win_count * per + one)
+    for copy in copies:
+        copy.start()
+    copies[0].wait()
+    mask = jnp.broadcast_to(mask_here[...].astype(F32), (MASK_ROWS, tokens)).astype(BF16)
+    own, _ = pieces(plan, 0)
+    for out in outs[:win_count]:
+        out[own : own + MASK_ROWS, :] = mask
+    for copy in copies[1:]:
+        copy.wait()
+
+
+def quads(refs, at, tokens):
+    return jnp.concatenate(
+        [
+            jnp.concatenate(
+                [ref[start + n * tokens : start + (n + 1) * tokens, :] for n in range(4)], axis=1
+            )
+            for ref, start in zip(refs, at)
+        ],
+        axis=0,
+    )
+
+
+def put_back(out, at, pick, result, tokens):
+    rows = dot(pick, result, 0, 0).astype(BF16)
+    for n in range(4):
+        out[at + n * tokens : at + (n + 1) * tokens, :] = rows[:, n * HEAD_DIM : (n + 1) * HEAD_DIM]
+
+
+def main_body(plan, *refs):
+    order, per, extra, tokens = plan
+    win_count = len(order)
     kept = win_count * tokens // 2
-    got, outs, masks_out = refs[: win_count - 1], refs[win_count - 1 : -1], refs[-1]
-    me = lax.axis_index("win")
-    masks = [jnp.broadcast_to(mask_ref[...].astype(F32), (MASK_ROWS, tokens)).astype(BF16)]
-    masks += [ref[tokens : tokens + MASK_ROWS, 0:tokens] for ref in got]
+    got, outs, masks_out = refs[:win_count], refs[win_count:-1], refs[-1]
+    own, _ = pieces(plan, 0)
+    masks = [ref[own : own + MASK_ROWS, :] for ref in got]
     for n, mask in enumerate(masks):
         masks_out[n] = mask
     pick = pick_matrix(masks, kept)
     for one in range(per):
-        lanes = head_lanes(me * per + one)
-        mine = jnp.concatenate([ref[0, :, lanes] for ref in (q_ref, k_ref, v_ref, g_ref)], axis=1)
-        at = slice(one * QUAD, (one + 1) * QUAD)
-        result = attend_head(gather_rows(pick, [mine] + [ref[0:tokens, at] for ref in got]))
+        at = 4 * tokens * one
+        rows = dot(pick, quads(got, [at] * win_count, tokens)).astype(BF16)
+        result = attend_head(rows)
         for n, out in enumerate(outs):
-            out[:, at] = dot(pick[:, n * tokens : (n + 1) * tokens], result, 0, 0).astype(BF16)
+            put_back(out, at, pick[:, n * tokens : (n + 1) * tokens], result, tokens)
 
 
 def extra_body(plan, masks_ref, *refs):
-    win_count, per, extra, tokens = plan
+    order, per, extra, tokens = plan
+    win_count = len(order)
     kept = win_count * tokens // 2
     blocks, out = refs[:-1], refs[-1]
     pick = pick_matrix([masks_ref[n] for n in range(win_count)], kept)
+    own, _ = pieces(plan, 0)
     for one in range(extra):
-        at = slice(one * QUAD, (one + 1) * QUAD)
-        result = attend_head(gather_rows(pick, [ref[:, at] for ref in blocks]))
-        out[:, at] = dot(pick[:, 0:tokens], result, 0, 0).astype(BF16)
+        at = 4 * tokens * one
+        starts = [at + (own + MASK_ROWS if pieces(plan, step)[1] else 0) for step in order]
+        rows = dot(pick, quads(blocks, starts, tokens)).astype(BF16)
+        put_back(out, at, pick[:, 0:tokens], attend_head(rows), tokens)
 
 
 def place_body(plan, *refs):
-    win_count, per, extra, tokens = plan
-    backs, outs = refs[:-4], refs[-4:]
+    order, per, extra, tokens = plan
+    win_count = len(order)
+    backs, outs, sems = refs[:-5], refs[-5:-1], refs[-1]
     me = lax.axis_index("win")
-    for step in range(win_count):
-        for one in range(per):
-            lanes = head_lanes((me ^ step) * per + one)
-            for n, out in enumerate(outs):
-                at = one * QUAD + n * HEAD_DIM
-                out[0, :, lanes] = backs[step][:, at : at + HEAD_DIM]
-    for one in range(extra):
-        head = win_count * per + one
+    made = [
+        (back, one, head_lanes((me ^ step) * per + one))
+        for back, step in zip(backs, order)
+        for one in range(per)
+    ]
+    made += [(backs[win_count], one, head_lanes(win_count * per + one)) for one in range(extra)]
+    copies = []
+    for back, one, lanes in made:
         for n, out in enumerate(outs):
-            at = one * QUAD + n * HEAD_DIM
-            out[0, :, head * HEAD_DIM : (head + 1) * HEAD_DIM] = backs[win_count][:, at : at + HEAD_DIM]
+            at = (4 * one + n) * tokens
+            copies.append(
+                pltpu.make_async_copy(
+                    back.at[at : at + tokens, :], out.at[0, :, lanes], sems.at[len(copies)]
+                )
+            )
+    for copy in copies:
+        copy.start()
+    for copy in copies:
+        copy.wait()
 
 
 def exchange(array, step):
+    if step == 0:
+        return array
     count = lax.axis_size("win")
     return lax.ppermute(array, "win", [(n, n ^ step) for n in range(count)])
+
+
+def after(array, other):
+    return lax.optimization_barrier((array, other))
 
 
 def shards_by_head(queries, key_vectors, value_vectors, out_grad, keep_mask):
@@ -144,51 +198,70 @@
     tokens, feat_dev = queries.shape[1:]
     head_count = feat_dev // HEAD_DIM
     per, extra = head_count // win_count, head_count % win_count
-    plan = (win_count, per, extra, tokens)
-    steps = range(1, win_count)
+    order = [0,2,1,3]
+    plan = (order, per, extra, tokens)
     arrays = (queries, key_vectors, value_vectors, out_grad)
     kept = win_count * tokens // 2
     cost = pl.CostEstimate(
         flops=2 * kept * kept * HEAD_DIM * 12, bytes_accessed=1 << 20, transcendentals=kept * kept
     )
-
-    def call(body, out_shape, *operands):
+    in_hbm = pl.BlockSpec(memory_space=pltpu.HBM)
+
+    def call(body, out_shape, *operands, **specs):
         return pl.pallas_call(
-            functools.partial(body, plan), out_shape=out_shape, cost_estimate=cost
+            functools.partial(body, plan),
+            out_shape=out_shape,
+            cost_estimate=cost,
+            compiler_params=pltpu.CompilerParams(vmem_limit_bytes=VMEM_BYTES),
+            **specs,
         )(*operands)
 
-    def shape(rows, heads):
-        return jax.ShapeDtypeStruct((rows, heads * QUAD), BF16)
-
+    def shape(rows):
+        return jax.ShapeDtypeStruct((rows, HEAD_DIM), BF16)
+
+    sent = [sum(pieces(plan, step)) + MASK_ROWS for step in order]
+    shared = sum(bool(pieces(plan, step)[1]) for step in order)
     packed = call(
         pack_body,
-        [shape(tokens + MASK_ROWS, per)] * (win_count - 1) + [shape(tokens, extra)] * bool(extra),
-        *arrays,
-        keep_mask,
-    )
-    got = {step: exchange(packed[step - 1], step) for step in reversed(steps)}
-    blocks = {0: packed[-1]}
+        [shape(rows) for rows in sent] + [shape(4 * tokens * extra)] * bool(extra),
+        *[pltpu.with_memory_space_constraint(one, pltpu.HBM) for one in (*arrays, keep_mask)],
+        in_specs=[in_hbm] * 5,
+        scratch_shapes=[
+            pltpu.VMEM(keep_mask.shape, keep_mask.dtype),
+            pltpu.SemaphoreType.DMA((1 + 4 * (head_count + extra * shared),)),
+        ],
+    )
+    got = {step: exchange(out, step) for step, out in zip(order, packed)}
     if extra:
-        span = win_count // 2
-        while span:
-            for have in sorted(blocks):
-                blocks[have ^ span] = exchange(blocks[have], span)
-            span //= 2
+        blocks = {0: packed[win_count]}
+        blocks.update({step: got[step] for step in order if pieces(plan, step)[1]})
+        for step in range(1, win_count):
+            if step not in blocks:
+                low = step & -step
+                near = blocks[step ^ low]
+                blocks[step] = exchange(near[near.shape[0] - 4 * tokens * extra :], low)
     *results, masks = call(
         main_body,
-        [shape(tokens, per)] * win_count
+        [shape(4 * tokens * per)] * win_count
         + [jax.ShapeDtypeStruct((win_count, MASK_ROWS, tokens), BF16)],
-        *arrays,
-        keep_mask,
-        *[got[step] for step in steps],
-    )
-    backs = [results[0]] + [exchange(results[step], step) for step in steps]
+        *[got[step] for step in order],
+    )
+    backs = [exchange(result, step) for step, result in zip(order, results)]
     if extra:
         backs.append(
-            call(extra_body, shape(tokens, extra), masks, *[blocks[n] for n in range(win_count)])
+            call(
+                extra_body,
+                shape(4 * tokens * extra),
+                masks,
+                *[blocks[step] for step in order],
+            )
         )
     return call(
-        place_body, [jax.ShapeDtypeStruct(queries.shape, BF16)] * 4, *backs
+        place_body,
+        [jax.ShapeDtypeStruct(queries.shape, BF16)] * 4,
+        *backs,
+        out_specs=[in_hbm] * 4,
+        scratch_shapes=[pltpu.SemaphoreType.DMA((4 * head_count,))],
     )
 
 

time: 48.9 us -> 39.9 us (0.82)
  Pallas kernels: 10.7 us -> 5.11 us
  local copies, waits for them, and re-layouts: 2.73 us -> 0.01 us
  starting transfers between devices: 14.5 us -> 12.8 us
  waiting for transfers between devices: 20 us -> 21 us
    pallas_call x4, Pallas kernels: 10.7 us -> 5.11 us  [call(): pl.pallas_call(functools.partial(body, plan), out_shape=out_shape, cost_e...]
    unnamed x18 -> x0, local copies, waits for them, and re-layouts: 2.73 us -> none
    ppermute x9 -> x8, starting transfers between devices: 14.5 us -> 12.8 us  [exchange(): return lax.ppermute(array, 'win', [(n, n ^ step) for n in range(count)])]
    ppermute x9 -> x8, waiting for transfers between devices: 20 us -> 21 us  [exchange(): return lax.ppermute(array, 'win', [(n, n ^ step) for n in range(count)])]
  transfers between devices with their start and end apart: 9 -> 8, of which waited for: 2 -> 3; matrix products, arithmetic and copies ran while one was open for 0% -> 0% of each run, Pallas kernels for 14% -> 7%
where the time goes in v2:
time: 39.9 us; the launch traced here: 39.7 us
  waiting for transfers between devices  21 us (53%)
  starting transfers between devices  12.8 us (32%)
  Pallas kernels  5.11 us (13%)
  between operations  0.69 us (2%)
    ppermute x8, waiting for transfers between devices, exchange(): return lax.ppermute(array, 'win', [(n, n ^ step) for n in range(count)])  21 us
    ppermute x8, starting transfers between devices, exchange(): return lax.ppermute(array, 'win', [(n, n ^ step) for n in range(count)])  12.8 us
    pallas_call x4, Pallas kernels, call(): pl.pallas_call(functools.partial(body, plan), out_shape=out_shape, cost_e...  5.11 us
  transfers between devices with their start and end apart: 8, of which 3 were waited for; matrix products, arithmetic and copies ran while one was open for 0% of the time, Pallas kernels for 7%

profile of v2, /device:TPU:0, one launch (start us, length us, event | category | flops | bytes accessed | tf_op | source)
XLA Modules:
  0.0 39.7 jit_solution(5057395478580498239)
XLA Ops:
  0.6 1.3 %shard_map.84 = (bf16[528,128]{1,0:T(8,128)(2,1)S(1)}, bf16[1040,128]{1,0:T(8,128)(2,1)S(1)}, bf16[528,128]{1,0:T(8,128)(2,1)S(1)}, bf16[528,128]{1,0:T(8,128)(2,1)S(1)}, bf16[512,128]{1,0:T(8,128)(2,1)S(1)}) custom-call(bf16[1,128,640]{2,1,0:T(8,128)(2,1)} %q_ref.1, bf16[1,128,640]{2,1,0:T(8,128)(2,1)} %k_ref.1, bf16[1,128,640]{2,1,0:T(8,128)(2,1)} %v_ref.1, ...), custom_call_target="tpu_custom_call" | custom-call | flops 201326592 | bytes 1048576 | tf_op jit(solution)/shard_map/pallas_call | solution.py:211
  2.0 4.1 %collective-permute-start = (bf16[1040,128]{1,0:T(8,128)(2,1)S(1)}, bf16[1040,128]{1,0:T(8,128)(2,1)S(1)}, u32[]{:S(2)}, u32[]{:S(2)}) collective-permute-start(bf16[1040,128]{1,0:T(8,128)(2,1)S(1)} %get-tuple-element.15), channel_id=1, source_target_pairs={{0,8},{4,12},{8,0},{12,4},{1,9},{5,13},{9,1},{13,5},{2,10},{6,14},... | collective-permute-start | bytes 798728 | tf_op jit(solution)/shard_map/ppermute | solution.py:189
  6.1 1.6 %collective-permute-start.1 = (bf16[528,128]{1,0:T(8,128)(2,1)S(1)}, bf16[528,128]{1,0:T(8,128)(2,1)S(1)}, u32[]{:S(2)}, u32[]{:S(2)}) collective-permute-start(bf16[528,128]{1,0:T(8,128)(2,1)S(1)} %get-tuple-element.16), channel_id=1, source_target_pairs={{0,4},{4,0},{8,12},{12,8},{1,5},{5,1},{9,13},{13,9},{2,6},{6,2},{1... | collective-permute-start | bytes 405512 | tf_op jit(solution)/shard_map/ppermute | solution.py:189
  7.7 0.0 collective-permute-start.2
  7.7 0.9 %collective-permute-start.6 = (bf16[512,128]{1,0:T(8,128)(2,1)S(1)}, bf16[512,128]{1,0:T(8,128)(2,1)S(1)}, u32[]{:S(2)}, u32[]{:S(2)}) collective-permute-start(bf16[512,128]{1,0:T(8,128)(2,1)S(1)} %get-tuple-element.23.refs_0_), channel_id=1, source_target_pairs={{0,4},{4,0},{8,12},{12,8},{1,5},{5,1},{9,13},{13,9},{2,6},{6,2},{1... | collective-permute-start | bytes 393224 | tf_op jit(solution)/shard_map/ppermute | solution.py:189
  8.6 13.4 %collective-permute-done.refs_1_ = bf16[1040,128]{1,0:T(8,128)(2,1)S(1)} collective-permute-done((bf16[1040,128]{1,0:T(8,128)(2,1)S(1)}, bf16[1040,128]{1,0:T(8,128)(2,1)S(1)}, u32[]{:S(2)}, u32[]{:S(2)}) %collective-permute-start) | collective-permute-done | bytes 266272 | tf_op jit(solution)/shard_map/ppermute | solution.py:189
  22.0 0.1 collective-permute-start.7
  22.0 0.0 collective-permute-done.1.refs_2_
  22.1 0.0 collective-permute-done.2.refs_3_
  22.1 1.4 %shard_map.85 = (bf16[512,128]{1,0:T(8,128)(2,1)S(1)}, bf16[512,128]{1,0:T(8,128)(2,1)S(1)}, bf16[512,128]{1,0:T(8,128)(2,1)S(1)}, bf16[512,128]{1,0:T(8,128)(2,1)S(1)}, bf16[4,16,128]{2,1,0:T(8,128)(2,1)S(1)}) custom-call(bf16[528,128]{1,0:T(8,128)(2,1)S(1)} %get-tuple-element.14.refs_0_, bf16[1040,128]{1,0:T(8,128)(2,1)S(1)} %collective-permute-done.refs_1_, ...), custom_call_target="tpu_custom_call" | custom-call | flops 201326592 | bytes 1048576 | tf_op jit(solution)/shard_map/pallas_call | solution.py:211
  23.5 4.7 %collective-permute-start.3 = (bf16[512,128]{1,0:T(8,128)(2,1)S(1)}, bf16[512,128]{1,0:T(8,128)(2,1)S(1)}, u32[]{:S(2)}, u32[]{:S(2)}) collective-permute-start(bf16[512,128]{1,0:T(8,128)(2,1)S(1)} %get-tuple-element.19), channel_id=1, source_target_pairs={{0,8},{4,12},{8,0},{12,4},{1,9},{5,13},{9,1},{13,5},{2,10},{6,14},... | collective-permute-start | bytes 393224 | tf_op jit(solution)/shard_map/ppermute | solution.py:189
  28.2 0.0 collective-permute-start.4
  28.2 1.5 %collective-permute-start.5 = (bf16[512,128]{1,0:T(8,128)(2,1)S(1)}, bf16[512,128]{1,0:T(8,128)(2,1)S(1)}, u32[]{:S(2)}, u32[]{:S(2)}) collective-permute-start(bf16[512,128]{1,0:T(8,128)(2,1)S(1)} %get-tuple-element.21), channel_id=1, source_target_pairs={{0,12},{4,8},{8,4},{12,0},{1,13},{5,9},{9,5},{13,1},{2,14},{6,10},... | collective-permute-start | bytes 393224 | tf_op jit(solution)/shard_map/ppermute | solution.py:189
  29.7 0.0 collective-permute-done.6.refs_2_
  29.7 0.0 collective-permute-done.7.refs_3_
  29.7 1.3 %shard_map.86.refs_4_ = bf16[512,128]{1,0:T(8,128)(2,1)S(1)} custom-call(bf16[4,16,128]{2,1,0:T(8,128)(2,1)S(1)} %get-tuple-element.22.masks_ref, bf16[512,128]{1,0:T(8,128)(2,1)S(1)} %get-tuple-element.23.refs_0_, bf16[1040,128]{1,0:T(8,128)(2,1)S(1)} %collective-permute-done.refs_1_, bf16[512,128]{1,0:T(8,128)(2,1)S(1)} %collective-permute-done.6.refs_2_, ...), custom_call_target="tpu_custom_call" | custom-call | flops 201326592 | bytes 1048576 | tf_op jit(solution)/shard_map/pallas_call | solution.py:211
  31.1 6.7 %collective-permute-done.3.refs_1_ = bf16[512,128]{1,0:T(8,128)(2,1)S(1)} collective-permute-done((bf16[512,128]{1,0:T(8,128)(2,1)S(1)}, bf16[512,128]{1,0:T(8,128)(2,1)S(1)}, u32[]{:S(2)}, u32[]{:S(2)}) %collective-permute-start.3) | collective-permute-done | bytes 131104 | tf_op jit(solution)/shard_map/ppermute | solution.py:189
  37.8 0.9 %collective-permute-done.4.refs_2_ = bf16[512,128]{1,0:T(8,128)(2,1)S(1)} collective-permute-done((bf16[512,128]{1,0:T(8,128)(2,1)S(1)}, bf16[512,128]{1,0:T(8,128)(2,1)S(1)}, u32[]{:S(2)}, u32[]{:S(2)}) %collective-permute-start.4) | collective-permute-done | bytes 131104 | tf_op jit(solution)/shard_map/ppermute | solution.py:189
  38.7 0.0 collective-permute-done.5.refs_3_
  38.7 1.0 %shard_map.87 = (bf16[1,128,640]{2,1,0:T(8,128)(2,1)}, bf16[1,128,640]{2,1,0:T(8,128)(2,1)}, bf16[1,128,640]{2,1,0:T(8,128)(2,1)}, bf16[1,128,640]{2,1,0:T(8,128)(2,1)}) custom-call(bf16[512,128]{1,0:T(8,128)(2,1)S(1)} %get-tuple-element.18.refs_0_, bf16[512,128]{1,0:T(8,128)(2,1)S(1)} %collective-permute-done.3.refs_1_, ...), custom_call_target="tpu_custom_call" | custom-call | flops 201326592 | bytes 1048576 | tf_op jit(solution)/shard_map/pallas_call | solution.py:211
  (1 shorter events, 0.0 us)
Async XLA Ops:
  2.0 20.0 %collective-permute-start = (bf16[1040,128]{1,0:T(8,128)(2,1)S(1)}, bf16[1040,128]{1,0:T(8,128)(2,1)S(1)}, u32[]{:S(2)}, u32[]{:S(2)}) collective-permute-start(bf16[1040,128]{1,0:T(8,128)(2,1)S(1)} %get-tuple-element.15), channel_id=1, source_target_pairs={{0,8},{4,12},{8,0},{12,4},{1,9},{5,13},{9,1},{13,5},{2,10},{6,14},... | collective-permute-start | bytes 798728 | tf_op jit(solution)/shard_map/ppermute | solution.py:189
  6.1 16.0 %collective-permute-start.1 = (bf16[528,128]{1,0:T(8,128)(2,1)S(1)}, bf16[528,128]{1,0:T(8,128)(2,1)S(1)}, u32[]{:S(2)}, u32[]{:S(2)}) collective-permute-start(bf16[528,128]{1,0:T(8,128)(2,1)S(1)} %get-tuple-element.16), channel_id=1, source_target_pairs={{0,4},{4,0},{8,12},{12,8},{1,5},{5,1},{9,13},{13,9},{2,6},{6,2},{1... | collective-permute-start | bytes 405512 | tf_op jit(solution)/shard_map/ppermute | solution.py:189
  7.7 14.4 %collective-permute-start.2 = (bf16[528,128]{1,0:T(8,128)(2,1)S(1)}, bf16[528,128]{1,0:T(8,128)(2,1)S(1)}, u32[]{:S(2)}, u32[]{:S(2)}) collective-permute-start(bf16[528,128]{1,0:T(8,128)(2,1)S(1)} %get-tuple-element.17), channel_id=1, source_target_pairs={{0,12},{4,8},{8,4},{12,0},{1,13},{5,9},{9,5},{13,1},{2,14},{6,10},... | collective-permute-start | bytes 405512 | tf_op jit(solution)/shard_map/ppermute | solution.py:189
  7.7 22.1 %collective-permute-start.6 = (bf16[512,128]{1,0:T(8,128)(2,1)S(1)}, bf16[512,128]{1,0:T(8,128)(2,1)S(1)}, u32[]{:S(2)}, u32[]{:S(2)}) collective-permute-start(bf16[512,128]{1,0:T(8,128)(2,1)S(1)} %get-tuple-element.23.refs_0_), channel_id=1, source_target_pairs={{0,4},{4,0},{8,12},{12,8},{1,5},{5,1},{9,13},{13,9},{2,6},{6,2},{1... | collective-permute-start | bytes 393224 | tf_op jit(solution)/shard_map/ppermute | solution.py:189
  22.0 7.8 %collective-permute-start.7 = (bf16[512,128]{1,0:T(8,128)(2,1)S(1)}, bf16[512,128]{1,0:T(8,128)(2,1)S(1)}, u32[]{:S(2)}, u32[]{:S(2)}) collective-permute-start(bf16[512,128]{1,0:T(8,128)(2,1)S(1)} %slice.4), channel_id=1, source_target_pairs={{0,4},{4,0},{8,12},{12,8},{1,5},{5,1},{9,13},{13,9},{2,6},{6,2},{1... | collective-permute-start | bytes 393224 | tf_op jit(solution)/shard_map/ppermute | solution.py:189
  23.5 14.3 %collective-permute-start.3 = (bf16[512,128]{1,0:T(8,128)(2,1)S(1)}, bf16[512,128]{1,0:T(8,128)(2,1)S(1)}, u32[]{:S(2)}, u32[]{:S(2)}) collective-permute-start(bf16[512,128]{1,0:T(8,128)(2,1)S(1)} %get-tuple-element.19), channel_id=1, source_target_pairs={{0,8},{4,12},{8,0},{12,4},{1,9},{5,13},{9,1},{13,5},{2,10},{6,14},... | collective-permute-start | bytes 393224 | tf_op jit(solution)/shard_map/ppermute | solution.py:189
  28.2 10.5 %collective-permute-start.4 = (bf16[512,128]{1,0:T(8,128)(2,1)S(1)}, bf16[512,128]{1,0:T(8,128)(2,1)S(1)}, u32[]{:S(2)}, u32[]{:S(2)}) collective-permute-start(bf16[512,128]{1,0:T(8,128)(2,1)S(1)} %get-tuple-element.20), channel_id=1, source_target_pairs={{0,4},{4,0},{8,12},{12,8},{1,5},{5,1},{9,13},{13,9},{2,6},{6,2},{1... | collective-permute-start | bytes 393224 | tf_op jit(solution)/shard_map/ppermute | solution.py:189
  28.2 10.5 %collective-permute-start.5 = (bf16[512,128]{1,0:T(8,128)(2,1)S(1)}, bf16[512,128]{1,0:T(8,128)(2,1)S(1)}, u32[]{:S(2)}, u32[]{:S(2)}) collective-permute-start(bf16[512,128]{1,0:T(8,128)(2,1)S(1)} %get-tuple-element.21), channel_id=1, source_target_pairs={{0,12},{4,8},{8,4},{12,0},{1,13},{5,9},{9,5},{13,1},{2,14},{6,10},... | collective-permute-start | bytes 393224 | tf_op jit(solution)/shard_map/ppermute | solution.py:189

commit v3 on v0

--- a/solution.py
+++ b/solution.py
@@ -1,11 +1,270 @@
+import functools
 import math
 
 import jax
 import jax.numpy as jnp
 from jax import lax
+from jax.experimental import pallas as pl
+from jax.experimental.pallas import tpu as pltpu
 from jax.sharding import PartitionSpec as P
 
 HEAD_DIM = 128
+TILE_ROWS = 16
+WINDOWS = 4
+DROPPED = 64.0
+VMEM_BYTES = 16 << 20
+BF16 = jnp.bfloat16
+F32 = jnp.float32
+
+
+def dot(left, right, left_dim=1, right_dim=0):
+    return lax.dot_general(
+        left, right, (((left_dim,), (right_dim,)), ((), ())), preferred_element_type=F32
+    )
+
+
+def attend_head(rows):
+    inv_root = 1.0 / math.sqrt(HEAD_DIM)
+    q, k, v, g = (rows[:, n * HEAD_DIM : (n + 1) * HEAD_DIM] for n in range(4))
+    scores = dot(q, k, 1, 1) * inv_root
+    highest = jnp.max(scores, axis=1, keepdims=True)
+    raised = jnp.exp(scores - highest)
+    totals = jnp.sum(raised, axis=1, keepdims=True)
+    attended = (dot(raised.astype(BF16), v) / totals).astype(BF16)
+    weights = (raised * (1.0 / totals)).astype(BF16)
+    inner = jnp.sum(g.astype(F32) * attended.astype(F32), axis=1, keepdims=True)
+    grad_scores = dot(g, v, 1, 1)
+    grad_logits = (weights.astype(F32) * (grad_scores - inner) * inv_root).astype(BF16)
+    grad_q = dot(grad_logits, k).astype(BF16)
+    grad_k = dot(grad_logits, q, 0, 0).astype(BF16)
+    grad_v = dot(weights, g, 0, 0).astype(BF16)
+    return jnp.concatenate([attended, grad_q, grad_k, grad_v], axis=1)
+
+
+def side_by_side(ref):
+    tokens = ref.shape[0] // 4
+    return jnp.concatenate([ref[n * tokens : (n + 1) * tokens, :] for n in range(4)], axis=1)
+
+
+def picks_of(blocks, kept, before):
+    tokens = blocks[0].shape[0] // 4
+    lead = (lax.broadcasted_iota(jnp.int32, (TILE_ROWS, HEAD_DIM), 1) == 0).astype(BF16)
+    upto = (
+        lax.broadcasted_iota(jnp.int32, (tokens, tokens), 0)
+        <= lax.broadcasted_iota(jnp.int32, (tokens, tokens), 1)
+    ).astype(BF16)
+    slot = lax.broadcasted_iota(jnp.int32, (kept, tokens), 0).astype(F32)
+    picks = []
+    for block in blocks:
+        live = dot(lead, block[0:tokens, :], 1, 1) < 0.5 * DROPPED
+        rank = dot(live.astype(F32).astype(BF16), upto)[0:1]
+        place = jnp.where(live[0:1], rank + (before - 1.0), -1.0)
+        picks.append((slot == place).astype(F32).astype(BF16))
+        before = before + rank[:, tokens - 1 : tokens]
+    return jnp.concatenate(picks, axis=1), before
+
+
+def put_back(out, picked, result):
+    tokens = picked.shape[0]
+    rows = dot(picked, result).astype(BF16)
+    for n in range(4):
+        out[n * tokens : (n + 1) * tokens, :] = rows[:, n * HEAD_DIM : (n + 1) * HEAD_DIM]
+
+
+def head_lanes(head):
+    if isinstance(head, int):
+        return pl.ds(head * HEAD_DIM, HEAD_DIM)
+    return pl.ds(pl.multiple_of(head * HEAD_DIM, HEAD_DIM), HEAD_DIM)
+
+
+def pack_body(steps, q_ref, k_ref, v_ref, g_ref, mask_ref, *refs):
+    outs, (mask_here, sems) = refs[:-2], refs[-2:]
+    tokens = mask_ref.shape[1]
+    me = lax.axis_index("win")
+    copies = [pltpu.make_async_copy(mask_ref, mask_here, sems.at[0])]
+    for out, step in zip(outs, steps):
+        lanes = head_lanes(WINDOWS if step is None else me ^ step)
+        for n, ref in enumerate((q_ref, k_ref, v_ref, g_ref)):
+            copies.append(
+                pltpu.make_async_copy(
+                    ref.at[0, :, lanes],
+                    out.at[n * tokens : (n + 1) * tokens, :],
+                    sems.at[len(copies)],
+                )
+            )
+    for copy in copies:
+        copy.start()
+    copies[0].wait()
+    live = jnp.broadcast_to(mask_here[...].astype(F32), (TILE_ROWS, tokens)).astype(BF16)
+    share = jnp.full((TILE_ROWS, HEAD_DIM), 1.0 / TILE_ROWS, BF16)
+    keep = dot(live, share, 0, 0)
+    mark = (1.0 - keep) * DROPPED
+    for copy in copies[1:]:
+        copy.wait()
+    for out, step in zip(outs, steps):
+        if step is not None:
+            out[0:tokens, :] = (out[0:tokens, :].astype(F32) * keep + mark).astype(BF16)
+
+
+def turned(pick):
+    kept = pick.shape[0]
+    unit = (
+        lax.broadcasted_iota(jnp.int32, (kept, kept), 0)
+        == lax.broadcasted_iota(jnp.int32, (kept, kept), 1)
+    ).astype(F32).astype(BF16)
+    return dot(pick, unit, 0, 0).astype(BF16)
+
+
+def early_body(own, near, far, pick_out, turned_out, rows_out, used_out):
+    kept = pick_out.shape[0]
+    blocks = (own, near, far)
+    pick, used = picks_of(blocks, kept, jnp.zeros((1, 1), F32))
+    pick_out[...] = pick
+    used_out[...] = jnp.broadcast_to(used, used_out.shape)
+    rows_out[...] = dot(pick, jnp.concatenate([side_by_side(ref) for ref in blocks], axis=0)).astype(
+        BF16
+    )
+    turned_out[...] = turned(pick)
+
+
+def main_body(cross, turned_ref, rows_ref, used_ref, own_out, near_out, far_out, cross_out, last_out):
+    kept = rows_ref.shape[0]
+    tokens = cross.shape[0] // 4
+    last, _ = picks_of((cross,), kept, used_ref[0:1, 0:1])
+    last_out[...] = last
+    rows = rows_ref[...] + dot(last, side_by_side(cross)).astype(BF16)
+    result = attend_head(rows)
+    put_back(cross_out, turned(last), result)
+    for n, out in ((1, near_out), (2, far_out), (0, own_out)):
+        put_back(out, turned_ref[n * tokens : (n + 1) * tokens, :], result)
+
+
+def shared_early_body(pick_ref, own, near, far, rows_out):
+    blocks = (own, near, far)
+    rows_out[...] = dot(
+        pick_ref[...], jnp.concatenate([side_by_side(ref) for ref in blocks], axis=0)
+    ).astype(BF16)
+
+
+def placed(back, tokens, lanes, outs, sems):
+    return [
+        pltpu.make_async_copy(
+            back.at[n * tokens : (n + 1) * tokens, :], out.at[0, :, lanes], sems.at[n]
+        )
+        for n, out in enumerate(outs)
+    ]
+
+
+def last_body(steps, *refs):
+    backs = list(refs[: len(steps) + 1])
+    relayed = backs.pop(3)
+    relpick_ref, turned_ref, rows_ref = refs[len(steps) + 1 : -6]
+    outs, shared, sems = refs[-6:-2], refs[-2], refs[-1]
+    tokens = outs[0].shape[1]
+    me = lax.axis_index("win")
+    copies = []
+    for n, (back, step) in enumerate(zip(backs, steps)):
+        copies += placed(back, tokens, head_lanes(me ^ step), outs, sems.at[n])
+    for copy in copies:
+        copy.start()
+    rows = rows_ref[...] + dot(relpick_ref[...], side_by_side(relayed)).astype(BF16)
+    put_back(shared, turned_ref[0:tokens, :], attend_head(rows))
+    more = placed(shared, tokens, head_lanes(WINDOWS), outs, sems.at[len(steps)])
+    for copy in more:
+        copy.start()
+    for copy in copies + more:
+        copy.wait()
+
+
+def exchange(array, step):
+    return lax.ppermute(array, "win", [(n, n ^ step) for n in range(WINDOWS)])
+
+
+def after(array, other):
+    return lax.optimization_barrier((array, other))
+
+
+def shards_by_head(queries, key_vectors, value_vectors, out_grad, keep_mask):
+    tokens = queries.shape[1]
+    kept = WINDOWS * tokens // 2
+    in_hbm = pl.BlockSpec(memory_space=pltpu.HBM)
+    block = jax.ShapeDtypeStruct((4 * tokens, HEAD_DIM), BF16)
+    rows = jax.ShapeDtypeStruct((kept, 4 * HEAD_DIM), BF16)
+    turned_picks = jax.ShapeDtypeStruct((3 * tokens, kept), BF16)
+    whole = jax.ShapeDtypeStruct(queries.shape, BF16)
+
+    def picks(windows):
+        return jax.ShapeDtypeStruct((kept, windows * tokens), BF16)
+
+    def call(body, out_shape, *operands, flops=0, **specs):
+        return pl.pallas_call(
+            body,
+            out_shape=out_shape,
+            cost_estimate=pl.CostEstimate(flops=flops, bytes_accessed=0, transcendentals=0),
+            compiler_params=pltpu.CompilerParams(vmem_limit_bytes=VMEM_BYTES),
+            **specs,
+        )(*operands)
+
+    pinned = [
+        pltpu.with_memory_space_constraint(one, pltpu.HBM)
+        for one in (queries, key_vectors, value_vectors, out_grad, keep_mask)
+    ]
+
+    def pack(*steps):
+        return call(
+            functools.partial(pack_body, steps),
+            [block] * len(steps),
+            *pinned,
+            in_specs=[in_hbm] * 5,
+            scratch_shapes=[
+                pltpu.VMEM(keep_mask.shape, keep_mask.dtype),
+                pltpu.SemaphoreType.DMA((1 + 4 * len(steps),)),
+            ],
+        )
+
+    (far,) = pack(2)
+    cross, near, own, shared = pack(3, 1, 0, None)
+    got_far = exchange(far, 2)
+    got_cross = exchange(cross, 3)
+    got_near = exchange(near, 1)
+    late, got_far = after(shared, got_far)
+    shared_far = exchange(late, 2)
+    shared_near = exchange(late, 1)
+    pick, turned_pick, some_rows, used = call(
+        early_body,
+        [picks(3), turned_picks, rows, jax.ShapeDtypeStruct((8, HEAD_DIM), F32)],
+        own,
+        got_near,
+        got_far,
+        flops=1 << 28,
+    )
+    own_result, near_result, far_result, cross_result, last = call(
+        main_body, [block] * 4 + [picks(1)], got_cross, turned_pick, some_rows, used, flops=1 << 29
+    )
+    back_far = exchange(far_result, 2)
+    back_cross = exchange(cross_result, 3)
+    back_near = exchange(near_result, 1)
+    shared_far, shared_near = after(shared_far, shared_near)
+    relayed = exchange(shared_far, 1)
+    shared_rows = call(shared_early_body, rows, pick, shared, shared_near, shared_far)
+    steps = (0, 2, 3, 1)
+    return call(
+        functools.partial(last_body, steps),
+        [whole] * 4,
+        own_result,
+        back_far,
+        back_cross,
+        relayed,
+        back_near,
+        last,
+        turned_pick,
+        shared_rows,
+        out_specs=[in_hbm] * 4,
+        scratch_shapes=[
+            pltpu.VMEM(block.shape, BF16),
+            pltpu.SemaphoreType.DMA((len(steps) + 1, 4)),
+        ],
+    )
 
 
 def fold_blocks(step_fn, carried, arrays):
@@ -226,6 +485,13 @@
     return (place(back_attended), place(back_query), grad_key_out, grad_value_out)
 
 
+def by_plan(queries, key_vectors, value_vectors, out_grad, keep_mask):
+    tokens, feat_dev = queries.shape[1:]
+    dealt = lax.axis_size("win") == WINDOWS and feat_dev == (WINDOWS + 1) * HEAD_DIM
+    run = shards_by_head if dealt and tokens == HEAD_DIM else shards
+    return run(queries, key_vectors, value_vectors, out_grad, keep_mask)
+
+
 def solution(mesh):
     placed = (
         P(("groups", "samp"), "win", "head"),
@@ -235,7 +501,7 @@
         P(("groups", "samp"), "win"),
     )
     return jax.shard_map(
-        shards,
+        by_plan,
         mesh=mesh,
         in_specs=placed,
         out_specs=(

time: 191 us -> 37.9 us (0.20)
  blocking collectives: 115 us -> 0 us
  local copies, waits for them, and re-layouts: 20.8 us -> 0 us
  other arithmetic: 16.8 us -> 0 us
  starting transfers between devices: 22.8 us -> 14 us
  Pallas kernels: 0 us -> 6.63 us
  waiting for transfers between devices: 10.8 us -> 16.4 us
    all_gather x6 -> x0, blocking collectives: 85.2 us -> none  [the longest x1 15.7 us: shards(): lax.all_gather(query_rows, 'win', axis=0, tiled=True)]
    all_to_all x6 -> x0, starting transfers between devices: 22.8 us -> none  [the longest x1 4.92 us: shards(): lax.all_to_all(pack(queries), 'win', split_axis=0, concat_axis=0, tiled=T...]
    all_to_all x2 -> x0, blocking collectives: 19.5 us -> none  [the longest x1 10.5 us: shards(): lax.all_to_all(repack(grad_value), 'win', split_axis=0, concat_axis=0, ti...]
    ppermute x0 -> x9, waiting for transfers between devices: none -> 16.4 us  [exchange(): return lax.ppermute(array, 'win', [(n, n ^ step) for n in range(WINDOWS)])]
    gather x22 -> x0, local copies, waits for them, and re-layouts: 16.3 us -> none  [the longest x4 3.54 us: place(): matrix[land_rows]]
    ppermute x0 -> x9, starting transfers between devices: none -> 14 us  [exchange(): return lax.ppermute(array, 'win', [(n, n ^ step) for n in range(WINDOWS)])]
    all_to_all x6 -> x0, waiting for transfers between devices: 10.8 us -> none  [the longest x1 4.8 us: shards(): lax.all_to_all(repack(grad_key), 'win', split_axis=0, concat_axis=0, tile...]
    unnamed x1 -> x0, blocking collectives: 9.89 us -> none
  transfers between devices with their start and end apart: 6 -> 9, of which waited for: 4 -> 5; matrix products, arithmetic and copies ran while one was open for 8% -> 0% of each run, Pallas kernels for 0% -> 10%
where the time goes in v3:
time: 37.9 us; the launch traced here: 37.6 us
  waiting for transfers between devices  16.4 us (43%)
  starting transfers between devices  14 us (37%)
  Pallas kernels  6.63 us (17%)
  between operations  0.68 us (2%)
    ppermute x9, waiting for transfers between devices, exchange(): return lax.ppermute(array, 'win', [(n, n ^ step) for n in range(WINDOWS)])  16.4 us
    ppermute x9, starting transfers between devices, exchange(): return lax.ppermute(array, 'win', [(n, n ^ step) for n in range(WINDOWS)])  14 us
    pallas_call x6, Pallas kernels, call(): pl.pallas_call(body, out_shape=out_shape, cost_estimate=pl.CostEstimate(f...  6.63 us
  transfers between devices with their start and end apart: 9, of which 5 were waited for; matrix products, arithmetic and copies ran while one was open for 0% of the time, Pallas kernels for 10%

profile of v3, /device:TPU:0, one launch (start us, length us, event | category | flops | bytes accessed | tf_op | source)
XLA Modules:
  0.0 37.6 jit_solution(8582004556637858215)
XLA Ops:
  0.6 0.9 %shard_map.85 = bf16[512,128]{1,0:T(8,128)(2,1)S(1)} custom-call(bf16[1,128,640]{2,1,0:T(8,128)(2,1)} %q_ref.3, bf16[1,128,640]{2,1,0:T(8,128)(2,1)} %k_ref.3, bf16[1,128,640]{2,1,0:T(8,128)(2,1)} %v_ref.3, bf16[1,128,640]{2,1,0:T(8,128)(2,1)} %g_ref.3, s32[1,128]{1,0:T(1,128)} %mask_ref.3), custom_call_target="tpu_custom_call" | custom-call | tf_op jit(solution)/shard_map/pallas_call | solution.py:200
  1.5 4.1 %collective-permute-start.2 = (bf16[512,128]{1,0:T(8,128)(2,1)S(1)}, bf16[512,128]{1,0:T(8,128)(2,1)S(1)}, u32[]{:S(2)}, u32[]{:S(2)}) collective-permute-start(bf16[512,128]{1,0:T(8,128)(2,1)S(1)} %shard_map.85), channel_id=1, source_target_pairs={{0,8},{4,12},{8,0},{12,4},{1,9},{5,13},{9,1},{13,5},{2,10},{6,14},... | collective-permute-start | bytes 393224 | tf_op jit(solution)/shard_map/ppermute | solution.py:180
  5.6 1.2 %shard_map.84 = (bf16[512,128]{1,0:T(8,128)(2,1)S(1)}, bf16[512,128]{1,0:T(8,128)(2,1)S(1)}, bf16[512,128]{1,0:T(8,128)(2,1)S(1)}, bf16[512,128]{1,0:T(8,128)(2,1)S(1)}) custom-call(bf16[1,128,640]{2,1,0:T(8,128)(2,1)} %q_ref.3, bf16[1,128,640]{2,1,0:T(8,128)(2,1)} %k_ref.3, bf16[1,128,640]{2,1,0:T(8,128)(2,1)} %v_ref.3, bf16[1,128,640]{2,1,0:T(8,128)(2,1)} %g_ref.3, ...), custom_call_target="tpu_custom_call" | custom-call | tf_op jit(solution)/shard_map/pallas_call | solution.py:200
  6.8 1.6 %collective-permute-start.1 = (bf16[512,128]{1,0:T(8,128)(2,1)S(1)}, bf16[512,128]{1,0:T(8,128)(2,1)S(1)}, u32[]{:S(2)}, u32[]{:S(2)}) collective-permute-start(bf16[512,128]{1,0:T(8,128)(2,1)S(1)} %get-tuple-element.23), channel_id=1, source_target_pairs={{0,4},{4,0},{8,12},{12,8},{1,5},{5,1},{9,13},{13,9},{2,6},{6,2},{1... | collective-permute-start | bytes 393224 | tf_op jit(solution)/shard_map/ppermute | solution.py:180
  8.5 0.0 collective-permute-start
  8.5 4.8 %collective-permute-done.2.far = bf16[512,128]{1,0:T(8,128)(2,1)S(1)} collective-permute-done((bf16[512,128]{1,0:T(8,128)(2,1)S(1)}, bf16[512,128]{1,0:T(8,128)(2,1)S(1)}, u32[]{:S(2)}, u32[]{:S(2)}) %collective-permute-start.2) | collective-permute-done | bytes 131104 | tf_op jit(solution)/shard_map/ppermute | solution.py:180
  13.3 0.4 %collective-permute-start.6 = (bf16[512,128]{1,0:T(8,128)(2,1)S(1)}, bf16[512,128]{1,0:T(8,128)(2,1)S(1)}, u32[]{:S(2)}, u32[]{:S(2)}) collective-permute-start(bf16[512,128]{1,0:T(8,128)(2,1)S(1)} %get-tuple-element.32.own), channel_id=1, source_target_pairs={{0,4},{4,0},{8,12},{12,8},{1,5},{5,1},{9,13},{13,9},{2,6},{6,2},{1... | collective-permute-start | bytes 393224 | tf_op jit(solution)/shard_map/ppermute | solution.py:180
  13.8 3.6 %collective-permute-start.5 = (bf16[512,128]{1,0:T(8,128)(2,1)S(1)}, bf16[512,128]{1,0:T(8,128)(2,1)S(1)}, u32[]{:S(2)}, u32[]{:S(2)}) collective-permute-start(bf16[512,128]{1,0:T(8,128)(2,1)S(1)} %get-tuple-element.32.own), channel_id=1, source_target_pairs={{0,8},{4,12},{8,0},{12,4},{1,9},{5,13},{9,1},{13,5},{2,10},{6,14},... | collective-permute-start | bytes 393224 | tf_op jit(solution)/shard_map/ppermute | solution.py:180
  17.4 0.0 collective-permute-done.1.near
  17.4 0.9 %shard_map.86 = (bf16[256,384]{1,0:T(8,128)(2,1)S(1)}, bf16[384,256]{1,0:T(8,128)(2,1)S(1)}, bf16[256,512]{1,0:T(8,128)(2,1)S(1)}, f32[8,128]{1,0:T(8,128)S(1)}) custom-call(bf16[512,128]{1,0:T(8,128)(2,1)S(1)} %get-tuple-element.22.own, bf16[512,128]{1,0:T(8,128)(2,1)S(1)} %collective-permute-done.1.near, bf16[512,128]{1,0:T(8,128)(2,1)S(1)} %collective-permute-done.2.far), custom_call_target="tpu_custom_call" | custom-call | flops 268435456 | tf_op jit(solution)/shard_map/pallas_call | solution.py:200
  18.3 0.0 collective-permute-done.cross
  18.3 1.4 %shard_map.87 = (bf16[512,128]{1,0:T(8,128)(2,1)S(1)}, bf16[512,128]{1,0:T(8,128)(2,1)S(1)}, bf16[512,128]{1,0:T(8,128)(2,1)S(1)}, bf16[512,128]{1,0:T(8,128)(2,1)S(1)}, bf16[256,128]{1,0:T(8,128)(2,1)S(1)}) custom-call(bf16[512,128]{1,0:T(8,128)(2,1)S(1)} %collective-permute-done.cross, bf16[384,256]{1,0:T(8,128)(2,1)S(1)} %get-tuple-element.26.turned_ref.refs_6_, ...), custom_call_target="tpu_custom_call" | custom-call | flops 536870912 | tf_op jit(solution)/shard_map/pallas_call | solution.py:200
  19.7 2.1 %collective-permute-start.3 = (bf16[512,128]{1,0:T(8,128)(2,1)S(1)}, bf16[512,128]{1,0:T(8,128)(2,1)S(1)}, u32[]{:S(2)}, u32[]{:S(2)}) collective-permute-start(bf16[512,128]{1,0:T(8,128)(2,1)S(1)} %get-tuple-element.30), channel_id=1, source_target_pairs={{0,8},{4,12},{8,0},{12,4},{1,9},{5,13},{9,1},{13,5},{2,10},{6,14},... | collective-permute-start | bytes 393224 | tf_op jit(solution)/shard_map/ppermute | solution.py:180
  21.9 0.4 %collective-permute-start.4 = (bf16[512,128]{1,0:T(8,128)(2,1)S(1)}, bf16[512,128]{1,0:T(8,128)(2,1)S(1)}, u32[]{:S(2)}, u32[]{:S(2)}) collective-permute-start(bf16[512,128]{1,0:T(8,128)(2,1)S(1)} %get-tuple-element.31), channel_id=1, source_target_pairs={{0,12},{4,8},{8,4},{12,0},{1,13},{5,9},{9,5},{13,1},{2,14},{6,10},... | collective-permute-start | bytes 393224 | tf_op jit(solution)/shard_map/ppermute | solution.py:180
  22.3 1.0 %collective-permute-start.8 = (bf16[512,128]{1,0:T(8,128)(2,1)S(1)}, bf16[512,128]{1,0:T(8,128)(2,1)S(1)}, u32[]{:S(2)}, u32[]{:S(2)}) collective-permute-start(bf16[512,128]{1,0:T(8,128)(2,1)S(1)} %get-tuple-element.34), channel_id=1, source_target_pairs={{0,4},{4,0},{8,12},{12,8},{1,5},{5,1},{9,13},{13,9},{2,6},{6,2},{1... | collective-permute-start | bytes 393224 | tf_op jit(solution)/shard_map/ppermute | solution.py:180
  23.3 0.0 collective-permute-done.6.near
  23.3 5.2 %collective-permute-done.5.far = bf16[512,128]{1,0:T(8,128)(2,1)S(1)} collective-permute-done((bf16[512,128]{1,0:T(8,128)(2,1)S(1)}, bf16[512,128]{1,0:T(8,128)(2,1)S(1)}, u32[]{:S(2)}, u32[]{:S(2)}) %collective-permute-start.5) | collective-permute-done | bytes 131104 | tf_op jit(solution)/shard_map/ppermute | solution.py:180
  28.5 0.6 %collective-permute-start.7 = (bf16[512,128]{1,0:T(8,128)(2,1)S(1)}, bf16[512,128]{1,0:T(8,128)(2,1)S(1)}, u32[]{:S(2)}, u32[]{:S(2)}) collective-permute-start(bf16[512,128]{1,0:T(8,128)(2,1)S(1)} %collective-permute-done.5.far), channel_id=1, source_target_pairs={{0,4},{4,0},{8,12},{12,8},{1,5},{5,1},{9,13},{13,9},{2,6},{6,2},{1... | collective-permute-start | bytes 393224 | tf_op jit(solution)/shard_map/ppermute | solution.py:180
  29.1 0.3 shard_map.88.refs_7_
  29.4 2.7 %collective-permute-done.3.refs_1_ = bf16[512,128]{1,0:T(8,128)(2,1)S(1)} collective-permute-done((bf16[512,128]{1,0:T(8,128)(2,1)S(1)}, bf16[512,128]{1,0:T(8,128)(2,1)S(1)}, u32[]{:S(2)}, u32[]{:S(2)}) %collective-permute-start.3) | collective-permute-done | bytes 131104 | tf_op jit(solution)/shard_map/ppermute | solution.py:180
  32.1 0.0 collective-permute-done.4.refs_2_
  32.1 2.3 %collective-permute-done.8.refs_4_ = bf16[512,128]{1,0:T(8,128)(2,1)S(1)} collective-permute-done((bf16[512,128]{1,0:T(8,128)(2,1)S(1)}, bf16[512,128]{1,0:T(8,128)(2,1)S(1)}, u32[]{:S(2)}, u32[]{:S(2)}) %collective-permute-start.8) | collective-permute-done | bytes 131104 | tf_op jit(solution)/shard_map/ppermute | solution.py:180
  34.3 1.4 %collective-permute-done.7.refs_3_ = bf16[512,128]{1,0:T(8,128)(2,1)S(1)} collective-permute-done((bf16[512,128]{1,0:T(8,128)(2,1)S(1)}, bf16[512,128]{1,0:T(8,128)(2,1)S(1)}, u32[]{:S(2)}, u32[]{:S(2)}) %collective-permute-start.7) | collective-permute-done | bytes 131104 | tf_op jit(solution)/shard_map/ppermute | solution.py:180
  35.7 1.9 %shard_map.89 = (bf16[1,128,640]{2,1,0:T(8,128)(2,1)}, bf16[1,128,640]{2,1,0:T(8,128)(2,1)}, bf16[1,128,640]{2,1,0:T(8,128)(2,1)}, bf16[1,128,640]{2,1,0:T(8,128)(2,1)}) custom-call(bf16[512,128]{1,0:T(8,128)(2,1)S(1)} %get-tuple-element.29.refs_0_, bf16[512,128]{1,0:T(8,128)(2,1)S(1)} %collective-permute-done.3.refs_1_, ...), custom_call_target="tpu_custom_call" | custom-call | tf_op jit(solution)/shard_map/pallas_call | solution.py:200
Async XLA Ops:
  1.5 11.8 %collective-permute-start.2 = (bf16[512,128]{1,0:T(8,128)(2,1)S(1)}, bf16[512,128]{1,0:T(8,128)(2,1)S(1)}, u32[]{:S(2)}, u32[]{:S(2)}) collective-permute-start(bf16[512,128]{1,0:T(8,128)(2,1)S(1)} %shard_map.85), channel_id=1, source_target_pairs={{0,8},{4,12},{8,0},{12,4},{1,9},{5,13},{9,1},{13,5},{2,10},{6,14},... | collective-permute-start | bytes 393224 | tf_op jit(solution)/shard_map/ppermute | solution.py:180
  6.8 10.5 %collective-permute-start.1 = (bf16[512,128]{1,0:T(8,128)(2,1)S(1)}, bf16[512,128]{1,0:T(8,128)(2,1)S(1)}, u32[]{:S(2)}, u32[]{:S(2)}) collective-permute-start(bf16[512,128]{1,0:T(8,128)(2,1)S(1)} %get-tuple-element.23), channel_id=1, source_target_pairs={{0,4},{4,0},{8,12},{12,8},{1,5},{5,1},{9,13},{13,9},{2,6},{6,2},{1... | collective-permute-start | bytes 393224 | tf_op jit(solution)/shard_map/ppermute | solution.py:180
  8.5 9.8 %collective-permute-start = (bf16[512,128]{1,0:T(8,128)(2,1)S(1)}, bf16[512,128]{1,0:T(8,128)(2,1)S(1)}, u32[]{:S(2)}, u32[]{:S(2)}) collective-permute-start(bf16[512,128]{1,0:T(8,128)(2,1)S(1)} %get-tuple-element.21), channel_id=1, source_target_pairs={{0,12},{4,8},{8,4},{12,0},{1,13},{5,9},{9,5},{13,1},{2,14},{6,10},... | collective-permute-start | bytes 393224 | tf_op jit(solution)/shard_map/ppermute | solution.py:180
  13.3 10.0 %collective-permute-start.6 = (bf16[512,128]{1,0:T(8,128)(2,1)S(1)}, bf16[512,128]{1,0:T(8,128)(2,1)S(1)}, u32[]{:S(2)}, u32[]{:S(2)}) collective-permute-start(bf16[512,128]{1,0:T(8,128)(2,1)S(1)} %get-tuple-element.32.own), channel_id=1, source_target_pairs={{0,4},{4,0},{8,12},{12,8},{1,5},{5,1},{9,13},{13,9},{2,6},{6,2},{1... | collective-permute-start | bytes 393224 | tf_op jit(solution)/shard_map/ppermute | solution.py:180
  13.8 14.7 %collective-permute-start.5 = (bf16[512,128]{1,0:T(8,128)(2,1)S(1)}, bf16[512,128]{1,0:T(8,128)(2,1)S(1)}, u32[]{:S(2)}, u32[]{:S(2)}) collective-permute-start(bf16[512,128]{1,0:T(8,128)(2,1)S(1)} %get-tuple-element.32.own), channel_id=1, source_target_pairs={{0,8},{4,12},{8,0},{12,4},{1,9},{5,13},{9,1},{13,5},{2,10},{6,14},... | collective-permute-start | bytes 393224 | tf_op jit(solution)/shard_map/ppermute | solution.py:180
  19.7 12.3 %collective-permute-start.3 = (bf16[512,128]{1,0:T(8,128)(2,1)S(1)}, bf16[512,128]{1,0:T(8,128)(2,1)S(1)}, u32[]{:S(2)}, u32[]{:S(2)}) collective-permute-start(bf16[512,128]{1,0:T(8,128)(2,1)S(1)} %get-tuple-element.30), channel_id=1, source_target_pairs={{0,8},{4,12},{8,0},{12,4},{1,9},{5,13},{9,1},{13,5},{2,10},{6,14},... | collective-permute-start | bytes 393224 | tf_op jit(solution)/shard_map/ppermute | solution.py:180
  21.9 10.2 %collective-permute-start.4 = (bf16[512,128]{1,0:T(8,128)(2,1)S(1)}, bf16[512,128]{1,0:T(8,128)(2,1)S(1)}, u32[]{:S(2)}, u32[]{:S(2)}) collective-permute-start(bf16[512,128]{1,0:T(8,128)(2,1)S(1)} %get-tuple-element.31), channel_id=1, source_target_pairs={{0,12},{4,8},{8,4},{12,0},{1,13},{5,9},{9,5},{13,1},{2,14},{6,10},... | collective-permute-start | bytes 393224 | tf_op jit(solution)/shard_map/ppermute | solution.py:180
  22.3 12.0 %collective-permute-start.8 = (bf16[512,128]{1,0:T(8,128)(2,1)S(1)}, bf16[512,128]{1,0:T(8,128)(2,1)S(1)}, u32[]{:S(2)}, u32[]{:S(2)}) collective-permute-start(bf16[512,128]{1,0:T(8,128)(2,1)S(1)} %get-tuple-element.34), channel_id=1, source_target_pairs={{0,4},{4,0},{8,12},{12,8},{1,5},{5,1},{9,13},{13,9},{2,6},{6,2},{1... | collective-permute-start | bytes 393224 | tf_op jit(solution)/shard_map/ppermute | solution.py:180
  28.5 7.2 %collective-permute-start.7 = (bf16[512,128]{1,0:T(8,128)(2,1)S(1)}, bf16[512,128]{1,0:T(8,128)(2,1)S(1)}, u32[]{:S(2)}, u32[]{:S(2)}) collective-permute-start(bf16[512,128]{1,0:T(8,128)(2,1)S(1)} %collective-permute-done.5.far), channel_id=1, source_target_pairs={{0,4},{4,0},{8,12},{12,8},{1,5},{5,1},{9,13},{13,9},{2,6},{6,2},{1... | collective-permute-start | bytes 393224 | tf_op jit(solution)/shard_map/ppermute | solution.py:180

commit v4 on v3

--- a/solution.py
+++ b/solution.py
@@ -23,21 +23,22 @@
     )
 
 
-def attend_head(rows):
+def attend_head(rows, needed=None):
     inv_root = 1.0 / math.sqrt(HEAD_DIM)
+    needed = rows.shape[0] if needed is None else needed
     q, k, v, g = (rows[:, n * HEAD_DIM : (n + 1) * HEAD_DIM] for n in range(4))
     scores = dot(q, k, 1, 1) * inv_root
-    highest = jnp.max(scores, axis=1, keepdims=True)
-    raised = jnp.exp(scores - highest)
-    totals = jnp.sum(raised, axis=1, keepdims=True)
-    attended = (dot(raised.astype(BF16), v) / totals).astype(BF16)
-    weights = (raised * (1.0 / totals)).astype(BF16)
-    inner = jnp.sum(g.astype(F32) * attended.astype(F32), axis=1, keepdims=True)
     grad_scores = dot(g, v, 1, 1)
-    grad_logits = (weights.astype(F32) * (grad_scores - inner) * inv_root).astype(BF16)
-    grad_q = dot(grad_logits, k).astype(BF16)
-    grad_k = dot(grad_logits, q, 0, 0).astype(BF16)
-    grad_v = dot(weights, g, 0, 0).astype(BF16)
+    raised = jnp.exp(scores - jnp.max(scores, axis=1, keepdims=True))
+    share = 1.0 / jnp.sum(raised, axis=1, keepdims=True)
+    inner = jnp.sum(raised * grad_scores, axis=1, keepdims=True) * share
+    weights = raised * share
+    grad_logits = (weights * ((grad_scores - inner) * inv_root)).astype(BF16)
+    weights = weights.astype(BF16)
+    attended = (dot(raised[:needed].astype(BF16), v) * share[:needed]).astype(BF16)
+    grad_q = dot(grad_logits[:needed], k).astype(BF16)
+    grad_k = dot(grad_logits[:, :needed], q, 0, 0).astype(BF16)
+    grad_v = dot(weights[:, :needed], g, 0, 0).astype(BF16)
     return jnp.concatenate([attended, grad_q, grad_k, grad_v], axis=1)
 
 
@@ -115,9 +116,9 @@
     return dot(pick, unit, 0, 0).astype(BF16)
 
 
-def early_body(own, near, far, pick_out, turned_out, rows_out, used_out):
+def early_body(own, near, cross, pick_out, turned_out, rows_out, used_out):
     kept = pick_out.shape[0]
-    blocks = (own, near, far)
+    blocks = (own, near, cross)
     pick, used = picks_of(blocks, kept, jnp.zeros((1, 1), F32))
     pick_out[...] = pick
     used_out[...] = jnp.broadcast_to(used, used_out.shape)
@@ -127,23 +128,25 @@
     turned_out[...] = turned(pick)
 
 
-def main_body(cross, turned_ref, rows_ref, used_ref, own_out, near_out, far_out, cross_out, last_out):
+def main_body(far, turned_ref, rows_ref, used_ref, own_out, near_out, far_out, cross_out, last_out):
     kept = rows_ref.shape[0]
-    tokens = cross.shape[0] // 4
-    last, _ = picks_of((cross,), kept, used_ref[0:1, 0:1])
+    tokens = far.shape[0] // 4
+    last, _ = picks_of((far,), kept, used_ref[0:1, 0:1])
     last_out[...] = last
-    rows = rows_ref[...] + dot(last, side_by_side(cross)).astype(BF16)
+    rows = rows_ref[...] + dot(last, side_by_side(far)).astype(BF16)
     result = attend_head(rows)
-    put_back(cross_out, turned(last), result)
-    for n, out in ((1, near_out), (2, far_out), (0, own_out)):
+    put_back(far_out, turned(last), result)
+    for n, out in ((1, near_out), (2, cross_out), (0, own_out)):
         put_back(out, turned_ref[n * tokens : (n + 1) * tokens, :], result)
 
 
-def shared_early_body(pick_ref, own, near, far, rows_out):
+def shared_early_body(pick_ref, last_ref, own, near, far, rows_out):
+    tokens = last_ref.shape[1]
+    pick = jnp.concatenate([pick_ref[:, 0 : 2 * tokens], last_ref[...]], axis=1)
     blocks = (own, near, far)
-    rows_out[...] = dot(
-        pick_ref[...], jnp.concatenate([side_by_side(ref) for ref in blocks], axis=0)
-    ).astype(BF16)
+    rows_out[...] = dot(pick, jnp.concatenate([side_by_side(ref) for ref in blocks], axis=0)).astype(
+        BF16
+    )
 
 
 def placed(back, tokens, lanes, outs, sems):
@@ -167,8 +170,8 @@
         copies += placed(back, tokens, head_lanes(me ^ step), outs, sems.at[n])
     for copy in copies:
         copy.start()
-    rows = rows_ref[...] + dot(relpick_ref[...], side_by_side(relayed)).astype(BF16)
-    put_back(shared, turned_ref[0:tokens, :], attend_head(rows))
+    rows = rows_ref[...] + dot(relpick_ref[:, 2 * tokens : 3 * tokens], side_by_side(relayed)).astype(BF16)
+    put_back(shared, turned_ref[0:tokens, 0:tokens], attend_head(rows, tokens))
     more = placed(shared, tokens, head_lanes(WINDOWS), outs, sems.at[len(steps)])
     for copy in more:
         copy.start()
@@ -222,12 +225,12 @@
             ],
         )
 
-    (far,) = pack(2)
-    cross, near, own, shared = pack(3, 1, 0, None)
+    (cross,) = pack(3)
+    far, near, own, shared = pack(2, 1, 0, None)
+    got_cross = exchange(cross, 3)
     got_far = exchange(far, 2)
-    got_cross = exchange(cross, 3)
     got_near = exchange(near, 1)
-    late, got_far = after(shared, got_far)
+    late, got_cross = after(shared, got_cross)
     shared_far = exchange(late, 2)
     shared_near = exchange(late, 1)
     pick, turned_pick, some_rows, used = call(
@@ -235,28 +238,28 @@
         [picks(3), turned_picks, rows, jax.ShapeDtypeStruct((8, HEAD_DIM), F32)],
         own,
         got_near,
-        got_far,
+        got_cross,
         flops=1 << 28,
     )
     own_result, near_result, far_result, cross_result, last = call(
-        main_body, [block] * 4 + [picks(1)], got_cross, turned_pick, some_rows, used, flops=1 << 29
-    )
+        main_body, [block] * 4 + [picks(1)], got_far, turned_pick, some_rows, used, flops=1 << 29
+    )
+    back_cross = exchange(cross_result, 3)
     back_far = exchange(far_result, 2)
-    back_cross = exchange(cross_result, 3)
     back_near = exchange(near_result, 1)
     shared_far, shared_near = after(shared_far, shared_near)
     relayed = exchange(shared_far, 1)
-    shared_rows = call(shared_early_body, rows, pick, shared, shared_near, shared_far)
-    steps = (0, 2, 3, 1)
+    shared_rows = call(shared_early_body, rows, pick, last, shared, shared_near, shared_far)
+    steps = (0, 3, 2, 1)
     return call(
         functools.partial(last_body, steps),
         [whole] * 4,
         own_result,
+        back_cross,
         back_far,
-        back_cross,
         relayed,
         back_near,
-        last,
+        pick,
         turned_pick,
         shared_rows,
         out_specs=[in_hbm] * 4,

time: 37.9 us -> 37.3 us (0.984)
  waiting for transfers between devices: 16.4 us -> 15.2 us
  starting transfers between devices: 14 us -> 14.6 us
    ppermute x9, waiting for transfers between devices: 16.4 us -> 15.2 us  [exchange(): return lax.ppermute(array, 'win', [(n, n ^ step) for n in range(WINDOWS)])]
    ppermute x9, starting transfers between devices: 14 us -> 14.6 us  [exchange(): return lax.ppermute(array, 'win', [(n, n ^ step) for n in range(WINDOWS)])]
where the time goes in v4:
time: 37.3 us; the launch traced here: 37 us
  waiting for transfers between devices  15.2 us (41%)
  starting transfers between devices  14.6 us (39%)
  Pallas kernels  6.4 us (17%)
  between operations  0.7 us (2%)
    ppermute x9, waiting for transfers between devices, exchange(): return lax.ppermute(array, 'win', [(n, n ^ step) for n in range(WINDOWS)])  15.2 us
    ppermute x9, starting transfers between devices, exchange(): return lax.ppermute(array, 'win', [(n, n ^ step) for n in range(WINDOWS)])  14.6 us
    pallas_call x6, Pallas kernels, call(): pl.pallas_call(body, out_shape=out_shape, cost_estimate=pl.CostEstimate(f...  6.4 us
  transfers between devices with their start and end apart: 9, of which 5 were waited for; matrix products, arithmetic and copies ran while one was open for 0% of the time, Pallas kernels for 10%

profile of v4, /device:TPU:0, one launch (start us, length us, event | category | flops | bytes accessed | tf_op | source)
XLA Modules:
  0.0 37.0 jit_solution(2699472981629220567)
XLA Ops:
  0.6 0.9 %shard_map.85 = bf16[512,128]{1,0:T(8,128)(2,1)S(1)} custom-call(bf16[1,128,640]{2,1,0:T(8,128)(2,1)} %q_ref.3, bf16[1,128,640]{2,1,0:T(8,128)(2,1)} %k_ref.3, bf16[1,128,640]{2,1,0:T(8,128)(2,1)} %v_ref.3, bf16[1,128,640]{2,1,0:T(8,128)(2,1)} %g_ref.3, s32[1,128]{1,0:T(1,128)} %mask_ref.3), custom_call_target="tpu_custom_call" | custom-call | tf_op jit(solution)/shard_map/pallas_call | solution.py:203
  1.5 5.1 %collective-permute-start.2 = (bf16[512,128]{1,0:T(8,128)(2,1)S(1)}, bf16[512,128]{1,0:T(8,128)(2,1)S(1)}, u32[]{:S(2)}, u32[]{:S(2)}) collective-permute-start(bf16[512,128]{1,0:T(8,128)(2,1)S(1)} %shard_map.85), channel_id=1, source_target_pairs={{0,12},{4,8},{8,4},{12,0},{1,13},{5,9},{9,5},{13,1},{2,14},{6,10},... | collective-permute-start | bytes 393224 | tf_op jit(solution)/shard_map/ppermute | solution.py:183
  6.7 1.2 %shard_map.84 = (bf16[512,128]{1,0:T(8,128)(2,1)S(1)}, bf16[512,128]{1,0:T(8,128)(2,1)S(1)}, bf16[512,128]{1,0:T(8,128)(2,1)S(1)}, bf16[512,128]{1,0:T(8,128)(2,1)S(1)}) custom-call(bf16[1,128,640]{2,1,0:T(8,128)(2,1)} %q_ref.3, bf16[1,128,640]{2,1,0:T(8,128)(2,1)} %k_ref.3, bf16[1,128,640]{2,1,0:T(8,128)(2,1)} %v_ref.3, bf16[1,128,640]{2,1,0:T(8,128)(2,1)} %g_ref.3, ...), custom_call_target="tpu_custom_call" | custom-call | tf_op jit(solution)/shard_map/pallas_call | solution.py:203
  7.9 0.1 collective-permute-start.1
  7.9 0.6 %collective-permute-start = (bf16[512,128]{1,0:T(8,128)(2,1)S(1)}, bf16[512,128]{1,0:T(8,128)(2,1)S(1)}, u32[]{:S(2)}, u32[]{:S(2)}) collective-permute-start(bf16[512,128]{1,0:T(8,128)(2,1)S(1)} %get-tuple-element.21), channel_id=1, source_target_pairs={{0,8},{4,12},{8,0},{12,4},{1,9},{5,13},{9,1},{13,5},{2,10},{6,14},... | collective-permute-start | bytes 393224 | tf_op jit(solution)/shard_map/ppermute | solution.py:183
  8.5 2.5 %collective-permute-done.2.cross = bf16[512,128]{1,0:T(8,128)(2,1)S(1)} collective-permute-done((bf16[512,128]{1,0:T(8,128)(2,1)S(1)}, bf16[512,128]{1,0:T(8,128)(2,1)S(1)}, u32[]{:S(2)}, u32[]{:S(2)}) %collective-permute-start.2) | collective-permute-done | bytes 131104 | tf_op jit(solution)/shard_map/ppermute | solution.py:183
  11.0 3.4 %collective-permute-start.6 = (bf16[512,128]{1,0:T(8,128)(2,1)S(1)}, bf16[512,128]{1,0:T(8,128)(2,1)S(1)}, u32[]{:S(2)}, u32[]{:S(2)}) collective-permute-start(bf16[512,128]{1,0:T(8,128)(2,1)S(1)} %get-tuple-element.32.own), channel_id=1, source_target_pairs={{0,4},{4,0},{8,12},{12,8},{1,5},{5,1},{9,13},{13,9},{2,6},{6,2},{1... | collective-permute-start | bytes 393224 | tf_op jit(solution)/shard_map/ppermute | solution.py:183
  14.5 0.9 %collective-permute-start.5 = (bf16[512,128]{1,0:T(8,128)(2,1)S(1)}, bf16[512,128]{1,0:T(8,128)(2,1)S(1)}, u32[]{:S(2)}, u32[]{:S(2)}) collective-permute-start(bf16[512,128]{1,0:T(8,128)(2,1)S(1)} %get-tuple-element.32.own), channel_id=1, source_target_pairs={{0,8},{4,12},{8,0},{12,4},{1,9},{5,13},{9,1},{13,5},{2,10},{6,14},... | collective-permute-start | bytes 393224 | tf_op jit(solution)/shard_map/ppermute | solution.py:183
  15.4 0.0 collective-permute-done.1.near
  15.4 0.9 %shard_map.86 = (bf16[256,384]{1,0:T(8,128)(2,1)S(1)}, bf16[384,256]{1,0:T(8,128)(2,1)S(1)}, bf16[256,512]{1,0:T(8,128)(2,1)S(1)}, f32[8,128]{1,0:T(8,128)S(1)}) custom-call(bf16[512,128]{1,0:T(8,128)(2,1)S(1)} %get-tuple-element.22.own, bf16[512,128]{1,0:T(8,128)(2,1)S(1)} %collective-permute-done.1.near, bf16[512,128]{1,0:T(8,128)(2,1)S(1)} %collective-permute-done.2.cross), custom_call_target="tpu_custom_call" | custom-call | flops 268435456 | tf_op jit(solution)/shard_map/pallas_call | solution.py:203
  16.3 5.2 %collective-permute-done.far = bf16[512,128]{1,0:T(8,128)(2,1)S(1)} collective-permute-done((bf16[512,128]{1,0:T(8,128)(2,1)S(1)}, bf16[512,128]{1,0:T(8,128)(2,1)S(1)}, u32[]{:S(2)}, u32[]{:S(2)}) %collective-permute-start) | collective-permute-done | bytes 131104 | tf_op jit(solution)/shard_map/ppermute | solution.py:183
  21.5 1.3 %shard_map.87 = (bf16[512,128]{1,0:T(8,128)(2,1)S(1)}, bf16[512,128]{1,0:T(8,128)(2,1)S(1)}, bf16[512,128]{1,0:T(8,128)(2,1)S(1)}, bf16[512,128]{1,0:T(8,128)(2,1)S(1)}, bf16[256,128]{1,0:T(8,128)(2,1)S(1)}) custom-call(bf16[512,128]{1,0:T(8,128)(2,1)S(1)} %collective-permute-done.far, bf16[384,256]{1,0:T(8,128)(2,1)S(1)} %get-tuple-element.26.turned_ref.refs_6_, ...), custom_call_target="tpu_custom_call" | custom-call | flops 536870912 | tf_op jit(solution)/shard_map/pallas_call | solution.py:203
  22.8 0.1 collective-permute-start.3
  22.9 0.1 collective-permute-start.4
  23.0 4.3 %collective-permute-start.8 = (bf16[512,128]{1,0:T(8,128)(2,1)S(1)}, bf16[512,128]{1,0:T(8,128)(2,1)S(1)}, u32[]{:S(2)}, u32[]{:S(2)}) collective-permute-start(bf16[512,128]{1,0:T(8,128)(2,1)S(1)} %get-tuple-element.34), channel_id=1, source_target_pairs={{0,4},{4,0},{8,12},{12,8},{1,5},{5,1},{9,13},{13,9},{2,6},{6,2},{1... | collective-permute-start | bytes 393224 | tf_op jit(solution)/shard_map/ppermute | solution.py:183
  27.3 0.0 collective-permute-done.6.near
  27.3 0.0 collective-permute-done.5.far
  27.3 0.1 collective-permute-start.7
  27.4 0.3 shard_map.88.refs_7_
  27.7 2.9 %collective-permute-done.3.refs_1_ = bf16[512,128]{1,0:T(8,128)(2,1)S(1)} collective-permute-done((bf16[512,128]{1,0:T(8,128)(2,1)S(1)}, bf16[512,128]{1,0:T(8,128)(2,1)S(1)}, u32[]{:S(2)}, u32[]{:S(2)}) %collective-permute-start.3) | collective-permute-done | bytes 131104 | tf_op jit(solution)/shard_map/ppermute | solution.py:183
  30.6 4.1 %collective-permute-done.4.refs_2_ = bf16[512,128]{1,0:T(8,128)(2,1)S(1)} collective-permute-done((bf16[512,128]{1,0:T(8,128)(2,1)S(1)}, bf16[512,128]{1,0:T(8,128)(2,1)S(1)}, u32[]{:S(2)}, u32[]{:S(2)}) %collective-permute-start.4) | collective-permute-done | bytes 131104 | tf_op jit(solution)/shard_map/ppermute | solution.py:183
  34.7 0.0 collective-permute-done.8.refs_4_
  34.7 0.5 %collective-permute-done.7.refs_3_ = bf16[512,128]{1,0:T(8,128)(2,1)S(1)} collective-permute-done((bf16[512,128]{1,0:T(8,128)(2,1)S(1)}, bf16[512,128]{1,0:T(8,128)(2,1)S(1)}, u32[]{:S(2)}, u32[]{:S(2)}) %collective-permute-start.7) | collective-permute-done | bytes 131104 | tf_op jit(solution)/shard_map/ppermute | solution.py:183
  35.2 1.8 %shard_map.89 = (bf16[1,128,640]{2,1,0:T(8,128)(2,1)}, bf16[1,128,640]{2,1,0:T(8,128)(2,1)}, bf16[1,128,640]{2,1,0:T(8,128)(2,1)}, bf16[1,128,640]{2,1,0:T(8,128)(2,1)}) custom-call(bf16[512,128]{1,0:T(8,128)(2,1)S(1)} %get-tuple-element.29.refs_0_, bf16[512,128]{1,0:T(8,128)(2,1)S(1)} %collective-permute-done.3.refs_1_, ...), custom_call_target="tpu_custom_call" | custom-call | tf_op jit(solution)/shard_map/pallas_call | solution.py:203
Async XLA Ops:
  1.5 9.5 %collective-permute-start.2 = (bf16[512,128]{1,0:T(8,128)(2,1)S(1)}, bf16[512,128]{1,0:T(8,128)(2,1)S(1)}, u32[]{:S(2)}, u32[]{:S(2)}) collective-permute-start(bf16[512,128]{1,0:T(8,128)(2,1)S(1)} %shard_map.85), channel_id=1, source_target_pairs={{0,12},{4,8},{8,4},{12,0},{1,13},{5,9},{9,5},{13,1},{2,14},{6,10},... | collective-permute-start | bytes 393224 | tf_op jit(solution)/shard_map/ppermute | solution.py:183
  7.9 7.6 %collective-permute-start.1 = (bf16[512,128]{1,0:T(8,128)(2,1)S(1)}, bf16[512,128]{1,0:T(8,128)(2,1)S(1)}, u32[]{:S(2)}, u32[]{:S(2)}) collective-permute-start(bf16[512,128]{1,0:T(8,128)(2,1)S(1)} %get-tuple-element.23), channel_id=1, source_target_pairs={{0,4},{4,0},{8,12},{12,8},{1,5},{5,1},{9,13},{13,9},{2,6},{6,2},{1... | collective-permute-start | bytes 393224 | tf_op jit(solution)/shard_map/ppermute | solution.py:183
  7.9 13.6 %collective-permute-start = (bf16[512,128]{1,0:T(8,128)(2,1)S(1)}, bf16[512,128]{1,0:T(8,128)(2,1)S(1)}, u32[]{:S(2)}, u32[]{:S(2)}) collective-permute-start(bf16[512,128]{1,0:T(8,128)(2,1)S(1)} %get-tuple-element.21), channel_id=1, source_target_pairs={{0,8},{4,12},{8,0},{12,4},{1,9},{5,13},{9,1},{13,5},{2,10},{6,14},... | collective-permute-start | bytes 393224 | tf_op jit(solution)/shard_map/ppermute | solution.py:183
  11.0 16.3 %collective-permute-start.6 = (bf16[512,128]{1,0:T(8,128)(2,1)S(1)}, bf16[512,128]{1,0:T(8,128)(2,1)S(1)}, u32[]{:S(2)}, u32[]{:S(2)}) collective-permute-start(bf16[512,128]{1,0:T(8,128)(2,1)S(1)} %get-tuple-element.32.own), channel_id=1, source_target_pairs={{0,4},{4,0},{8,12},{12,8},{1,5},{5,1},{9,13},{13,9},{2,6},{6,2},{1... | collective-permute-start | bytes 393224 | tf_op jit(solution)/shard_map/ppermute | solution.py:183
  14.5 12.8 %collective-permute-start.5 = (bf16[512,128]{1,0:T(8,128)(2,1)S(1)}, bf16[512,128]{1,0:T(8,128)(2,1)S(1)}, u32[]{:S(2)}, u32[]{:S(2)}) collective-permute-start(bf16[512,128]{1,0:T(8,128)(2,1)S(1)} %get-tuple-element.32.own), channel_id=1, source_target_pairs={{0,8},{4,12},{8,0},{12,4},{1,9},{5,13},{9,1},{13,5},{2,10},{6,14},... | collective-permute-start | bytes 393224 | tf_op jit(solution)/shard_map/ppermute | solution.py:183
  22.8 7.7 %collective-permute-start.3 = (bf16[512,128]{1,0:T(8,128)(2,1)S(1)}, bf16[512,128]{1,0:T(8,128)(2,1)S(1)}, u32[]{:S(2)}, u32[]{:S(2)}) collective-permute-start(bf16[512,128]{1,0:T(8,128)(2,1)S(1)} %get-tuple-element.30), channel_id=1, source_target_pairs={{0,12},{4,8},{8,4},{12,0},{1,13},{5,9},{9,5},{13,1},{2,14},{6,10},... | collective-permute-start | bytes 393224 | tf_op jit(solution)/shard_map/ppermute | solution.py:183
  22.9 11.8 %collective-permute-start.4 = (bf16[512,128]{1,0:T(8,128)(2,1)S(1)}, bf16[512,128]{1,0:T(8,128)(2,1)S(1)}, u32[]{:S(2)}, u32[]{:S(2)}) collective-permute-start(bf16[512,128]{1,0:T(8,128)(2,1)S(1)} %get-tuple-element.31), channel_id=1, source_target_pairs={{0,8},{4,12},{8,0},{12,4},{1,9},{5,13},{9,1},{13,5},{2,10},{6,14},... | collective-permute-start | bytes 393224 | tf_op jit(solution)/shard_map/ppermute | solution.py:183
  23.0 11.7 %collective-permute-start.8 = (bf16[512,128]{1,0:T(8,128)(2,1)S(1)}, bf16[512,128]{1,0:T(8,128)(2,1)S(1)}, u32[]{:S(2)}, u32[]{:S(2)}) collective-permute-start(bf16[512,128]{1,0:T(8,128)(2,1)S(1)} %get-tuple-element.34), channel_id=1, source_target_pairs={{0,4},{4,0},{8,12},{12,8},{1,5},{5,1},{9,13},{13,9},{2,6},{6,2},{1... | collective-permute-start | bytes 393224 | tf_op jit(solution)/shard_map/ppermute | solution.py:183
  27.3 7.9 %collective-permute-start.7 = (bf16[512,128]{1,0:T(8,128)(2,1)S(1)}, bf16[512,128]{1,0:T(8,128)(2,1)S(1)}, u32[]{:S(2)}, u32[]{:S(2)}) collective-permute-start(bf16[512,128]{1,0:T(8,128)(2,1)S(1)} %collective-permute-done.5.far), channel_id=1, source_target_pairs={{0,4},{4,0},{8,12},{12,8},{1,5},{5,1},{9,13},{13,9},{2,6},{6,2},{1... | collective-permute-start | bytes 393224 | tf_op jit(solution)/shard_map/ppermute | solution.py:183

commit v5 on v4

--- a/solution.py
+++ b/solution.py
@@ -140,13 +140,14 @@
         put_back(out, turned_ref[n * tokens : (n + 1) * tokens, :], result)
 
 
-def shared_early_body(pick_ref, last_ref, own, near, far, rows_out):
+def shared_body(pick_ref, last_ref, turned_ref, own, near, cross, far, own_out, near_out):
     tokens = last_ref.shape[1]
-    pick = jnp.concatenate([pick_ref[:, 0 : 2 * tokens], last_ref[...]], axis=1)
-    blocks = (own, near, far)
-    rows_out[...] = dot(pick, jnp.concatenate([side_by_side(ref) for ref in blocks], axis=0)).astype(
-        BF16
-    )
+    pick = jnp.concatenate([pick_ref[...], last_ref[...]], axis=1)
+    blocks = (own, near, cross, far)
+    rows = dot(pick, jnp.concatenate([side_by_side(ref) for ref in blocks], axis=0)).astype(BF16)
+    result = attend_head(rows)
+    put_back(own_out, turned_ref[0:tokens, :], result)
+    put_back(near_out, turned_ref[tokens : 2 * tokens, :], result)
 
 
 def placed(back, tokens, lanes, outs, sems):
@@ -159,9 +160,7 @@
 
 
 def last_body(steps, *refs):
-    backs = list(refs[: len(steps) + 1])
-    relayed = backs.pop(3)
-    relpick_ref, turned_ref, rows_ref = refs[len(steps) + 1 : -6]
+    backs, (shared_here, shared_there) = refs[: len(steps)], refs[len(steps) : -6]
     outs, shared, sems = refs[-6:-2], refs[-2], refs[-1]
     tokens = outs[0].shape[1]
     me = lax.axis_index("win")
@@ -170,8 +169,16 @@
         copies += placed(back, tokens, head_lanes(me ^ step), outs, sems.at[n])
     for copy in copies:
         copy.start()
-    rows = rows_ref[...] + dot(relpick_ref[:, 2 * tokens : 3 * tokens], side_by_side(relayed)).astype(BF16)
-    put_back(shared, turned_ref[0:tokens, 0:tokens], attend_head(rows, tokens))
+    at_end = jnp.logical_or(me == 0, me == WINDOWS - 1)
+
+    @pl.when(at_end)
+    def _():
+        shared[...] = shared_there[...]
+
+    @pl.when(jnp.logical_not(at_end))
+    def _():
+        shared[...] = shared_here[...]
+
     more = placed(shared, tokens, head_lanes(WINDOWS), outs, sems.at[len(steps)])
     for copy in more:
         copy.start()
@@ -181,6 +188,10 @@
 
 def exchange(array, step):
     return lax.ppermute(array, "win", [(n, n ^ step) for n in range(WINDOWS)])
+
+
+def along(array, *pairs):
+    return lax.ppermute(array, "win", pairs)
 
 
 def after(array, other):
@@ -231,8 +242,9 @@
     got_far = exchange(far, 2)
     got_near = exchange(near, 1)
     late, got_cross = after(shared, got_cross)
-    shared_far = exchange(late, 2)
-    shared_near = exchange(late, 1)
+    shared_near = along(shared, (0, 1), (3, 2))
+    shared_cross = along(late, (1, 2), (2, 1))
+    shared_far = along(shared_near, (1, 2), (2, 1))
     pick, turned_pick, some_rows, used = call(
         early_body,
         [picks(3), turned_picks, rows, jax.ShapeDtypeStruct((8, HEAD_DIM), F32)],
@@ -244,24 +256,31 @@
     own_result, near_result, far_result, cross_result, last = call(
         main_body, [block] * 4 + [picks(1)], got_far, turned_pick, some_rows, used, flops=1 << 29
     )
+    back_near = exchange(near_result, 1)
     back_cross = exchange(cross_result, 3)
     back_far = exchange(far_result, 2)
-    back_near = exchange(near_result, 1)
-    shared_far, shared_near = after(shared_far, shared_near)
-    relayed = exchange(shared_far, 1)
-    shared_rows = call(shared_early_body, rows, pick, last, shared, shared_near, shared_far)
-    steps = (0, 3, 2, 1)
+    shared_here, for_near = call(
+        shared_body,
+        [block] * 2,
+        pick,
+        last,
+        turned_pick,
+        shared,
+        shared_near,
+        shared_cross,
+        shared_far,
+    )
+    shared_there = along(for_near, (1, 0), (2, 3))
+    steps = (0, 1, 3, 2)
     return call(
         functools.partial(last_body, steps),
         [whole] * 4,
         own_result,
+        back_near,
         back_cross,
         back_far,
-        relayed,
-        back_near,
-        pick,
-        turned_pick,
-        shared_rows,
+        shared_here,
+        shared_there,
         out_specs=[in_hbm] * 4,
         scratch_shapes=[
             pltpu.VMEM(block.shape, BF16),

time: 37.3 us -> 36.3 us (0.973)
  waiting for transfers between devices: 15.2 us -> 12.7 us
  starting transfers between devices: 14.6 us -> 16.1 us
    ppermute x0 -> x4, starting transfers between devices: none -> 4.07 us  [along(): return lax.ppermute(array, 'win', pairs)]
    ppermute x9 -> x6, waiting for transfers between devices: 15.2 us -> 11.5 us  [exchange(): return lax.ppermute(array, 'win', [(n, n ^ step) for n in range(WINDOWS)])]
    ppermute x9 -> x6, starting transfers between devices: 14.6 us -> 12.1 us  [exchange(): return lax.ppermute(array, 'win', [(n, n ^ step) for n in range(WINDOWS)])]
    ppermute x0 -> x4, waiting for transfers between devices: none -> 1.26 us  [along(): return lax.ppermute(array, 'win', pairs)]
  transfers between devices with their start and end apart: 9 -> 10, of which waited for: 5 -> 4; matrix products, arithmetic and copies ran while one was open for 0% -> 0% of each run, Pallas kernels for 10% -> 13%
where the time goes in v5:
time: 36.3 us; the launch traced here: 36 us
  starting transfers between devices  16.1 us (44%)
  waiting for transfers between devices  12.7 us (35%)
  Pallas kernels  6.44 us (18%)
  between operations  0.72 us (2%)
    ppermute x6, starting transfers between devices, exchange(): return lax.ppermute(array, 'win', [(n, n ^ step) for n in range(WINDOWS)])  12.1 us
    ppermute x6, waiting for transfers between devices, exchange(): return lax.ppermute(array, 'win', [(n, n ^ step) for n in range(WINDOWS)])  11.5 us
    pallas_call x6, Pallas kernels, call(): pl.pallas_call(body, out_shape=out_shape, cost_estimate=pl.CostEstimate(f...  6.44 us
    ppermute x4, starting transfers between devices, along(): return lax.ppermute(array, 'win', pairs)  4.07 us
    ppermute x4, waiting for transfers between devices, along(): return lax.ppermute(array, 'win', pairs)  1.26 us
  transfers between devices with their start and end apart: 10, of which 4 were waited for; matrix products, arithmetic and copies ran while one was open for 0% of the time, Pallas kernels for 13%

profile of v5, /device:TPU:0, one launch (start us, length us, event | category | flops | bytes accessed | tf_op | source)
XLA Modules:
  0.0 36.0 jit_solution(11472436278243885840)
XLA Ops:
  0.6 0.9 %shard_map.85 = bf16[512,128]{1,0:T(8,128)(2,1)S(1)} custom-call(bf16[1,128,640]{2,1,0:T(8,128)(2,1)} %q_ref.3, bf16[1,128,640]{2,1,0:T(8,128)(2,1)} %k_ref.3, bf16[1,128,640]{2,1,0:T(8,128)(2,1)} %v_ref.3, bf16[1,128,640]{2,1,0:T(8,128)(2,1)} %g_ref.3, s32[1,128]{1,0:T(1,128)} %mask_ref.3), custom_call_target="tpu_custom_call" | custom-call | tf_op jit(solution)/shard_map/pallas_call | solution.py:214
  1.5 5.1 %collective-permute-start.2 = (bf16[512,128]{1,0:T(8,128)(2,1)S(1)}, bf16[512,128]{1,0:T(8,128)(2,1)S(1)}, u32[]{:S(2)}, u32[]{:S(2)}) collective-permute-start(bf16[512,128]{1,0:T(8,128)(2,1)S(1)} %shard_map.85), channel_id=1, source_target_pairs={{0,12},{4,8},{8,4},{12,0},{1,13},{5,9},{9,5},{13,1},{2,14},{6,10},... | collective-permute-start | bytes 393224 | tf_op jit(solution)/shard_map/ppermute | solution.py:190
  6.7 1.2 %shard_map.84 = (bf16[512,128]{1,0:T(8,128)(2,1)S(1)}, bf16[512,128]{1,0:T(8,128)(2,1)S(1)}, bf16[512,128]{1,0:T(8,128)(2,1)S(1)}, bf16[512,128]{1,0:T(8,128)(2,1)S(1)}) custom-call(bf16[1,128,640]{2,1,0:T(8,128)(2,1)} %q_ref.3, bf16[1,128,640]{2,1,0:T(8,128)(2,1)} %k_ref.3, bf16[1,128,640]{2,1,0:T(8,128)(2,1)} %v_ref.3, bf16[1,128,640]{2,1,0:T(8,128)(2,1)} %g_ref.3, ...), custom_call_target="tpu_custom_call" | custom-call | tf_op jit(solution)/shard_map/pallas_call | solution.py:214
  7.9 1.5 %collective-permute-start.6 = (bf16[512,128]{1,0:T(8,128)(2,1)S(1)}, bf16[512,128]{1,0:T(8,128)(2,1)S(1)}, u32[]{:S(2)}, u32[]{:S(2)}) collective-permute-start(bf16[512,128]{1,0:T(8,128)(2,1)S(1)} %get-tuple-element.35.own), channel_id=1, source_target_pairs={{0,4},{12,8},{1,5},{13,9},{2,6},{14,10},{3,7},{15,11},{16,20},{28,... | collective-permute-start | bytes 393224 | tf_op jit(solution)/shard_map/ppermute | solution.py:194
  9.3 0.1 collective-permute-start.1
  9.4 1.9 %collective-permute-start = (bf16[512,128]{1,0:T(8,128)(2,1)S(1)}, bf16[512,128]{1,0:T(8,128)(2,1)S(1)}, u32[]{:S(2)}, u32[]{:S(2)}) collective-permute-start(bf16[512,128]{1,0:T(8,128)(2,1)S(1)} %get-tuple-element.21), channel_id=1, source_target_pairs={{0,8},{4,12},{8,0},{12,4},{1,9},{5,13},{9,1},{13,5},{2,10},{6,14},... | collective-permute-start | bytes 393224 | tf_op jit(solution)/shard_map/ppermute | solution.py:190
  11.3 0.0 collective-permute-done.2.cross
  11.3 0.7 %collective-permute-start.7 = (bf16[512,128]{1,0:T(8,128)(2,1)S(1)}, bf16[512,128]{1,0:T(8,128)(2,1)S(1)}, u32[]{:S(2)}, u32[]{:S(2)}) collective-permute-start(bf16[512,128]{1,0:T(8,128)(2,1)S(1)} %get-tuple-element.35.own), channel_id=1, source_target_pairs={{4,8},{8,4},{5,9},{9,5},{6,10},{10,6},{7,11},{11,7},{20,24},{24,20... | collective-permute-start | bytes 393224 | tf_op jit(solution)/shard_map/ppermute | solution.py:194
  12.0 1.3 %collective-permute-done.6.near = bf16[512,128]{1,0:T(8,128)(2,1)S(1)} collective-permute-done((bf16[512,128]{1,0:T(8,128)(2,1)S(1)}, bf16[512,128]{1,0:T(8,128)(2,1)S(1)}, u32[]{:S(2)}, u32[]{:S(2)}) %collective-permute-start.6) | collective-permute-done | bytes 131104 | tf_op jit(solution)/shard_map/ppermute | solution.py:194
  13.2 0.7 %collective-permute-start.8 = (bf16[512,128]{1,0:T(8,128)(2,1)S(1)}, bf16[512,128]{1,0:T(8,128)(2,1)S(1)}, u32[]{:S(2)}, u32[]{:S(2)}) collective-permute-start(bf16[512,128]{1,0:T(8,128)(2,1)S(1)} %collective-permute-done.6.near), channel_id=1, source_target_pairs={{4,8},{8,4},{5,9},{9,5},{6,10},{10,6},{7,11},{11,7},{20,24},{24,20... | collective-permute-start | bytes 393224 | tf_op jit(solution)/shard_map/ppermute | solution.py:194
  13.9 3.1 %collective-permute-done.1.near = bf16[512,128]{1,0:T(8,128)(2,1)S(1)} collective-permute-done((bf16[512,128]{1,0:T(8,128)(2,1)S(1)}, bf16[512,128]{1,0:T(8,128)(2,1)S(1)}, u32[]{:S(2)}, u32[]{:S(2)}) %collective-permute-start.1) | collective-permute-done | bytes 131104 | tf_op jit(solution)/shard_map/ppermute | solution.py:190
  17.0 0.9 %shard_map.86 = (bf16[256,384]{1,0:T(8,128)(2,1)S(1)}, bf16[384,256]{1,0:T(8,128)(2,1)S(1)}, bf16[256,512]{1,0:T(8,128)(2,1)S(1)}, f32[8,128]{1,0:T(8,128)S(1)}) custom-call(bf16[512,128]{1,0:T(8,128)(2,1)S(1)} %get-tuple-element.22.own, bf16[512,128]{1,0:T(8,128)(2,1)S(1)} %collective-permute-done.1.near, bf16[512,128]{1,0:T(8,128)(2,1)S(1)} %collective-permute-done.2.cross), custom_call_target="tpu_custom_call" | custom-call | flops 268435456 | tf_op jit(solution)/shard_map/pallas_call | solution.py:214
  17.9 0.0 collective-permute-done.far
  17.9 1.3 %shard_map.87 = (bf16[512,128]{1,0:T(8,128)(2,1)S(1)}, bf16[512,128]{1,0:T(8,128)(2,1)S(1)}, bf16[512,128]{1,0:T(8,128)(2,1)S(1)}, bf16[512,128]{1,0:T(8,128)(2,1)S(1)}, bf16[256,128]{1,0:T(8,128)(2,1)S(1)}) custom-call(bf16[512,128]{1,0:T(8,128)(2,1)S(1)} %collective-permute-done.far, bf16[384,256]{1,0:T(8,128)(2,1)S(1)} %get-tuple-element.26.turned_ref, ...), custom_call_target="tpu_custom_call" | custom-call | flops 536870912 | tf_op jit(solution)/shard_map/pallas_call | solution.py:214
  19.3 2.0 %collective-permute-start.3 = (bf16[512,128]{1,0:T(8,128)(2,1)S(1)}, bf16[512,128]{1,0:T(8,128)(2,1)S(1)}, u32[]{:S(2)}, u32[]{:S(2)}) collective-permute-start(bf16[512,128]{1,0:T(8,128)(2,1)S(1)} %get-tuple-element.30), channel_id=1, source_target_pairs={{0,4},{4,0},{8,12},{12,8},{1,5},{5,1},{9,13},{13,9},{2,6},{6,2},{1... | collective-permute-start | bytes 393224 | tf_op jit(solution)/shard_map/ppermute | solution.py:190
  21.3 3.0 %collective-permute-start.4 = (bf16[512,128]{1,0:T(8,128)(2,1)S(1)}, bf16[512,128]{1,0:T(8,128)(2,1)S(1)}, u32[]{:S(2)}, u32[]{:S(2)}) collective-permute-start(bf16[512,128]{1,0:T(8,128)(2,1)S(1)} %get-tuple-element.31), channel_id=1, source_target_pairs={{0,12},{4,8},{8,4},{12,0},{1,13},{5,9},{9,5},{13,1},{2,14},{6,10},... | collective-permute-start | bytes 393224 | tf_op jit(solution)/shard_map/ppermute | solution.py:190
  24.2 0.0 collective-permute-start.5
  24.3 0.0 collective-permute-done.7.cross
  24.3 0.0 collective-permute-done.8.far
  24.3 1.1 %shard_map.88 = (bf16[512,128]{1,0:T(8,128)(2,1)S(1)}, bf16[512,128]{1,0:T(8,128)(2,1)S(1)}) custom-call(bf16[256,384]{1,0:T(8,128)(2,1)S(1)} %get-tuple-element.33.pick_ref, bf16[256,128]{1,0:T(8,128)(2,1)S(1)} %get-tuple-element.34.last_ref, bf16[384,256]{1,0:T(8,128)(2,1)S(1)} %get-tuple-element.26.turned_ref, ...), custom_call_target="tpu_custom_call" | custom-call | tf_op jit(solution)/shard_map/pallas_call | solution.py:214
  25.4 1.3 %collective-permute-start.9 = (bf16[512,128]{1,0:T(8,128)(2,1)S(1)}, bf16[512,128]{1,0:T(8,128)(2,1)S(1)}, u32[]{:S(2)}, u32[]{:S(2)}) collective-permute-start(bf16[512,128]{1,0:T(8,128)(2,1)S(1)} %get-tuple-element.37), channel_id=1, source_target_pairs={{4,0},{8,12},{5,1},{9,13},{6,2},{10,14},{7,3},{11,15},{20,16},{24,... | collective-permute-start | bytes 393224 | tf_op jit(solution)/shard_map/ppermute | solution.py:194
  26.7 0.0 collective-permute-done.3.refs_1_
  26.7 4.3 %collective-permute-done.4.refs_2_ = bf16[512,128]{1,0:T(8,128)(2,1)S(1)} collective-permute-done((bf16[512,128]{1,0:T(8,128)(2,1)S(1)}, bf16[512,128]{1,0:T(8,128)(2,1)S(1)}, u32[]{:S(2)}, u32[]{:S(2)}) %collective-permute-start.4) | collective-permute-done | bytes 131104 | tf_op jit(solution)/shard_map/ppermute | solution.py:190
  31.0 4.0 %collective-permute-done.5.refs_3_ = bf16[512,128]{1,0:T(8,128)(2,1)S(1)} collective-permute-done((bf16[512,128]{1,0:T(8,128)(2,1)S(1)}, bf16[512,128]{1,0:T(8,128)(2,1)S(1)}, u32[]{:S(2)}, u32[]{:S(2)}) %collective-permute-start.5) | collective-permute-done | bytes 131104 | tf_op jit(solution)/shard_map/ppermute | solution.py:190
  35.0 0.0 collective-permute-done.9.refs_5_
  35.0 1.0 %shard_map.89 = (bf16[1,128,640]{2,1,0:T(8,128)(2,1)}, bf16[1,128,640]{2,1,0:T(8,128)(2,1)}, bf16[1,128,640]{2,1,0:T(8,128)(2,1)}, bf16[1,128,640]{2,1,0:T(8,128)(2,1)}) custom-call(bf16[512,128]{1,0:T(8,128)(2,1)S(1)} %get-tuple-element.29.refs_0_, bf16[512,128]{1,0:T(8,128)(2,1)S(1)} %collective-permute-done.3.refs_1_, ...), custom_call_target="tpu_custom_call" | custom-call | tf_op jit(solution)/shard_map/pallas_call | solution.py:214
Async XLA Ops:
  1.5 9.8 %collective-permute-start.2 = (bf16[512,128]{1,0:T(8,128)(2,1)S(1)}, bf16[512,128]{1,0:T(8,128)(2,1)S(1)}, u32[]{:S(2)}, u32[]{:S(2)}) collective-permute-start(bf16[512,128]{1,0:T(8,128)(2,1)S(1)} %shard_map.85), channel_id=1, source_target_pairs={{0,12},{4,8},{8,4},{12,0},{1,13},{5,9},{9,5},{13,1},{2,14},{6,10},... | collective-permute-start | bytes 393224 | tf_op jit(solution)/shard_map/ppermute | solution.py:190
  7.9 5.4 %collective-permute-start.6 = (bf16[512,128]{1,0:T(8,128)(2,1)S(1)}, bf16[512,128]{1,0:T(8,128)(2,1)S(1)}, u32[]{:S(2)}, u32[]{:S(2)}) collective-permute-start(bf16[512,128]{1,0:T(8,128)(2,1)S(1)} %get-tuple-element.35.own), channel_id=1, source_target_pairs={{0,4},{12,8},{1,5},{13,9},{2,6},{14,10},{3,7},{15,11},{16,20},{28,... | collective-permute-start | bytes 393224 | tf_op jit(solution)/shard_map/ppermute | solution.py:194
  9.3 7.7 %collective-permute-start.1 = (bf16[512,128]{1,0:T(8,128)(2,1)S(1)}, bf16[512,128]{1,0:T(8,128)(2,1)S(1)}, u32[]{:S(2)}, u32[]{:S(2)}) collective-permute-start(bf16[512,128]{1,0:T(8,128)(2,1)S(1)} %get-tuple-element.23), channel_id=1, source_target_pairs={{0,4},{4,0},{8,12},{12,8},{1,5},{5,1},{9,13},{13,9},{2,6},{6,2},{1... | collective-permute-start | bytes 393224 | tf_op jit(solution)/shard_map/ppermute | solution.py:190
  9.4 8.5 %collective-permute-start = (bf16[512,128]{1,0:T(8,128)(2,1)S(1)}, bf16[512,128]{1,0:T(8,128)(2,1)S(1)}, u32[]{:S(2)}, u32[]{:S(2)}) collective-permute-start(bf16[512,128]{1,0:T(8,128)(2,1)S(1)} %get-tuple-element.21), channel_id=1, source_target_pairs={{0,8},{4,12},{8,0},{12,4},{1,9},{5,13},{9,1},{13,5},{2,10},{6,14},... | collective-permute-start | bytes 393224 | tf_op jit(solution)/shard_map/ppermute | solution.py:190
  11.3 12.9 %collective-permute-start.7 = (bf16[512,128]{1,0:T(8,128)(2,1)S(1)}, bf16[512,128]{1,0:T(8,128)(2,1)S(1)}, u32[]{:S(2)}, u32[]{:S(2)}) collective-permute-start(bf16[512,128]{1,0:T(8,128)(2,1)S(1)} %get-tuple-element.35.own), channel_id=1, source_target_pairs={{4,8},{8,4},{5,9},{9,5},{6,10},{10,6},{7,11},{11,7},{20,24},{24,20... | collective-permute-start | bytes 393224 | tf_op jit(solution)/shard_map/ppermute | solution.py:194
  13.2 11.0 %collective-permute-start.8 = (bf16[512,128]{1,0:T(8,128)(2,1)S(1)}, bf16[512,128]{1,0:T(8,128)(2,1)S(1)}, u32[]{:S(2)}, u32[]{:S(2)}) collective-permute-start(bf16[512,128]{1,0:T(8,128)(2,1)S(1)} %collective-permute-done.6.near), channel_id=1, source_target_pairs={{4,8},{8,4},{5,9},{9,5},{6,10},{10,6},{7,11},{11,7},{20,24},{24,20... | collective-permute-start | bytes 393224 | tf_op jit(solution)/shard_map/ppermute | solution.py:194
  19.3 7.4 %collective-permute-start.3 = (bf16[512,128]{1,0:T(8,128)(2,1)S(1)}, bf16[512,128]{1,0:T(8,128)(2,1)S(1)}, u32[]{:S(2)}, u32[]{:S(2)}) collective-permute-start(bf16[512,128]{1,0:T(8,128)(2,1)S(1)} %get-tuple-element.30), channel_id=1, source_target_pairs={{0,4},{4,0},{8,12},{12,8},{1,5},{5,1},{9,13},{13,9},{2,6},{6,2},{1... | collective-permute-start | bytes 393224 | tf_op jit(solution)/shard_map/ppermute | solution.py:190
  21.3 9.7 %collective-permute-start.4 = (bf16[512,128]{1,0:T(8,128)(2,1)S(1)}, bf16[512,128]{1,0:T(8,128)(2,1)S(1)}, u32[]{:S(2)}, u32[]{:S(2)}) collective-permute-start(bf16[512,128]{1,0:T(8,128)(2,1)S(1)} %get-tuple-element.31), channel_id=1, source_target_pairs={{0,12},{4,8},{8,4},{12,0},{1,13},{5,9},{9,5},{13,1},{2,14},{6,10},... | collective-permute-start | bytes 393224 | tf_op jit(solution)/shard_map/ppermute | solution.py:190
  24.2 10.8 %collective-permute-start.5 = (bf16[512,128]{1,0:T(8,128)(2,1)S(1)}, bf16[512,128]{1,0:T(8,128)(2,1)S(1)}, u32[]{:S(2)}, u32[]{:S(2)}) collective-permute-start(bf16[512,128]{1,0:T(8,128)(2,1)S(1)} %get-tuple-element.32), channel_id=1, source_target_pairs={{0,8},{4,12},{8,0},{12,4},{1,9},{5,13},{9,1},{13,5},{2,10},{6,14},... | collective-permute-start | bytes 393224 | tf_op jit(solution)/shard_map/ppermute | solution.py:190
  25.4 9.6 %collective-permute-start.9 = (bf16[512,128]{1,0:T(8,128)(2,1)S(1)}, bf16[512,128]{1,0:T(8,128)(2,1)S(1)}, u32[]{:S(2)}, u32[]{:S(2)}) collective-permute-start(bf16[512,128]{1,0:T(8,128)(2,1)S(1)} %get-tuple-element.37), channel_id=1, source_target_pairs={{4,0},{8,12},{5,1},{9,13},{6,2},{10,14},{7,3},{11,15},{20,16},{24,... | collective-permute-start | bytes 393224 | tf_op jit(solution)/shard_map/ppermute | solution.py:194

commit v6 on v5

--- a/solution.py
+++ b/solution.py
@@ -257,8 +257,8 @@
         main_body, [block] * 4 + [picks(1)], got_far, turned_pick, some_rows, used, flops=1 << 29
     )
     back_near = exchange(near_result, 1)
+    back_far = exchange(far_result, 2)
     back_cross = exchange(cross_result, 3)
-    back_far = exchange(far_result, 2)
     shared_here, for_near = call(
         shared_body,
         [block] * 2,
@@ -271,14 +271,14 @@
         shared_far,
     )
     shared_there = along(for_near, (1, 0), (2, 3))
-    steps = (0, 1, 3, 2)
+    steps = (0, 1, 2, 3)
     return call(
         functools.partial(last_body, steps),
         [whole] * 4,
         own_result,
         back_near,
+        back_far,
         back_cross,
-        back_far,
         shared_here,
         shared_there,
         out_specs=[in_hbm] * 4,

time: 36.3 us -> 35.7 us (0.983)
  waiting for transfers between devices: 12.7 us -> 12.1 us
    ppermute x6, waiting for transfers between devices: 11.5 us -> 10.2 us  [exchange(): return lax.ppermute(array, 'win', [(n, n ^ step) for n in range(WINDOWS)])]
    ppermute x4, waiting for transfers between devices: 1.26 us -> 1.9 us  [along(): return lax.ppermute(array, 'win', pairs)]
where the time goes in v6:
time: 35.7 us; the launch traced here: 35.4 us
  starting transfers between devices  16.1 us (45%)
  waiting for transfers between devices  12.1 us (34%)
  Pallas kernels  6.44 us (18%)
  between operations  0.72 us (2%)
    ppermute x6, starting transfers between devices, exchange(): return lax.ppermute(array, 'win', [(n, n ^ step) for n in range(WINDOWS)])  12.1 us
    ppermute x6, waiting for transfers between devices, exchange(): return lax.ppermute(array, 'win', [(n, n ^ step) for n in range(WINDOWS)])  10.2 us
    pallas_call x6, Pallas kernels, call(): pl.pallas_call(body, out_shape=out_shape, cost_estimate=pl.CostEstimate(f...  6.44 us
    ppermute x4, starting transfers between devices, along(): return lax.ppermute(array, 'win', pairs)  4.07 us
    ppermute x4, waiting for transfers between devices, along(): return lax.ppermute(array, 'win', pairs)  1.9 us
  transfers between devices with their start and end apart: 10, of which 4 were waited for; matrix products, arithmetic and copies ran while one was open for 0% of the time, Pallas kernels for 13%

profile of v6, /device:TPU:0, one launch (start us, length us, event | category | flops | bytes accessed | tf_op | source)
XLA Modules:
  0.0 35.4 jit_solution(6110526864932614624)
XLA Ops:
  0.6 0.9 %shard_map.85 = bf16[512,128]{1,0:T(8,128)(2,1)S(1)} custom-call(bf16[1,128,640]{2,1,0:T(8,128)(2,1)} %q_ref.3, bf16[1,128,640]{2,1,0:T(8,128)(2,1)} %k_ref.3, bf16[1,128,640]{2,1,0:T(8,128)(2,1)} %v_ref.3, bf16[1,128,640]{2,1,0:T(8,128)(2,1)} %g_ref.3, s32[1,128]{1,0:T(1,128)} %mask_ref.3), custom_call_target="tpu_custom_call" | custom-call | tf_op jit(solution)/shard_map/pallas_call | solution.py:214
  1.5 5.1 %collective-permute-start.2 = (bf16[512,128]{1,0:T(8,128)(2,1)S(1)}, bf16[512,128]{1,0:T(8,128)(2,1)S(1)}, u32[]{:S(2)}, u32[]{:S(2)}) collective-permute-start(bf16[512,128]{1,0:T(8,128)(2,1)S(1)} %shard_map.85), channel_id=1, source_target_pairs={{0,12},{4,8},{8,4},{12,0},{1,13},{5,9},{9,5},{13,1},{2,14},{6,10},... | collective-permute-start | bytes 393224 | tf_op jit(solution)/shard_map/ppermute | solution.py:190
  6.7 1.2 %shard_map.84 = (bf16[512,128]{1,0:T(8,128)(2,1)S(1)}, bf16[512,128]{1,0:T(8,128)(2,1)S(1)}, bf16[512,128]{1,0:T(8,128)(2,1)S(1)}, bf16[512,128]{1,0:T(8,128)(2,1)S(1)}) custom-call(bf16[1,128,640]{2,1,0:T(8,128)(2,1)} %q_ref.3, bf16[1,128,640]{2,1,0:T(8,128)(2,1)} %k_ref.3, bf16[1,128,640]{2,1,0:T(8,128)(2,1)} %v_ref.3, bf16[1,128,640]{2,1,0:T(8,128)(2,1)} %g_ref.3, ...), custom_call_target="tpu_custom_call" | custom-call | tf_op jit(solution)/shard_map/pallas_call | solution.py:214
  7.9 1.5 %collective-permute-start.6 = (bf16[512,128]{1,0:T(8,128)(2,1)S(1)}, bf16[512,128]{1,0:T(8,128)(2,1)S(1)}, u32[]{:S(2)}, u32[]{:S(2)}) collective-permute-start(bf16[512,128]{1,0:T(8,128)(2,1)S(1)} %get-tuple-element.35.own), channel_id=1, source_target_pairs={{0,4},{12,8},{1,5},{13,9},{2,6},{14,10},{3,7},{15,11},{16,20},{28,... | collective-permute-start | bytes 393224 | tf_op jit(solution)/shard_map/ppermute | solution.py:194
  9.3 0.1 collective-permute-start.1
  9.4 1.9 %collective-permute-start = (bf16[512,128]{1,0:T(8,128)(2,1)S(1)}, bf16[512,128]{1,0:T(8,128)(2,1)S(1)}, u32[]{:S(2)}, u32[]{:S(2)}) collective-permute-start(bf16[512,128]{1,0:T(8,128)(2,1)S(1)} %get-tuple-element.21), channel_id=1, source_target_pairs={{0,8},{4,12},{8,0},{12,4},{1,9},{5,13},{9,1},{13,5},{2,10},{6,14},... | collective-permute-start | bytes 393224 | tf_op jit(solution)/shard_map/ppermute | solution.py:190
  11.3 0.0 collective-permute-done.2.cross
  11.3 0.7 %collective-permute-start.7 = (bf16[512,128]{1,0:T(8,128)(2,1)S(1)}, bf16[512,128]{1,0:T(8,128)(2,1)S(1)}, u32[]{:S(2)}, u32[]{:S(2)}) collective-permute-start(bf16[512,128]{1,0:T(8,128)(2,1)S(1)} %get-tuple-element.35.own), channel_id=1, source_target_pairs={{4,8},{8,4},{5,9},{9,5},{6,10},{10,6},{7,11},{11,7},{20,24},{24,20... | collective-permute-start | bytes 393224 | tf_op jit(solution)/shard_map/ppermute | solution.py:194
  12.0 1.3 %collective-permute-done.6.near = bf16[512,128]{1,0:T(8,128)(2,1)S(1)} collective-permute-done((bf16[512,128]{1,0:T(8,128)(2,1)S(1)}, bf16[512,128]{1,0:T(8,128)(2,1)S(1)}, u32[]{:S(2)}, u32[]{:S(2)}) %collective-permute-start.6) | collective-permute-done | bytes 131104 | tf_op jit(solution)/shard_map/ppermute | solution.py:194
  13.2 0.7 %collective-permute-start.8 = (bf16[512,128]{1,0:T(8,128)(2,1)S(1)}, bf16[512,128]{1,0:T(8,128)(2,1)S(1)}, u32[]{:S(2)}, u32[]{:S(2)}) collective-permute-start(bf16[512,128]{1,0:T(8,128)(2,1)S(1)} %collective-permute-done.6.near), channel_id=1, source_target_pairs={{4,8},{8,4},{5,9},{9,5},{6,10},{10,6},{7,11},{11,7},{20,24},{24,20... | collective-permute-start | bytes 393224 | tf_op jit(solution)/shard_map/ppermute | solution.py:194
  13.9 3.1 %collective-permute-done.1.near = bf16[512,128]{1,0:T(8,128)(2,1)S(1)} collective-permute-done((bf16[512,128]{1,0:T(8,128)(2,1)S(1)}, bf16[512,128]{1,0:T(8,128)(2,1)S(1)}, u32[]{:S(2)}, u32[]{:S(2)}) %collective-permute-start.1) | collective-permute-done | bytes 131104 | tf_op jit(solution)/shard_map/ppermute | solution.py:190
  17.0 0.9 %shard_map.86 = (bf16[256,384]{1,0:T(8,128)(2,1)S(1)}, bf16[384,256]{1,0:T(8,128)(2,1)S(1)}, bf16[256,512]{1,0:T(8,128)(2,1)S(1)}, f32[8,128]{1,0:T(8,128)S(1)}) custom-call(bf16[512,128]{1,0:T(8,128)(2,1)S(1)} %get-tuple-element.22.own, bf16[512,128]{1,0:T(8,128)(2,1)S(1)} %collective-permute-done.1.near, bf16[512,128]{1,0:T(8,128)(2,1)S(1)} %collective-permute-done.2.cross), custom_call_target="tpu_custom_call" | custom-call | flops 268435456 | tf_op jit(solution)/shard_map/pallas_call | solution.py:214
  17.9 0.0 collective-permute-done.far
  17.9 1.3 %shard_map.87 = (bf16[512,128]{1,0:T(8,128)(2,1)S(1)}, bf16[512,128]{1,0:T(8,128)(2,1)S(1)}, bf16[512,128]{1,0:T(8,128)(2,1)S(1)}, bf16[512,128]{1,0:T(8,128)(2,1)S(1)}, bf16[256,128]{1,0:T(8,128)(2,1)S(1)}) custom-call(bf16[512,128]{1,0:T(8,128)(2,1)S(1)} %collective-permute-done.far, bf16[384,256]{1,0:T(8,128)(2,1)S(1)} %get-tuple-element.26.turned_ref, ...), custom_call_target="tpu_custom_call" | custom-call | flops 536870912 | tf_op jit(solution)/shard_map/pallas_call | solution.py:214
  19.3 2.0 %collective-permute-start.3 = (bf16[512,128]{1,0:T(8,128)(2,1)S(1)}, bf16[512,128]{1,0:T(8,128)(2,1)S(1)}, u32[]{:S(2)}, u32[]{:S(2)}) collective-permute-start(bf16[512,128]{1,0:T(8,128)(2,1)S(1)} %get-tuple-element.30), channel_id=1, source_target_pairs={{0,4},{4,0},{8,12},{12,8},{1,5},{5,1},{9,13},{13,9},{2,6},{6,2},{1... | collective-permute-start | bytes 393224 | tf_op jit(solution)/shard_map/ppermute | solution.py:190
  21.3 1.6 %collective-permute-start.4 = (bf16[512,128]{1,0:T(8,128)(2,1)S(1)}, bf16[512,128]{1,0:T(8,128)(2,1)S(1)}, u32[]{:S(2)}, u32[]{:S(2)}) collective-permute-start(bf16[512,128]{1,0:T(8,128)(2,1)S(1)} %get-tuple-element.31), channel_id=1, source_target_pairs={{0,8},{4,12},{8,0},{12,4},{1,9},{5,13},{9,1},{13,5},{2,10},{6,14},... | collective-permute-start | bytes 393224 | tf_op jit(solution)/shard_map/ppermute | solution.py:190
  22.9 1.4 %collective-permute-start.5 = (bf16[512,128]{1,0:T(8,128)(2,1)S(1)}, bf16[512,128]{1,0:T(8,128)(2,1)S(1)}, u32[]{:S(2)}, u32[]{:S(2)}) collective-permute-start(bf16[512,128]{1,0:T(8,128)(2,1)S(1)} %get-tuple-element.32), channel_id=1, source_target_pairs={{0,12},{4,8},{8,4},{12,0},{1,13},{5,9},{9,5},{13,1},{2,14},{6,10},... | collective-permute-start | bytes 393224 | tf_op jit(solution)/shard_map/ppermute | solution.py:190
  24.3 0.0 collective-permute-done.7.cross
  24.3 0.0 collective-permute-done.8.far
  24.3 1.1 %shard_map.88 = (bf16[512,128]{1,0:T(8,128)(2,1)S(1)}, bf16[512,128]{1,0:T(8,128)(2,1)S(1)}) custom-call(bf16[256,384]{1,0:T(8,128)(2,1)S(1)} %get-tuple-element.33.pick_ref, bf16[256,128]{1,0:T(8,128)(2,1)S(1)} %get-tuple-element.34.last_ref, bf16[384,256]{1,0:T(8,128)(2,1)S(1)} %get-tuple-element.26.turned_ref, ...), custom_call_target="tpu_custom_call" | custom-call | tf_op jit(solution)/shard_map/pallas_call | solution.py:214
  25.4 1.3 %collective-permute-start.9 = (bf16[512,128]{1,0:T(8,128)(2,1)S(1)}, bf16[512,128]{1,0:T(8,128)(2,1)S(1)}, u32[]{:S(2)}, u32[]{:S(2)}) collective-permute-start(bf16[512,128]{1,0:T(8,128)(2,1)S(1)} %get-tuple-element.37), channel_id=1, source_target_pairs={{4,0},{8,12},{5,1},{9,13},{6,2},{10,14},{7,3},{11,15},{20,16},{24,... | collective-permute-start | bytes 393224 | tf_op jit(solution)/shard_map/ppermute | solution.py:194
  26.7 0.0 collective-permute-done.3.refs_1_
  26.7 7.0 %collective-permute-done.4.refs_2_ = bf16[512,128]{1,0:T(8,128)(2,1)S(1)} collective-permute-done((bf16[512,128]{1,0:T(8,128)(2,1)S(1)}, bf16[512,128]{1,0:T(8,128)(2,1)S(1)}, u32[]{:S(2)}, u32[]{:S(2)}) %collective-permute-start.4) | collective-permute-done | bytes 131104 | tf_op jit(solution)/shard_map/ppermute | solution.py:190
  33.7 0.0 collective-permute-done.5.refs_3_
  33.7 0.6 %collective-permute-done.9.refs_5_ = bf16[512,128]{1,0:T(8,128)(2,1)S(1)} collective-permute-done((bf16[512,128]{1,0:T(8,128)(2,1)S(1)}, bf16[512,128]{1,0:T(8,128)(2,1)S(1)}, u32[]{:S(2)}, u32[]{:S(2)}) %collective-permute-start.9) | collective-permute-done | bytes 131104 | tf_op jit(solution)/shard_map/ppermute | solution.py:194
  34.4 1.0 %shard_map.89 = (bf16[1,128,640]{2,1,0:T(8,128)(2,1)}, bf16[1,128,640]{2,1,0:T(8,128)(2,1)}, bf16[1,128,640]{2,1,0:T(8,128)(2,1)}, bf16[1,128,640]{2,1,0:T(8,128)(2,1)}) custom-call(bf16[512,128]{1,0:T(8,128)(2,1)S(1)} %get-tuple-element.29.refs_0_, bf16[512,128]{1,0:T(8,128)(2,1)S(1)} %collective-permute-done.3.refs_1_, ...), custom_call_target="tpu_custom_call" | custom-call | tf_op jit(solution)/shard_map/pallas_call | solution.py:214
Async XLA Ops:
  1.5 9.8 %collective-permute-start.2 = (bf16[512,128]{1,0:T(8,128)(2,1)S(1)}, bf16[512,128]{1,0:T(8,128)(2,1)S(1)}, u32[]{:S(2)}, u32[]{:S(2)}) collective-permute-start(bf16[512,128]{1,0:T(8,128)(2,1)S(1)} %shard_map.85), channel_id=1, source_target_pairs={{0,12},{4,8},{8,4},{12,0},{1,13},{5,9},{9,5},{13,1},{2,14},{6,10},... | collective-permute-start | bytes 393224 | tf_op jit(solution)/shard_map/ppermute | solution.py:190
  7.9 5.4 %collective-permute-start.6 = (bf16[512,128]{1,0:T(8,128)(2,1)S(1)}, bf16[512,128]{1,0:T(8,128)(2,1)S(1)}, u32[]{:S(2)}, u32[]{:S(2)}) collective-permute-start(bf16[512,128]{1,0:T(8,128)(2,1)S(1)} %get-tuple-element.35.own), channel_id=1, source_target_pairs={{0,4},{12,8},{1,5},{13,9},{2,6},{14,10},{3,7},{15,11},{16,20},{28,... | collective-permute-start | bytes 393224 | tf_op jit(solution)/shard_map/ppermute | solution.py:194
  9.3 7.7 %collective-permute-start.1 = (bf16[512,128]{1,0:T(8,128)(2,1)S(1)}, bf16[512,128]{1,0:T(8,128)(2,1)S(1)}, u32[]{:S(2)}, u32[]{:S(2)}) collective-permute-start(bf16[512,128]{1,0:T(8,128)(2,1)S(1)} %get-tuple-element.23), channel_id=1, source_target_pairs={{0,4},{4,0},{8,12},{12,8},{1,5},{5,1},{9,13},{13,9},{2,6},{6,2},{1... | collective-permute-start | bytes 393224 | tf_op jit(solution)/shard_map/ppermute | solution.py:190
  9.4 8.5 %collective-permute-start = (bf16[512,128]{1,0:T(8,128)(2,1)S(1)}, bf16[512,128]{1,0:T(8,128)(2,1)S(1)}, u32[]{:S(2)}, u32[]{:S(2)}) collective-permute-start(bf16[512,128]{1,0:T(8,128)(2,1)S(1)} %get-tuple-element.21), channel_id=1, source_target_pairs={{0,8},{4,12},{8,0},{12,4},{1,9},{5,13},{9,1},{13,5},{2,10},{6,14},... | collective-permute-start | bytes 393224 | tf_op jit(solution)/shard_map/ppermute | solution.py:190
  11.3 12.9 %collective-permute-start.7 = (bf16[512,128]{1,0:T(8,128)(2,1)S(1)}, bf16[512,128]{1,0:T(8,128)(2,1)S(1)}, u32[]{:S(2)}, u32[]{:S(2)}) collective-permute-start(bf16[512,128]{1,0:T(8,128)(2,1)S(1)} %get-tuple-element.35.own), channel_id=1, source_target_pairs={{4,8},{8,4},{5,9},{9,5},{6,10},{10,6},{7,11},{11,7},{20,24},{24,20... | collective-permute-start | bytes 393224 | tf_op jit(solution)/shard_map/ppermute | solution.py:194
  13.2 11.0 %collective-permute-start.8 = (bf16[512,128]{1,0:T(8,128)(2,1)S(1)}, bf16[512,128]{1,0:T(8,128)(2,1)S(1)}, u32[]{:S(2)}, u32[]{:S(2)}) collective-permute-start(bf16[512,128]{1,0:T(8,128)(2,1)S(1)} %collective-permute-done.6.near), channel_id=1, source_target_pairs={{4,8},{8,4},{5,9},{9,5},{6,10},{10,6},{7,11},{11,7},{20,24},{24,20... | collective-permute-start | bytes 393224 | tf_op jit(solution)/shard_map/ppermute | solution.py:194
  19.3 7.4 %collective-permute-start.3 = (bf16[512,128]{1,0:T(8,128)(2,1)S(1)}, bf16[512,128]{1,0:T(8,128)(2,1)S(1)}, u32[]{:S(2)}, u32[]{:S(2)}) collective-permute-start(bf16[512,128]{1,0:T(8,128)(2,1)S(1)} %get-tuple-element.30), channel_id=1, source_target_pairs={{0,4},{4,0},{8,12},{12,8},{1,5},{5,1},{9,13},{13,9},{2,6},{6,2},{1... | collective-permute-start | bytes 393224 | tf_op jit(solution)/shard_map/ppermute | solution.py:190
  21.3 12.4 %collective-permute-start.4 = (bf16[512,128]{1,0:T(8,128)(2,1)S(1)}, bf16[512,128]{1,0:T(8,128)(2,1)S(1)}, u32[]{:S(2)}, u32[]{:S(2)}) collective-permute-start(bf16[512,128]{1,0:T(8,128)(2,1)S(1)} %get-tuple-element.31), channel_id=1, source_target_pairs={{0,8},{4,12},{8,0},{12,4},{1,9},{5,13},{9,1},{13,5},{2,10},{6,14},... | collective-permute-start | bytes 393224 | tf_op jit(solution)/shard_map/ppermute | solution.py:190
  22.9 10.9 %collective-permute-start.5 = (bf16[512,128]{1,0:T(8,128)(2,1)S(1)}, bf16[512,128]{1,0:T(8,128)(2,1)S(1)}, u32[]{:S(2)}, u32[]{:S(2)}) collective-permute-start(bf16[512,128]{1,0:T(8,128)(2,1)S(1)} %get-tuple-element.32), channel_id=1, source_target_pairs={{0,12},{4,8},{8,4},{12,0},{1,13},{5,9},{9,5},{13,1},{2,14},{6,10},... | collective-permute-start | bytes 393224 | tf_op jit(solution)/shard_map/ppermute | solution.py:190
  25.4 9.0 %collective-permute-start.9 = (bf16[512,128]{1,0:T(8,128)(2,1)S(1)}, bf16[512,128]{1,0:T(8,128)(2,1)S(1)}, u32[]{:S(2)}, u32[]{:S(2)}) collective-permute-start(bf16[512,128]{1,0:T(8,128)(2,1)S(1)} %get-tuple-element.37), channel_id=1, source_target_pairs={{4,0},{8,12},{5,1},{9,13},{6,2},{10,14},{7,3},{11,15},{20,16},{24,... | collective-permute-start | bytes 393224 | tf_op jit(solution)/shard_map/ppermute | solution.py:194

commit v7 on v6

--- a/solution.py
+++ b/solution.py
@@ -116,9 +116,9 @@
     return dot(pick, unit, 0, 0).astype(BF16)
 
 
-def early_body(own, near, cross, pick_out, turned_out, rows_out, used_out):
+def early_body(own, cross, pick_out, turned_out, rows_out, used_out):
     kept = pick_out.shape[0]
-    blocks = (own, near, cross)
+    blocks = (own, cross)
     pick, used = picks_of(blocks, kept, jnp.zeros((1, 1), F32))
     pick_out[...] = pick
     used_out[...] = jnp.broadcast_to(used, used_out.shape)
@@ -128,26 +128,42 @@
     turned_out[...] = turned(pick)
 
 
-def main_body(far, turned_ref, rows_ref, used_ref, own_out, near_out, far_out, cross_out, last_out):
+def main_body(
+    far,
+    near,
+    turned_ref,
+    rows_ref,
+    used_ref,
+    own_out,
+    near_out,
+    far_out,
+    cross_out,
+    last_out,
+    turned_out,
+):
     kept = rows_ref.shape[0]
     tokens = far.shape[0] // 4
-    last, _ = picks_of((far,), kept, used_ref[0:1, 0:1])
+    last, _ = picks_of((near, far), kept, used_ref[0:1, 0:1])
     last_out[...] = last
-    rows = rows_ref[...] + dot(last, side_by_side(far)).astype(BF16)
+    blocks = jnp.concatenate([side_by_side(near), side_by_side(far)], axis=0)
+    rows = rows_ref[...] + dot(last, blocks).astype(BF16)
+    turned_last = turned(last)
+    turned_out[...] = turned_last
     result = attend_head(rows)
-    put_back(far_out, turned(last), result)
-    for n, out in ((1, near_out), (2, cross_out), (0, own_out)):
+    put_back(near_out, turned_last[0:tokens, :], result)
+    put_back(far_out, turned_last[tokens:, :], result)
+    for n, out in ((1, cross_out), (0, own_out)):
         put_back(out, turned_ref[n * tokens : (n + 1) * tokens, :], result)
 
 
-def shared_body(pick_ref, last_ref, turned_ref, own, near, cross, far, own_out, near_out):
-    tokens = last_ref.shape[1]
+def shared_body(pick_ref, last_ref, turned_ref, turned_last_ref, own, cross, near, far, own_out, near_out):
+    tokens = last_ref.shape[1] // 2
     pick = jnp.concatenate([pick_ref[...], last_ref[...]], axis=1)
-    blocks = (own, near, cross, far)
+    blocks = (own, cross, near, far)
     rows = dot(pick, jnp.concatenate([side_by_side(ref) for ref in blocks], axis=0)).astype(BF16)
     result = attend_head(rows)
     put_back(own_out, turned_ref[0:tokens, :], result)
-    put_back(near_out, turned_ref[tokens : 2 * tokens, :], result)
+    put_back(near_out, turned_last_ref[0:tokens, :], result)
 
 
 def placed(back, tokens, lanes, outs, sems):
@@ -204,7 +220,7 @@
     in_hbm = pl.BlockSpec(memory_space=pltpu.HBM)
     block = jax.ShapeDtypeStruct((4 * tokens, HEAD_DIM), BF16)
     rows = jax.ShapeDtypeStruct((kept, 4 * HEAD_DIM), BF16)
-    turned_picks = jax.ShapeDtypeStruct((3 * tokens, kept), BF16)
+    turned_picks = jax.ShapeDtypeStruct((2 * tokens, kept), BF16)
     whole = jax.ShapeDtypeStruct(queries.shape, BF16)
 
     def picks(windows):
@@ -247,14 +263,20 @@
     shared_far = along(shared_near, (1, 2), (2, 1))
     pick, turned_pick, some_rows, used = call(
         early_body,
-        [picks(3), turned_picks, rows, jax.ShapeDtypeStruct((8, HEAD_DIM), F32)],
+        [picks(2), turned_picks, rows, jax.ShapeDtypeStruct((8, HEAD_DIM), F32)],
         own,
-        got_near,
         got_cross,
         flops=1 << 28,
     )
-    own_result, near_result, far_result, cross_result, last = call(
-        main_body, [block] * 4 + [picks(1)], got_far, turned_pick, some_rows, used, flops=1 << 29
+    own_result, near_result, far_result, cross_result, last, turned_last = call(
+        main_body,
+        [block] * 4 + [picks(2), turned_picks],
+        got_far,
+        got_near,
+        turned_pick,
+        some_rows,
+        used,
+        flops=1 << 29,
     )
     back_near = exchange(near_result, 1)
     back_far = exchange(far_result, 2)
@@ -265,9 +287,10 @@
         pick,
         last,
         turned_pick,
+        turned_last,
         shared,
+        shared_cross,
         shared_near,
-        shared_cross,
         shared_far,
     )
     shared_there = along(for_near, (1, 0), (2, 3))

time: 35.7 us -> 35.6 us (level)
  starting transfers between devices: 16.1 us -> 15.6 us
  waiting for transfers between devices: 12.1 us -> 12.5 us
    ppermute x4, waiting for transfers between devices: 1.9 us -> 2.44 us  [along(): return lax.ppermute(array, 'win', pairs)]
    ppermute x6, starting transfers between devices: 12.1 us -> 11.5 us  [exchange(): return lax.ppermute(array, 'win', [(n, n ^ step) for n in range(WINDOWS)])]
where the time goes in v7:
time: 35.6 us; the launch traced here: 35.2 us
  starting transfers between devices  15.6 us (44%)
  waiting for transfers between devices  12.5 us (35%)
  Pallas kernels  6.43 us (18%)
  between operations  0.72 us (2%)
    ppermute x6, starting transfers between devices, exchange(): return lax.ppermute(array, 'win', [(n, n ^ step) for n in range(WINDOWS)])  11.5 us
    ppermute x6, waiting for transfers between devices, exchange(): return lax.ppermute(array, 'win', [(n, n ^ step) for n in range(WINDOWS)])  10 us
    pallas_call x6, Pallas kernels, call(): pl.pallas_call(body, out_shape=out_shape, cost_estimate=pl.CostEstimate(f...  6.43 us
    ppermute x4, starting transfers between devices, along(): return lax.ppermute(array, 'win', pairs)  4.07 us
    ppermute x4, waiting for transfers between devices, along(): return lax.ppermute(array, 'win', pairs)  2.44 us
  transfers between devices with their start and end apart: 10, of which 4 were waited for; matrix products, arithmetic and copies ran while one was open for 0% of the time, Pallas kernels for 13%

profile of v7, /device:TPU:0, one launch (start us, length us, event | category | flops | bytes accessed | tf_op | source)
XLA Modules:
  0.0 35.2 jit_solution(17352866348720759400)
XLA Ops:
  0.6 0.9 %shard_map.85 = bf16[512,128]{1,0:T(8,128)(2,1)S(1)} custom-call(bf16[1,128,640]{2,1,0:T(8,128)(2,1)} %q_ref.3, bf16[1,128,640]{2,1,0:T(8,128)(2,1)} %k_ref.3, bf16[1,128,640]{2,1,0:T(8,128)(2,1)} %v_ref.3, bf16[1,128,640]{2,1,0:T(8,128)(2,1)} %g_ref.3, s32[1,128]{1,0:T(1,128)} %mask_ref.3), custom_call_target="tpu_custom_call" | custom-call | tf_op jit(solution)/shard_map/pallas_call | solution.py:230
  1.5 5.1 %collective-permute-start.2 = (bf16[512,128]{1,0:T(8,128)(2,1)S(1)}, bf16[512,128]{1,0:T(8,128)(2,1)S(1)}, u32[]{:S(2)}, u32[]{:S(2)}) collective-permute-start(bf16[512,128]{1,0:T(8,128)(2,1)S(1)} %shard_map.85), channel_id=1, source_target_pairs={{0,12},{4,8},{8,4},{12,0},{1,13},{5,9},{9,5},{13,1},{2,14},{6,10},... | collective-permute-start | bytes 393224 | tf_op jit(solution)/shard_map/ppermute | solution.py:206
  6.7 1.2 %shard_map.84 = (bf16[512,128]{1,0:T(8,128)(2,1)S(1)}, bf16[512,128]{1,0:T(8,128)(2,1)S(1)}, bf16[512,128]{1,0:T(8,128)(2,1)S(1)}, bf16[512,128]{1,0:T(8,128)(2,1)S(1)}) custom-call(bf16[1,128,640]{2,1,0:T(8,128)(2,1)} %q_ref.3, bf16[1,128,640]{2,1,0:T(8,128)(2,1)} %k_ref.3, bf16[1,128,640]{2,1,0:T(8,128)(2,1)} %v_ref.3, bf16[1,128,640]{2,1,0:T(8,128)(2,1)} %g_ref.3, ...), custom_call_target="tpu_custom_call" | custom-call | tf_op jit(solution)/shard_map/pallas_call | solution.py:230
  7.9 1.5 %collective-permute-start.7 = (bf16[512,128]{1,0:T(8,128)(2,1)S(1)}, bf16[512,128]{1,0:T(8,128)(2,1)S(1)}, u32[]{:S(2)}, u32[]{:S(2)}) collective-permute-start(bf16[512,128]{1,0:T(8,128)(2,1)S(1)} %get-tuple-element.37.own), channel_id=1, source_target_pairs={{0,4},{12,8},{1,5},{13,9},{2,6},{14,10},{3,7},{15,11},{16,20},{28,... | collective-permute-start | bytes 393224 | tf_op jit(solution)/shard_map/ppermute | solution.py:210
  9.3 0.1 collective-permute-start
  9.4 1.9 %collective-permute-start.1 = (bf16[512,128]{1,0:T(8,128)(2,1)S(1)}, bf16[512,128]{1,0:T(8,128)(2,1)S(1)}, u32[]{:S(2)}, u32[]{:S(2)}) collective-permute-start(bf16[512,128]{1,0:T(8,128)(2,1)S(1)} %get-tuple-element.23), channel_id=1, source_target_pairs={{0,4},{4,0},{8,12},{12,8},{1,5},{5,1},{9,13},{13,9},{2,6},{6,2},{1... | collective-permute-start | bytes 393224 | tf_op jit(solution)/shard_map/ppermute | solution.py:206
  11.3 0.0 collective-permute-done.2.cross
  11.3 0.7 %collective-permute-start.6 = (bf16[512,128]{1,0:T(8,128)(2,1)S(1)}, bf16[512,128]{1,0:T(8,128)(2,1)S(1)}, u32[]{:S(2)}, u32[]{:S(2)}) collective-permute-start(bf16[512,128]{1,0:T(8,128)(2,1)S(1)} %get-tuple-element.37.own), channel_id=1, source_target_pairs={{4,8},{8,4},{5,9},{9,5},{6,10},{10,6},{7,11},{11,7},{20,24},{24,20... | collective-permute-start | bytes 393224 | tf_op jit(solution)/shard_map/ppermute | solution.py:210
  12.0 1.3 %collective-permute-done.7.near = bf16[512,128]{1,0:T(8,128)(2,1)S(1)} collective-permute-done((bf16[512,128]{1,0:T(8,128)(2,1)S(1)}, bf16[512,128]{1,0:T(8,128)(2,1)S(1)}, u32[]{:S(2)}, u32[]{:S(2)}) %collective-permute-start.7) | collective-permute-done | bytes 131104 | tf_op jit(solution)/shard_map/ppermute | solution.py:210
  13.2 0.7 %collective-permute-start.8 = (bf16[512,128]{1,0:T(8,128)(2,1)S(1)}, bf16[512,128]{1,0:T(8,128)(2,1)S(1)}, u32[]{:S(2)}, u32[]{:S(2)}) collective-permute-start(bf16[512,128]{1,0:T(8,128)(2,1)S(1)} %collective-permute-done.7.near), channel_id=1, source_target_pairs={{4,8},{8,4},{5,9},{9,5},{6,10},{10,6},{7,11},{11,7},{20,24},{24,20... | collective-permute-start | bytes 393224 | tf_op jit(solution)/shard_map/ppermute | solution.py:210
  13.9 0.7 %shard_map.86 = (bf16[256,256]{1,0:T(8,128)(2,1)S(1)}, bf16[256,256]{1,0:T(8,128)(2,1)S(1)}, bf16[256,512]{1,0:T(8,128)(2,1)S(1)}, f32[8,128]{1,0:T(8,128)S(1)}) custom-call(bf16[512,128]{1,0:T(8,128)(2,1)S(1)} %get-tuple-element.24.own, bf16[512,128]{1,0:T(8,128)(2,1)S(1)} %collective-permute-done.2.cross), custom_call_target="tpu_custom_call" | custom-call | flops 268435456 | tf_op jit(solution)/shard_map/pallas_call | solution.py:230
  14.6 4.1 %collective-permute-done.far = bf16[512,128]{1,0:T(8,128)(2,1)S(1)} collective-permute-done((bf16[512,128]{1,0:T(8,128)(2,1)S(1)}, bf16[512,128]{1,0:T(8,128)(2,1)S(1)}, u32[]{:S(2)}, u32[]{:S(2)}) %collective-permute-start) | collective-permute-done | bytes 131104 | tf_op jit(solution)/shard_map/ppermute | solution.py:206
  18.7 0.0 collective-permute-done.1.near
  18.7 1.5 %shard_map.87 = (bf16[512,128]{1,0:T(8,128)(2,1)S(1)}, bf16[512,128]{1,0:T(8,128)(2,1)S(1)}, bf16[512,128]{1,0:T(8,128)(2,1)S(1)}, bf16[512,128]{1,0:T(8,128)(2,...) custom-call(bf16[512,128]{1,0:T(8,128)(2,1)S(1)} %collective-permute-done.far, ...), custom_call_target="tpu_custom_call" | custom-call | flops 536870912 | tf_op jit(solution)/shard_map/pallas_call | solution.py:230
  20.2 1.8 %collective-permute-start.3 = (bf16[512,128]{1,0:T(8,128)(2,1)S(1)}, bf16[512,128]{1,0:T(8,128)(2,1)S(1)}, u32[]{:S(2)}, u32[]{:S(2)}) collective-permute-start(bf16[512,128]{1,0:T(8,128)(2,1)S(1)} %get-tuple-element.31), channel_id=1, source_target_pairs={{0,4},{4,0},{8,12},{12,8},{1,5},{5,1},{9,13},{13,9},{2,6},{6,2},{1... | collective-permute-start | bytes 393224 | tf_op jit(solution)/shard_map/ppermute | solution.py:206
  22.0 1.1 %collective-permute-start.4 = (bf16[512,128]{1,0:T(8,128)(2,1)S(1)}, bf16[512,128]{1,0:T(8,128)(2,1)S(1)}, u32[]{:S(2)}, u32[]{:S(2)}) collective-permute-start(bf16[512,128]{1,0:T(8,128)(2,1)S(1)} %get-tuple-element.32), channel_id=1, source_target_pairs={{0,8},{4,12},{8,0},{12,4},{1,9},{5,13},{9,1},{13,5},{2,10},{6,14},... | collective-permute-start | bytes 393224 | tf_op jit(solution)/shard_map/ppermute | solution.py:206
  23.1 1.6 %collective-permute-start.5 = (bf16[512,128]{1,0:T(8,128)(2,1)S(1)}, bf16[512,128]{1,0:T(8,128)(2,1)S(1)}, u32[]{:S(2)}, u32[]{:S(2)}) collective-permute-start(bf16[512,128]{1,0:T(8,128)(2,1)S(1)} %get-tuple-element.33), channel_id=1, source_target_pairs={{0,12},{4,8},{8,4},{12,0},{1,13},{5,9},{9,5},{13,1},{2,14},{6,10},... | collective-permute-start | bytes 393224 | tf_op jit(solution)/shard_map/ppermute | solution.py:206
  24.7 0.0 collective-permute-done.6.cross
  24.7 0.0 collective-permute-done.8.far
  24.7 1.1 %shard_map.88 = (bf16[512,128]{1,0:T(8,128)(2,1)S(1)}, bf16[512,128]{1,0:T(8,128)(2,1)S(1)}) custom-call(bf16[256,256]{1,0:T(8,128)(2,1)S(1)} %get-tuple-element.34.pick_ref, bf16[256,256]{1,0:T(8,128)(2,1)S(1)} %get-tuple-element.35.last_ref, bf16[256,256]{1,0:T(8,128)(2,1)S(1)} %get-tuple-element.27.turned_ref, ...), custom_call_target="tpu_custom_call" | custom-call | tf_op jit(solution)/shard_map/pallas_call | solution.py:230
  25.8 1.3 %collective-permute-start.9 = (bf16[512,128]{1,0:T(8,128)(2,1)S(1)}, bf16[512,128]{1,0:T(8,128)(2,1)S(1)}, u32[]{:S(2)}, u32[]{:S(2)}) collective-permute-start(bf16[512,128]{1,0:T(8,128)(2,1)S(1)} %get-tuple-element.39), channel_id=1, source_target_pairs={{4,0},{8,12},{5,1},{9,13},{6,2},{10,14},{7,3},{11,15},{20,16},{24,... | collective-permute-start | bytes 393224 | tf_op jit(solution)/shard_map/ppermute | solution.py:210
  27.1 0.0 collective-permute-done.3.refs_1_
  27.1 5.9 %collective-permute-done.4.refs_2_ = bf16[512,128]{1,0:T(8,128)(2,1)S(1)} collective-permute-done((bf16[512,128]{1,0:T(8,128)(2,1)S(1)}, bf16[512,128]{1,0:T(8,128)(2,1)S(1)}, u32[]{:S(2)}, u32[]{:S(2)}) %collective-permute-start.4) | collective-permute-done | bytes 131104 | tf_op jit(solution)/shard_map/ppermute | solution.py:206
  33.0 0.0 collective-permute-done.5.refs_3_
  33.1 1.2 %collective-permute-done.9.refs_5_ = bf16[512,128]{1,0:T(8,128)(2,1)S(1)} collective-permute-done((bf16[512,128]{1,0:T(8,128)(2,1)S(1)}, bf16[512,128]{1,0:T(8,128)(2,1)S(1)}, u32[]{:S(2)}, u32[]{:S(2)}) %collective-permute-start.9) | collective-permute-done | bytes 131104 | tf_op jit(solution)/shard_map/ppermute | solution.py:210
  34.2 1.0 %shard_map.89 = (bf16[1,128,640]{2,1,0:T(8,128)(2,1)}, bf16[1,128,640]{2,1,0:T(8,128)(2,1)}, bf16[1,128,640]{2,1,0:T(8,128)(2,1)}, bf16[1,128,640]{2,1,0:T(8,128)(2,1)}) custom-call(bf16[512,128]{1,0:T(8,128)(2,1)S(1)} %get-tuple-element.30.refs_0_, bf16[512,128]{1,0:T(8,128)(2,1)S(1)} %collective-permute-done.3.refs_1_, ...), custom_call_target="tpu_custom_call" | custom-call | tf_op jit(solution)/shard_map/pallas_call | solution.py:230
Async XLA Ops:
  1.5 9.8 %collective-permute-start.2 = (bf16[512,128]{1,0:T(8,128)(2,1)S(1)}, bf16[512,128]{1,0:T(8,128)(2,1)S(1)}, u32[]{:S(2)}, u32[]{:S(2)}) collective-permute-start(bf16[512,128]{1,0:T(8,128)(2,1)S(1)} %shard_map.85), channel_id=1, source_target_pairs={{0,12},{4,8},{8,4},{12,0},{1,13},{5,9},{9,5},{13,1},{2,14},{6,10},... | collective-permute-start | bytes 393224 | tf_op jit(solution)/shard_map/ppermute | solution.py:206
  7.9 5.4 %collective-permute-start.7 = (bf16[512,128]{1,0:T(8,128)(2,1)S(1)}, bf16[512,128]{1,0:T(8,128)(2,1)S(1)}, u32[]{:S(2)}, u32[]{:S(2)}) collective-permute-start(bf16[512,128]{1,0:T(8,128)(2,1)S(1)} %get-tuple-element.37.own), channel_id=1, source_target_pairs={{0,4},{12,8},{1,5},{13,9},{2,6},{14,10},{3,7},{15,11},{16,20},{28,... | collective-permute-start | bytes 393224 | tf_op jit(solution)/shard_map/ppermute | solution.py:210
  9.3 9.3 %collective-permute-start = (bf16[512,128]{1,0:T(8,128)(2,1)S(1)}, bf16[512,128]{1,0:T(8,128)(2,1)S(1)}, u32[]{:S(2)}, u32[]{:S(2)}) collective-permute-start(bf16[512,128]{1,0:T(8,128)(2,1)S(1)} %get-tuple-element.22), channel_id=1, source_target_pairs={{0,8},{4,12},{8,0},{12,4},{1,9},{5,13},{9,1},{13,5},{2,10},{6,14},... | collective-permute-start | bytes 393224 | tf_op jit(solution)/shard_map/ppermute | solution.py:206
  9.4 9.3 %collective-permute-start.1 = (bf16[512,128]{1,0:T(8,128)(2,1)S(1)}, bf16[512,128]{1,0:T(8,128)(2,1)S(1)}, u32[]{:S(2)}, u32[]{:S(2)}) collective-permute-start(bf16[512,128]{1,0:T(8,128)(2,1)S(1)} %get-tuple-element.23), channel_id=1, source_target_pairs={{0,4},{4,0},{8,12},{12,8},{1,5},{5,1},{9,13},{13,9},{2,6},{6,2},{1... | collective-permute-start | bytes 393224 | tf_op jit(solution)/shard_map/ppermute | solution.py:206
  11.3 13.4 %collective-permute-start.6 = (bf16[512,128]{1,0:T(8,128)(2,1)S(1)}, bf16[512,128]{1,0:T(8,128)(2,1)S(1)}, u32[]{:S(2)}, u32[]{:S(2)}) collective-permute-start(bf16[512,128]{1,0:T(8,128)(2,1)S(1)} %get-tuple-element.37.own), channel_id=1, source_target_pairs={{4,8},{8,4},{5,9},{9,5},{6,10},{10,6},{7,11},{11,7},{20,24},{24,20... | collective-permute-start | bytes 393224 | tf_op jit(solution)/shard_map/ppermute | solution.py:210
  13.2 11.4 %collective-permute-start.8 = (bf16[512,128]{1,0:T(8,128)(2,1)S(1)}, bf16[512,128]{1,0:T(8,128)(2,1)S(1)}, u32[]{:S(2)}, u32[]{:S(2)}) collective-permute-start(bf16[512,128]{1,0:T(8,128)(2,1)S(1)} %collective-permute-done.7.near), channel_id=1, source_target_pairs={{4,8},{8,4},{5,9},{9,5},{6,10},{10,6},{7,11},{11,7},{20,24},{24,20... | collective-permute-start | bytes 393224 | tf_op jit(solution)/shard_map/ppermute | solution.py:210
  20.2 6.9 %collective-permute-start.3 = (bf16[512,128]{1,0:T(8,128)(2,1)S(1)}, bf16[512,128]{1,0:T(8,128)(2,1)S(1)}, u32[]{:S(2)}, u32[]{:S(2)}) collective-permute-start(bf16[512,128]{1,0:T(8,128)(2,1)S(1)} %get-tuple-element.31), channel_id=1, source_target_pairs={{0,4},{4,0},{8,12},{12,8},{1,5},{5,1},{9,13},{13,9},{2,6},{6,2},{1... | collective-permute-start | bytes 393224 | tf_op jit(solution)/shard_map/ppermute | solution.py:206
  22.0 11.1 %collective-permute-start.4 = (bf16[512,128]{1,0:T(8,128)(2,1)S(1)}, bf16[512,128]{1,0:T(8,128)(2,1)S(1)}, u32[]{:S(2)}, u32[]{:S(2)}) collective-permute-start(bf16[512,128]{1,0:T(8,128)(2,1)S(1)} %get-tuple-element.32), channel_id=1, source_target_pairs={{0,8},{4,12},{8,0},{12,4},{1,9},{5,13},{9,1},{13,5},{2,10},{6,14},... | collective-permute-start | bytes 393224 | tf_op jit(solution)/shard_map/ppermute | solution.py:206
  23.1 10.0 %collective-permute-start.5 = (bf16[512,128]{1,0:T(8,128)(2,1)S(1)}, bf16[512,128]{1,0:T(8,128)(2,1)S(1)}, u32[]{:S(2)}, u32[]{:S(2)}) collective-permute-start(bf16[512,128]{1,0:T(8,128)(2,1)S(1)} %get-tuple-element.33), channel_id=1, source_target_pairs={{0,12},{4,8},{8,4},{12,0},{1,13},{5,9},{9,5},{13,1},{2,14},{6,10},... | collective-permute-start | bytes 393224 | tf_op jit(solution)/shard_map/ppermute | solution.py:206
  25.8 8.4 %collective-permute-start.9 = (bf16[512,128]{1,0:T(8,128)(2,1)S(1)}, bf16[512,128]{1,0:T(8,128)(2,1)S(1)}, u32[]{:S(2)}, u32[]{:S(2)}) collective-permute-start(bf16[512,128]{1,0:T(8,128)(2,1)S(1)} %get-tuple-element.39), channel_id=1, source_target_pairs={{4,0},{8,12},{5,1},{9,13},{6,2},{10,14},{7,3},{11,15},{20,16},{24,... | collective-permute-start | bytes 393224 | tf_op jit(solution)/shard_map/ppermute | solution.py:210

commit v8 on v6

--- a/solution.py
+++ b/solution.py
@@ -236,8 +236,8 @@
             ],
         )
 
-    (cross,) = pack(3)
-    far, near, own, shared = pack(2, 1, 0, None)
+    cross, shared = pack(3, None)
+    near, far, own = pack(1, 2, 0)
     got_cross = exchange(cross, 3)
     got_far = exchange(far, 2)
     got_near = exchange(near, 1)

time: 35.7 us -> 35.7 us (level)
  transfers between devices with their start and end apart: 10 -> 10, of which waited for: 4 -> 5; matrix products, arithmetic and copies ran while one was open for 0% -> 0% of each run, Pallas kernels for 13% -> 13%
where the time goes in v8:
time: 35.7 us; the launch traced here: 35.4 us
  starting transfers between devices  16.1 us (45%)
  waiting for transfers between devices  12.2 us (34%)
  Pallas kernels  6.41 us (18%)
  between operations  0.72 us (2%)
    ppermute x6, starting transfers between devices, exchange(): return lax.ppermute(array, 'win', [(n, n ^ step) for n in range(WINDOWS)])  12.1 us
    ppermute x6, waiting for transfers between devices, exchange(): return lax.ppermute(array, 'win', [(n, n ^ step) for n in range(WINDOWS)])  9.95 us
    pallas_call x6, Pallas kernels, call(): pl.pallas_call(body, out_shape=out_shape, cost_estimate=pl.CostEstimate(f...  6.41 us
    ppermute x4, starting transfers between devices, along(): return lax.ppermute(array, 'win', pairs)  4.06 us
    ppermute x4, waiting for transfers between devices, along(): return lax.ppermute(array, 'win', pairs)  2.2 us
  transfers between devices with their start and end apart: 10, of which 5 were waited for; matrix products, arithmetic and copies ran while one was open for 0% of the time, Pallas kernels for 13%

profile of v8, /device:TPU:0, one launch (start us, length us, event | category | flops | bytes accessed | tf_op | source)
XLA Modules:
  0.0 35.4 jit_solution(10794052753613511722)
XLA Ops:
  0.6 1.0 %shard_map.85 = (bf16[512,128]{1,0:T(8,128)(2,1)S(1)}, bf16[512,128]{1,0:T(8,128)(2,1)S(1)}) custom-call(bf16[1,128,640]{2,1,0:T(8,128)(2,1)} %q_ref.3, bf16[1,128,640]{2,1,0:T(8,128)(2,1)} %k_ref.3, bf16[1,128,640]{2,1,0:T(8,128)(2,1)} %v_ref.3, bf16[1,128,640]{2,1,0:T(8,128)(2,1)} %g_ref.3, s32[1,128]{1,0:T(1,128)} %mask_ref.3), custom_call_target="tpu_custom_call" | custom-call | tf_op jit(solution)/shard_map/pallas_call | solution.py:214
  1.6 5.1 %collective-permute-start.2 = (bf16[512,128]{1,0:T(8,128)(2,1)S(1)}, bf16[512,128]{1,0:T(8,128)(2,1)S(1)}, u32[]{:S(2)}, u32[]{:S(2)}) collective-permute-start(bf16[512,128]{1,0:T(8,128)(2,1)S(1)} %get-tuple-element.26), channel_id=1, source_target_pairs={{0,12},{4,8},{8,4},{12,0},{1,13},{5,9},{9,5},{13,1},{2,14},{6,10},... | collective-permute-start | bytes 393224 | tf_op jit(solution)/shard_map/ppermute | solution.py:190
  6.7 1.5 %collective-permute-start.6 = (bf16[512,128]{1,0:T(8,128)(2,1)S(1)}, bf16[512,128]{1,0:T(8,128)(2,1)S(1)}, u32[]{:S(2)}, u32[]{:S(2)}) collective-permute-start(bf16[512,128]{1,0:T(8,128)(2,1)S(1)} %get-tuple-element.37.own), channel_id=1, source_target_pairs={{0,4},{12,8},{1,5},{13,9},{2,6},{14,10},{3,7},{15,11},{16,20},{28,... | collective-permute-start | bytes 393224 | tf_op jit(solution)/shard_map/ppermute | solution.py:194
  8.2 1.1 %shard_map.84 = (bf16[512,128]{1,0:T(8,128)(2,1)S(1)}, bf16[512,128]{1,0:T(8,128)(2,1)S(1)}, bf16[512,128]{1,0:T(8,128)(2,1)S(1)}) custom-call(bf16[1,128,640]{2,1,0:T(8,128)(2,1)} %q_ref.3, bf16[1,128,640]{2,1,0:T(8,128)(2,1)} %k_ref.3, bf16[1,128,640]{2,1,0:T(8,128)(2,1)} %v_ref.3, bf16[1,128,640]{2,1,0:T(8,128)(2,1)} %g_ref.3, s32[1,128]{1,0:T(1,128)} %mask_ref.3), custom_call_target="tpu_custom_call" | custom-call | tf_op jit(solution)/shard_map/pallas_call | solution.py:214
  9.3 0.1 collective-permute-start.1
  9.4 1.9 %collective-permute-start = (bf16[512,128]{1,0:T(8,128)(2,1)S(1)}, bf16[512,128]{1,0:T(8,128)(2,1)S(1)}, u32[]{:S(2)}, u32[]{:S(2)}) collective-permute-start(bf16[512,128]{1,0:T(8,128)(2,1)S(1)} %get-tuple-element.22), channel_id=1, source_target_pairs={{0,8},{4,12},{8,0},{12,4},{1,9},{5,13},{9,1},{13,5},{2,10},{6,14},... | collective-permute-start | bytes 393224 | tf_op jit(solution)/shard_map/ppermute | solution.py:190
  11.3 0.0 collective-permute-done.2.cross
  11.3 0.7 %collective-permute-start.7 = (bf16[512,128]{1,0:T(8,128)(2,1)S(1)}, bf16[512,128]{1,0:T(8,128)(2,1)S(1)}, u32[]{:S(2)}, u32[]{:S(2)}) collective-permute-start(bf16[512,128]{1,0:T(8,128)(2,1)S(1)} %get-tuple-element.37.own), channel_id=1, source_target_pairs={{4,8},{8,4},{5,9},{9,5},{6,10},{10,6},{7,11},{11,7},{20,24},{24,20... | collective-permute-start | bytes 393224 | tf_op jit(solution)/shard_map/ppermute | solution.py:194
  11.9 1.5 %collective-permute-done.6.near = bf16[512,128]{1,0:T(8,128)(2,1)S(1)} collective-permute-done((bf16[512,128]{1,0:T(8,128)(2,1)S(1)}, bf16[512,128]{1,0:T(8,128)(2,1)S(1)}, u32[]{:S(2)}, u32[]{:S(2)}) %collective-permute-start.6) | collective-permute-done | bytes 131104 | tf_op jit(solution)/shard_map/ppermute | solution.py:194
  13.4 0.7 %collective-permute-start.8 = (bf16[512,128]{1,0:T(8,128)(2,1)S(1)}, bf16[512,128]{1,0:T(8,128)(2,1)S(1)}, u32[]{:S(2)}, u32[]{:S(2)}) collective-permute-start(bf16[512,128]{1,0:T(8,128)(2,1)S(1)} %collective-permute-done.6.near), channel_id=1, source_target_pairs={{4,8},{8,4},{5,9},{9,5},{6,10},{10,6},{7,11},{11,7},{20,24},{24,20... | collective-permute-start | bytes 393224 | tf_op jit(solution)/shard_map/ppermute | solution.py:194
  14.1 2.9 %collective-permute-done.1.near = bf16[512,128]{1,0:T(8,128)(2,1)S(1)} collective-permute-done((bf16[512,128]{1,0:T(8,128)(2,1)S(1)}, bf16[512,128]{1,0:T(8,128)(2,1)S(1)}, u32[]{:S(2)}, u32[]{:S(2)}) %collective-permute-start.1) | collective-permute-done | bytes 131104 | tf_op jit(solution)/shard_map/ppermute | solution.py:190
  17.0 0.9 %shard_map.86 = (bf16[256,384]{1,0:T(8,128)(2,1)S(1)}, bf16[384,256]{1,0:T(8,128)(2,1)S(1)}, bf16[256,512]{1,0:T(8,128)(2,1)S(1)}, f32[8,128]{1,0:T(8,128)S(1)}) custom-call(bf16[512,128]{1,0:T(8,128)(2,1)S(1)} %get-tuple-element.23.own, bf16[512,128]{1,0:T(8,128)(2,1)S(1)} %collective-permute-done.1.near, bf16[512,128]{1,0:T(8,128)(2,1)S(1)} %collective-permute-done.2.cross), custom_call_target="tpu_custom_call" | custom-call | flops 268435456 | tf_op jit(solution)/shard_map/pallas_call | solution.py:214
  17.9 0.2 collective-permute-done.far
  18.0 1.3 %shard_map.87 = (bf16[512,128]{1,0:T(8,128)(2,1)S(1)}, bf16[512,128]{1,0:T(8,128)(2,1)S(1)}, bf16[512,128]{1,0:T(8,128)(2,1)S(1)}, bf16[512,128]{1,0:T(8,128)(2,1)S(1)}, bf16[256,128]{1,0:T(8,128)(2,1)S(1)}) custom-call(bf16[512,128]{1,0:T(8,128)(2,1)S(1)} %collective-permute-done.far, bf16[384,256]{1,0:T(8,128)(2,1)S(1)} %get-tuple-element.28.turned_ref, ...), custom_call_target="tpu_custom_call" | custom-call | flops 536870912 | tf_op jit(solution)/shard_map/pallas_call | solution.py:214
  19.3 1.7 %collective-permute-start.3 = (bf16[512,128]{1,0:T(8,128)(2,1)S(1)}, bf16[512,128]{1,0:T(8,128)(2,1)S(1)}, u32[]{:S(2)}, u32[]{:S(2)}) collective-permute-start(bf16[512,128]{1,0:T(8,128)(2,1)S(1)} %get-tuple-element.32), channel_id=1, source_target_pairs={{0,4},{4,0},{8,12},{12,8},{1,5},{5,1},{9,13},{13,9},{2,6},{6,2},{1... | collective-permute-start | bytes 393224 | tf_op jit(solution)/shard_map/ppermute | solution.py:190
  21.0 1.9 %collective-permute-start.4 = (bf16[512,128]{1,0:T(8,128)(2,1)S(1)}, bf16[512,128]{1,0:T(8,128)(2,1)S(1)}, u32[]{:S(2)}, u32[]{:S(2)}) collective-permute-start(bf16[512,128]{1,0:T(8,128)(2,1)S(1)} %get-tuple-element.33), channel_id=1, source_target_pairs={{0,8},{4,12},{8,0},{12,4},{1,9},{5,13},{9,1},{13,5},{2,10},{6,14},... | collective-permute-start | bytes 393224 | tf_op jit(solution)/shard_map/ppermute | solution.py:190
  22.9 1.4 %collective-permute-start.5 = (bf16[512,128]{1,0:T(8,128)(2,1)S(1)}, bf16[512,128]{1,0:T(8,128)(2,1)S(1)}, u32[]{:S(2)}, u32[]{:S(2)}) collective-permute-start(bf16[512,128]{1,0:T(8,128)(2,1)S(1)} %get-tuple-element.34), channel_id=1, source_target_pairs={{0,12},{4,8},{8,4},{12,0},{1,13},{5,9},{9,5},{13,1},{2,14},{6,10},... | collective-permute-start | bytes 393224 | tf_op jit(solution)/shard_map/ppermute | solution.py:190
  24.3 0.0 collective-permute-done.7.cross
  24.3 0.0 collective-permute-done.8.far
  24.3 1.1 %shard_map.88 = (bf16[512,128]{1,0:T(8,128)(2,1)S(1)}, bf16[512,128]{1,0:T(8,128)(2,1)S(1)}) custom-call(bf16[256,384]{1,0:T(8,128)(2,1)S(1)} %get-tuple-element.35.pick_ref, bf16[256,128]{1,0:T(8,128)(2,1)S(1)} %get-tuple-element.36.last_ref, bf16[384,256]{1,0:T(8,128)(2,1)S(1)} %get-tuple-element.28.turned_ref, ...), custom_call_target="tpu_custom_call" | custom-call | tf_op jit(solution)/shard_map/pallas_call | solution.py:214
  25.5 1.3 %collective-permute-start.9 = (bf16[512,128]{1,0:T(8,128)(2,1)S(1)}, bf16[512,128]{1,0:T(8,128)(2,1)S(1)}, u32[]{:S(2)}, u32[]{:S(2)}) collective-permute-start(bf16[512,128]{1,0:T(8,128)(2,1)S(1)} %get-tuple-element.39), channel_id=1, source_target_pairs={{4,0},{8,12},{5,1},{9,13},{6,2},{10,14},{7,3},{11,15},{20,16},{24,... | collective-permute-start | bytes 393224 | tf_op jit(solution)/shard_map/ppermute | solution.py:194
  26.8 0.0 collective-permute-done.3.refs_1_
  26.8 6.9 %collective-permute-done.4.refs_2_ = bf16[512,128]{1,0:T(8,128)(2,1)S(1)} collective-permute-done((bf16[512,128]{1,0:T(8,128)(2,1)S(1)}, bf16[512,128]{1,0:T(8,128)(2,1)S(1)}, u32[]{:S(2)}, u32[]{:S(2)}) %collective-permute-start.4) | collective-permute-done | bytes 131104 | tf_op jit(solution)/shard_map/ppermute | solution.py:190
  33.7 0.0 collective-permute-done.5.refs_3_
  33.7 0.7 %collective-permute-done.9.refs_5_ = bf16[512,128]{1,0:T(8,128)(2,1)S(1)} collective-permute-done((bf16[512,128]{1,0:T(8,128)(2,1)S(1)}, bf16[512,128]{1,0:T(8,128)(2,1)S(1)}, u32[]{:S(2)}, u32[]{:S(2)}) %collective-permute-start.9) | collective-permute-done | bytes 131104 | tf_op jit(solution)/shard_map/ppermute | solution.py:194
  34.4 1.0 %shard_map.89 = (bf16[1,128,640]{2,1,0:T(8,128)(2,1)}, bf16[1,128,640]{2,1,0:T(8,128)(2,1)}, bf16[1,128,640]{2,1,0:T(8,128)(2,1)}, bf16[1,128,640]{2,1,0:T(8,128)(2,1)}) custom-call(bf16[512,128]{1,0:T(8,128)(2,1)S(1)} %get-tuple-element.31.refs_0_, bf16[512,128]{1,0:T(8,128)(2,1)S(1)} %collective-permute-done.3.refs_1_, ...), custom_call_target="tpu_custom_call" | custom-call | tf_op jit(solution)/shard_map/pallas_call | solution.py:214
Async XLA Ops:
  1.6 9.7 %collective-permute-start.2 = (bf16[512,128]{1,0:T(8,128)(2,1)S(1)}, bf16[512,128]{1,0:T(8,128)(2,1)S(1)}, u32[]{:S(2)}, u32[]{:S(2)}) collective-permute-start(bf16[512,128]{1,0:T(8,128)(2,1)S(1)} %get-tuple-element.26), channel_id=1, source_target_pairs={{0,12},{4,8},{8,4},{12,0},{1,13},{5,9},{9,5},{13,1},{2,14},{6,10},... | collective-permute-start | bytes 393224 | tf_op jit(solution)/shard_map/ppermute | solution.py:190
  6.7 6.7 %collective-permute-start.6 = (bf16[512,128]{1,0:T(8,128)(2,1)S(1)}, bf16[512,128]{1,0:T(8,128)(2,1)S(1)}, u32[]{:S(2)}, u32[]{:S(2)}) collective-permute-start(bf16[512,128]{1,0:T(8,128)(2,1)S(1)} %get-tuple-element.37.own), channel_id=1, source_target_pairs={{0,4},{12,8},{1,5},{13,9},{2,6},{14,10},{3,7},{15,11},{16,20},{28,... | collective-permute-start | bytes 393224 | tf_op jit(solution)/shard_map/ppermute | solution.py:194
  9.3 7.7 %collective-permute-start.1 = (bf16[512,128]{1,0:T(8,128)(2,1)S(1)}, bf16[512,128]{1,0:T(8,128)(2,1)S(1)}, u32[]{:S(2)}, u32[]{:S(2)}) collective-permute-start(bf16[512,128]{1,0:T(8,128)(2,1)S(1)} %get-tuple-element.24), channel_id=1, source_target_pairs={{0,4},{4,0},{8,12},{12,8},{1,5},{5,1},{9,13},{13,9},{2,6},{6,2},{1... | collective-permute-start | bytes 393224 | tf_op jit(solution)/shard_map/ppermute | solution.py:190
  9.4 8.6 %collective-permute-start = (bf16[512,128]{1,0:T(8,128)(2,1)S(1)}, bf16[512,128]{1,0:T(8,128)(2,1)S(1)}, u32[]{:S(2)}, u32[]{:S(2)}) collective-permute-start(bf16[512,128]{1,0:T(8,128)(2,1)S(1)} %get-tuple-element.22), channel_id=1, source_target_pairs={{0,8},{4,12},{8,0},{12,4},{1,9},{5,13},{9,1},{13,5},{2,10},{6,14},... | collective-permute-start | bytes 393224 | tf_op jit(solution)/shard_map/ppermute | solution.py:190
  11.3 13.0 %collective-permute-start.7 = (bf16[512,128]{1,0:T(8,128)(2,1)S(1)}, bf16[512,128]{1,0:T(8,128)(2,1)S(1)}, u32[]{:S(2)}, u32[]{:S(2)}) collective-permute-start(bf16[512,128]{1,0:T(8,128)(2,1)S(1)} %get-tuple-element.37.own), channel_id=1, source_target_pairs={{4,8},{8,4},{5,9},{9,5},{6,10},{10,6},{7,11},{11,7},{20,24},{24,20... | collective-permute-start | bytes 393224 | tf_op jit(solution)/shard_map/ppermute | solution.py:194
  13.4 10.9 %collective-permute-start.8 = (bf16[512,128]{1,0:T(8,128)(2,1)S(1)}, bf16[512,128]{1,0:T(8,128)(2,1)S(1)}, u32[]{:S(2)}, u32[]{:S(2)}) collective-permute-start(bf16[512,128]{1,0:T(8,128)(2,1)S(1)} %collective-permute-done.6.near), channel_id=1, source_target_pairs={{4,8},{8,4},{5,9},{9,5},{6,10},{10,6},{7,11},{11,7},{20,24},{24,20... | collective-permute-start | bytes 393224 | tf_op jit(solution)/shard_map/ppermute | solution.py:194
  19.3 7.4 %collective-permute-start.3 = (bf16[512,128]{1,0:T(8,128)(2,1)S(1)}, bf16[512,128]{1,0:T(8,128)(2,1)S(1)}, u32[]{:S(2)}, u32[]{:S(2)}) collective-permute-start(bf16[512,128]{1,0:T(8,128)(2,1)S(1)} %get-tuple-element.32), channel_id=1, source_target_pairs={{0,4},{4,0},{8,12},{12,8},{1,5},{5,1},{9,13},{13,9},{2,6},{6,2},{1... | collective-permute-start | bytes 393224 | tf_op jit(solution)/shard_map/ppermute | solution.py:190
  21.0 12.7 %collective-permute-start.4 = (bf16[512,128]{1,0:T(8,128)(2,1)S(1)}, bf16[512,128]{1,0:T(8,128)(2,1)S(1)}, u32[]{:S(2)}, u32[]{:S(2)}) collective-permute-start(bf16[512,128]{1,0:T(8,128)(2,1)S(1)} %get-tuple-element.33), channel_id=1, source_target_pairs={{0,8},{4,12},{8,0},{12,4},{1,9},{5,13},{9,1},{13,5},{2,10},{6,14},... | collective-permute-start | bytes 393224 | tf_op jit(solution)/shard_map/ppermute | solution.py:190
  22.9 10.8 %collective-permute-start.5 = (bf16[512,128]{1,0:T(8,128)(2,1)S(1)}, bf16[512,128]{1,0:T(8,128)(2,1)S(1)}, u32[]{:S(2)}, u32[]{:S(2)}) collective-permute-start(bf16[512,128]{1,0:T(8,128)(2,1)S(1)} %get-tuple-element.34), channel_id=1, source_target_pairs={{0,12},{4,8},{8,4},{12,0},{1,13},{5,9},{9,5},{13,1},{2,14},{6,10},... | collective-permute-start | bytes 393224 | tf_op jit(solution)/shard_map/ppermute | solution.py:190
  25.5 9.0 %collective-permute-start.9 = (bf16[512,128]{1,0:T(8,128)(2,1)S(1)}, bf16[512,128]{1,0:T(8,128)(2,1)S(1)}, u32[]{:S(2)}, u32[]{:S(2)}) collective-permute-start(bf16[512,128]{1,0:T(8,128)(2,1)S(1)} %get-tuple-element.39), channel_id=1, source_target_pairs={{4,0},{8,12},{5,1},{9,13},{6,2},{10,14},{7,3},{11,15},{20,16},{24,... | collective-permute-start | bytes 393224 | tf_op jit(solution)/shard_map/ppermute | solution.py:194
